TPU v7x, 32 devices: a whole 2x2x4 slice. The times are simulated.
32 devices in a mesh: row: 8 (over y, x, core), col: 4 (over z).
Axes of the slice: x: 2, y: 2, z: 4, core: 2. Of those that a mesh axis runs over, the one named last changes fastest.
Arguments:
- vectors: float32 [16384, 512], P(('row', 'col')), may hold values from -6 to 6
- panels: float32 [2, 16384, 256], P(None, 'row', 'col'), may hold values from -0.046875 to 0.046875
- tfactors: float32 [2, 256, 256], replicated, may hold values from -3 to 3, as said below
Outputs:
- transformed: float32 [16384, 512], P('row', 'col')
Inputs may be any that keep to these rules, and one draw needn't show every extreme that they name: tfactors[p] is upper triangular with its diagonal between 1 and 2.
All inputs are finite; a program needn't handle non-finite values.
Results may differ from a plain program's by a relative error of at most 0.000071.
Values sent between devices are 32-bit elements; how exact they have to be, the bound alone decides.
No kernel may reach another device: no remote copies, remote signals or barrier semaphores. Data moves between devices by JAX's collectives and lax.ppermute only.
A program may use at most 64 MiB of HBM per device.

v0:
```python
import jax
import jax.numpy as jnp
from jax import lax
from jax.sharding import PartitionSpec as P


def panel_product(panel, field):
    return lax.dot_general(
        panel,
        field,
        (((0,), (0,)), ((), ())),
        precision=lax.Precision.HIGHEST,
        preferred_element_type=jnp.float32,
    )


def matmul(left, right):
    return jnp.dot(left, right, precision=lax.Precision.HIGHEST, preferred_element_type=jnp.float32)


def per_device(vectors, panels, tfactors):
    field = lax.all_to_all(vectors, "col", split_axis=1, concat_axis=0, tiled=True)
    gathered = lax.all_gather(panels, "col", axis=2, tiled=True)
    first_vecs = gathered[0]
    second_vecs = gathered[1]
    first_w = lax.psum(panel_product(first_vecs, field), "row")
    updated = field - matmul(first_vecs, matmul(tfactors[0], first_w))
    second_w = lax.psum(panel_product(second_vecs, updated), "row")
    return updated - matmul(second_vecs, matmul(tfactors[1], second_w))


def solution(mesh):
    in_specs = (P(("row", "col"), None), P(None, "row", "col"), P())
    out_specs = P("row", "col")
    return jax.shard_map(
        per_device, mesh=mesh, in_specs=in_specs, out_specs=out_specs, check_vma=False
    )
```

profile of v0, /device:TPU:8, one launch (start us, length us, event | category | flops | bytes accessed | tf_op | source)
XLA Modules:
  0.0 235.1 jit_solution(17954824005193018069)
XLA Ops:
  6.5 0.0 all-gather.2.cloned.1.call-start
  6.5 0.7 all-gather.2.cloned.1.call-update
  7.3 0.0 all-reduce.3.cloned.1.call-start
  7.3 1.6 copy.6
  8.9 0.0 copy-start.1
  8.9 54.4 %all_to_all.19 = f32[512,4,128]{0,2,1:T(8,128)S(1)} all-to-all(f32[512,4,128]{0,2,1:T(8,128)S(1)} %bitcast.39), channel_id=1, replica_groups=mesh['row'=8,'col'=4] {'col'}, dimensions={1} | all-to-all | bytes 2097152 | tf_op jit(solution)/shard_map/all_to_all | solution.py:22
  63.3 0.1 copy.9
  63.4 40.8 %all-gather.2.cloned.1.call-done = f32[2,2048,256]{1,2,0:T(8,128)} async-done(((f32[2,2048,64]{1,2,0:T(8,128)}), f32[2,2048,256]{1,2,0:T(8,128)}) %all-gather.2.cloned.1.call-update) | async-done | bytes 4194320 | tf_op jit(solution)/shard_map/all_gather | solution.py:23
  104.1 4.0 %fusion.2 = f32[256,128]{1,0:T(8,128)} fusion(f32[2048,128]{0,1:T(8,128)S(1)} %bitcast.36, f32[2,2048,256]{1,2,0:T(8,128)} %all-gather.2.cloned.1.call-done), kind=kOutput, calls=%fused_computation.6 | convolution fusion | flops 805306368 | bytes 3276800 | tf_op jit(solution)/shard_map/dot_general | solution.py:8
  108.2 0.0 all-reduce.3.cloned.1.call-update
  108.2 0.0 all-reduce.5.cloned.1.call-start
  108.3 55.2 %all-reduce.3.cloned.1.call-done = f32[256,128]{1,0:T(8,128)} async-done(((f32[256,128]{1,0:T(8,128)}), f32[256,128]{1,0:T(8,128)}) %all-reduce.3.cloned.1.call-update) | async-done | bytes 131088 | tf_op jit(solution)/shard_map/psum | solution.py:26
  163.5 0.0 copy-done.1
  163.5 0.0 copy-start
  163.5 1.4 fusion.7
  164.9 2.8 %fusion.1 = f32[2048,128]{0,1:T(8,128)S(1)} fusion(f32[2048,128]{0,1:T(8,128)S(1)} %bitcast.37, f32[128,256]{1,0:T(8,128)S(1)} %fusion.7, f32[2,2048,256]{1,2,0:T(8,128)} %all-gather.2.cloned.1.call-done), kind=kOutput, calls=%fused_computation.3 | convolution fusion | flops 805568512 | bytes 4325376 | tf_op jit(solution)/shard_map/dot_general | solution.py:18
  167.8 0.0 copy-done
  167.8 2.9 %fusion.4 = f32[256,128]{0,1:T(8,128)} fusion(f32[2048,128]{0,1:T(8,128)S(1)} %fusion.1, f32[2,2048,256]{1,2,0:T(8,128)S(1)} %copy-done), kind=kOutput, calls=%fused_computation.8 | convolution fusion | flops 805306368 | bytes 3276800 | tf_op jit(solution)/shard_map/dot_general | solution.py:8
  170.7 0.0 all-reduce.5.cloned.1.call-update
  170.7 52.4 %all-reduce.5.cloned.1.call-done = f32[256,128]{0,1:T(8,128)} async-done(((f32[256,128]{0,1:T(8,128)}), f32[256,128]{0,1:T(8,128)}) %all-reduce.5.cloned.1.call-update) | async-done | bytes 131088 | tf_op jit(solution)/shard_map/psum | solution.py:28
  223.1 1.3 fusion.5
  224.4 2.8 %fusion = f32[2048,128]{0,1:T(8,128)S(1)} fusion(f32[2048,128]{0,1:T(8,128)S(1)} %fusion.1, f32[128,256]{1,0:T(8,128)S(1)} %fusion.5, f32[2,2048,256]{1,2,0:T(8,128)} %all-gather.2.cloned.1.call-done), kind=kOutput, calls=%fused_computation.1 | convolution fusion | flops 805568512 | bytes 4325376 | tf_op jit(solution)/shard_map/dot_general | solution.py:18
  227.3 1.3 copy.8
Async XLA Ops:
  6.5 97.6 %all-gather.2.cloned.1.call-start = ((), (), s32[]{:S(2)}) async-start(), calls=%async_computation.1 | async-start | bytes 5242880 | tf_op jit(solution)/shard_map/all_gather | solution.py:23
  7.3 156.2 %all-reduce.3.cloned.1.call-start = ((), (), s32[]{:S(2)}) async-start(), calls=%async_computation.2 | async-start | bytes 262144 | tf_op jit(solution)/shard_map/psum | solution.py:26
  8.9 154.6 %copy-start.1 = (f32[2,256,256]{2,1,0:T(8,128)S(1)}, f32[2,256,256]{2,1,0:T(8,128)}, u32[]{:S(2)}) copy-start(f32[2,256,256]{2,1,0:T(8,128)} %param.5) | copy-start | bytes 1572868
  108.2 114.9 %all-reduce.5.cloned.1.call-start = ((), (), s32[]{:S(2)}) async-start(), calls=%async_computation.3 | async-start | bytes 262144 | tf_op jit(solution)/shard_map/psum | solution.py:28
  163.5 4.3 %copy-start = (f32[2,2048,256]{1,2,0:T(8,128)S(1)}, f32[2,2048,256]{1,2,0:T(8,128)}, u32[]{:S(2)}) copy-start(f32[2,2048,256]{1,2,0:T(8,128)} %all-gather.2.cloned.1.call-done) | copy-start | bytes 12582916
Sparse Core Ops, SparseCore 0:
  8.9 95.1 all-gather.1
  108.3 55.1 all-reduce.2
  170.8 52.2 all-reduce.4
where the time goes:
time: 237 us; the launch traced here: 235 us
  waiting for transfers between devices  149 us (63%)
  blocking collectives  54.4 us (23%)
  matrix products  15.3 us (6%)
  between operations  13.2 us (6%)
  local copies, waits for them, and re-layouts  2.96 us (1%)
    psum x1, waiting for transfers between devices, per_device(): first_w = lax.psum(panel_product(first_vecs, field), 'row')  55.2 us
    all_to_all x1, blocking collectives, per_device(): lax.all_to_all(vectors, 'col', split_axis=1, concat_axis=0, tiled=True)  54.4 us
    psum x1, waiting for transfers between devices, per_device(): second_w = lax.psum(panel_product(second_vecs, updated), 'row')  52.4 us
    all_gather x1, waiting for transfers between devices, per_device(): gathered = lax.all_gather(panels, 'col', axis=2, tiled=True)  40.8 us
    dot_general x4, matrix products, matmul(): jnp.dot(left, right, precision=lax.Precision.HIGHEST, preferred_element_t...  8.39 us
    dot_general x2, matrix products, panel_product(): lax.dot_general(panel, field, (((0,), (0,)), ((), ())), precision=lax.Pre...  6.93 us
  transfers between devices with their start and end apart: 3, of which 3 were waited for; matrix products, arithmetic and copies ran while one was open for 1% of the time, Pallas kernels for 0%

commit v1 on v0

v1 whole, which is shorter than its diff:
```python
import jax
import jax.numpy as jnp
from jax import lax
from jax.sharding import PartitionSpec as P


def matmul(left, right, contract):
    return lax.dot_general(
        left,
        right,
        (contract, ((), ())),
        precision=lax.Precision.HIGH,
        preferred_element_type=jnp.float32,
    )


def swap(block, axis, size, mask):
    return lax.ppermute(block, axis, [(i, i ^ mask) for i in range(size)])


def row_stages(size):
    stages = []
    shift = 0
    while (1 << shift) < size:
        bits = 1 if shift == 0 or (2 << shift) == size else 2
        stages.append((shift, 1 << bits))
        shift += bits
    return stages


def reduce_scatter_rows(partial, size):
    row = lax.axis_index("row")
    current = partial.reshape((size, partial.shape[0] // size, partial.shape[1]))
    for shift, group in row_stages(size):
        me = (row >> shift) & (group - 1)
        current = current.reshape((current.shape[0] // group, group) + current.shape[1:])
        pick = lambda k: lax.dynamic_index_in_dim(current, me ^ k, 1, keepdims=False)
        received = [swap(pick(k), "row", size, k << shift) for k in range(1, group)]
        current = pick(0)
        for block in received:
            current = current + block
    return current[0]


def all_gather_rows(part, size):
    row = lax.axis_index("row")
    current = part[None]
    for shift, group in reversed(row_stages(size)):
        me = (row >> shift) & (group - 1)
        received = [swap(current, "row", size, k << shift) for k in range(1, group)]
        whole = jnp.zeros((current.shape[0], group) + current.shape[1:], current.dtype)
        for k, block in enumerate([current] + received):
            whole = lax.dynamic_update_index_in_dim(whole, block, me ^ k, 1)
        current = whole.reshape((current.shape[0] * group,) + current.shape[1:])
    return current.reshape((-1, part.shape[1]))


def all_reduce_cols(part, size):
    received = [swap(part, "col", size, k) for k in range(1, size)]
    for block in received:
        part = part + block
    return part


def make_per_device(rows_size, cols_size):
    def per_device(vectors, panels, tfactors):
        col = lax.axis_index("col")
        local_rows, eigvecs = vectors.shape
        own = panels.shape[2]
        width = own * cols_size
        out_cols = eigvecs // cols_size

        vt = panels.transpose(0, 2, 1)
        pieces = []
        for k in range(cols_size):
            piece = lax.dynamic_slice_in_dim(vt, (col ^ k) * local_rows, local_rows, 2)
            pieces.append(swap(piece, "col", cols_size, k) if k else piece)
        house = jnp.zeros((2, cols_size, own, local_rows), jnp.float32)
        for k, piece in enumerate(pieces):
            house = lax.dynamic_update_index_in_dim(house, piece, col ^ k, 1)
        house = house.reshape((2, width, local_rows))

        u1 = matmul(tfactors[0], house[0], ((1,), (0,)))
        u2 = matmul(tfactors[1], house[1], ((1,), (0,)))
        scaled = matmul(jnp.concatenate([u1, u2], 0), vectors, ((1,), (0,)))
        cross = matmul(u2, house[0], ((1,), (1,)))
        half = width // 2
        cross = jnp.concatenate([cross[:, :half], cross[:, half:]], 0)
        partial = jnp.concatenate([scaled, cross], 1)

        part = reduce_scatter_rows(partial, rows_size)
        part = all_reduce_cols(part, cols_size)
        total = all_gather_rows(part, rows_size)

        scaled = total[:, :eigvecs]
        cross = jnp.concatenate([total[:width, eigvecs:], total[width:, eigvecs:]], 1)
        first = house[0] - matmul(cross, house[1], ((0,), (0,)))
        both = jnp.concatenate([first, house[1]], 0)
        result = vectors - matmul(both, scaled, ((0,), (0,)))

        out = jnp.zeros((cols_size, local_rows, out_cols), jnp.float32)
        for k in range(cols_size):
            block = lax.dynamic_slice_in_dim(result, (col ^ k) * out_cols, out_cols, 1)
            block = swap(block, "col", cols_size, k) if k else block
            out = lax.dynamic_update_index_in_dim(out, block, col ^ k, 0)
        return out.reshape((cols_size * local_rows, out_cols))

    return per_device


def solution(mesh):
    in_specs = (P(("row", "col"), None), P(None, "row", "col"), P())
    out_specs = P("row", "col")
    per_device = make_per_device(mesh.shape["row"], mesh.shape["col"])
    return jax.shard_map(
        per_device, mesh=mesh, in_specs=in_specs, out_specs=out_specs, check_vma=False
    )
```

time: 237 us -> 109 us (0.46)
  waiting for transfers between devices: 149 us -> 74.5 us
  blocking collectives: 54.4 us -> 0 us
  starting transfers between devices: 0.08 us -> 18.1 us
  between operations: 13.2 us -> 0.36 us
  matrix products: 15.3 us -> 3.76 us
  local copies, waits for them, and re-layouts: 2.96 us -> 7.8 us
  other arithmetic: 0 us -> 3.33 us
    psum x2 -> x0, waiting for transfers between devices: 108 us -> none  [the longest x1 55.2 us: per_device(): first_w = lax.psum(panel_product(first_vecs, field), 'row')]
    ppermute x0 -> x17, waiting for transfers between devices: none -> 74.5 us  [swap(): return lax.ppermute(block, axis, [(i, i ^ mask) for i in range(size)])]
    all_to_all x1 -> x0, blocking collectives: 54.4 us -> none  [per_device(): lax.all_to_all(vectors, 'col', split_axis=1, concat_axis=0, tiled=True)]
    all_gather x1 -> x0, waiting for transfers between devices: 40.8 us -> none  [per_device(): gathered = lax.all_gather(panels, 'col', axis=2, tiled=True)]
    ppermute x0 -> x17, starting transfers between devices: none -> 18.1 us  [swap(): return lax.ppermute(block, axis, [(i, i ^ mask) for i in range(size)])]
    dot_general x6, matrix products: 15.3 us -> 3.76 us  [matmul(): lax.dot_general(left, right, (contract, ((), ())), precision=lax.Precisio...]
  transfers between devices with their start and end apart: 3 -> 17, of which waited for: 3 -> 15; matrix products, arithmetic and copies ran while one was open for 1% -> 1% of each run, Pallas kernels for 0% -> 0%
where the time goes in v1:
time: 109 us; the launch traced here: 108 us
  waiting for transfers between devices  74.5 us (68%)
  starting transfers between devices  18.1 us (17%)
  local copies, waits for them, and re-layouts  7.8 us (7%)
  matrix products  3.76 us (3%)
  other arithmetic  3.33 us (3%)
    ppermute x17, waiting for transfers between devices, swap(): return lax.ppermute(block, axis, [(i, i ^ mask) for i in range(size)])  74.5 us
    ppermute x17, starting transfers between devices, swap(): return lax.ppermute(block, axis, [(i, i ^ mask) for i in range(size)])  18.1 us
    dot_general x6, matrix products, matmul(): lax.dot_general(left, right, (contract, ((), ())), precision=lax.Precisio...  3.76 us
  transfers between devices with their start and end apart: 17, of which 15 were waited for; matrix products, arithmetic and copies ran while one was open for 1% of the time, Pallas kernels for 0%

profile of v1, /device:TPU:8, one launch (start us, length us, event | category | flops | bytes accessed | tf_op | source)
XLA Modules:
  0.0 107.9 jit_solution(15491169938135610618)
XLA Ops:
  0.0 1.2 %dynamic-slice_bitcast_fusion.1 = (f32[2,64,512]{2,1,0:T(8,128)S(1)}, f32[2,64,512]{2,1,0:T(8,128)S(1)}, f32[2,64,512]{2,1,0:T(8,128)S(1)}) fusion(f32[2,2048,64]{1,2,0:T(8,128)} %param.4, s32[]{:T(128)S(6)} %select_n.76, s32[]{:T(128)S(6)} %select_n.72, s32[]{:T(128)S(6)} %select_n.74), kind=kLoop, calls=%fused_computation.32 | loop fusion | bytes 1572876 | tf_op jit(solution)/shard_map/dynamic_slice | solution.py:76
  1.3 3.0 %collective-permute-start.1 = (f32[2,64,512]{2,1,0:T(8,128)S(1)}, f32[2,64,512]{2,1,0:T(8,128)S(1)}, u32[]{:S(2)}, u32[]{:S(2)}) collective-permute-start(f32[2,64,512]{2,1,0:T(8,128)S(1)} %get-tuple-element.16), channel_id=1, source_target_pairs={{0,2},{1,3},{2,0},{3,1},{4,6},{5,7},{6,4},{7,5},{8,10},{9,11},{10,... | collective-permute-start | bytes 786440 | tf_op jit(solution)/shard_map/ppermute | solution.py:18
  4.3 0.5 collective-permute-start.2
  4.7 0.1 broadcast_in_dim.50
  4.9 1.0 bitcast_dynamic-update-slice_fusion.2
  5.9 6.1 %collective-permute-done = f32[2,64,512]{2,1,0:T(8,128)S(1)} collective-permute-done((f32[2,64,512]{2,1,0:T(8,128)S(1)}, f32[2,64,512]{2,1,0:T(8,128)S(1)}, u32[]{:S(2)}, u32[]{:S(2)}) %collective-permute-start) | collective-permute-done | bytes 262176 | tf_op jit(solution)/shard_map/ppermute | solution.py:18
  12.0 10.3 %collective-permute-done.1 = f32[2,64,512]{2,1,0:T(8,128)S(1)} collective-permute-done((f32[2,64,512]{2,1,0:T(8,128)S(1)}, f32[2,64,512]{2,1,0:T(8,128)S(1)}, u32[]{:S(2)}, u32[]{:S(2)}) %collective-permute-start.1) | collective-permute-done | bytes 262176 | tf_op jit(solution)/shard_map/ppermute | solution.py:18
  22.3 5.1 %collective-permute-done.2 = f32[2,64,512]{2,1,0:T(8,128)S(1)} collective-permute-done((f32[2,64,512]{2,1,0:T(8,128)S(1)}, f32[2,64,512]{2,1,0:T(8,128)S(1)}, u32[]{:S(2)}, u32[]{:S(2)}) %collective-permute-start.2) | collective-permute-done | bytes 262176 | tf_op jit(solution)/shard_map/ppermute | solution.py:18
  27.4 0.1 fusion.20
  27.5 0.4 fusion.11
  27.9 0.4 convolution_bitcast_fusion
  28.3 0.4 fusion.22
  28.8 0.4 copy-done
  29.1 1.0 fusion.1
  30.2 1.2 %maximum_maximum_fusion = f32[512,640]{0,1:T(8,128)} fusion(f32[256,128]{0,1:T(8,128)S(1)} %get-tuple-element.21, f32[256,128]{0,1:T(8,128)S(1)} %get-tuple-element.20, f32[512,512]{0,1:T(8,128)S(1)} %fusion.1), kind=kLoop, calls=%fused_computation.1 | loop fusion | flops 655360 | bytes 2621440 | tf_op jit(solution)/shard_map/concatenate | solution.py:89
  31.4 1.7 %copy.8 = f32[512,640]{1,0:T(8,128)S(1)} copy(f32[512,640]{0,1:T(8,128)} %maximum_maximum_fusion) | data formatting | bytes 2621440 | tf_op jit(solution)/shard_map/concatenate | solution.py:89
  33.1 0.9 dynamic-slice_bitcast_fusion
  34.0 2.4 %collective-permute-done.3 = f32[4,64,640]{2,1,0:T(8,128)} collective-permute-done((f32[4,64,640]{2,1,0:T(8,128)}, f32[4,64,640]{2,1,0:T(8,128)}, u32[]{:S(2)}, u32[]{:S(2)}) %collective-permute-start.3) | collective-permute-done | bytes 655392 | tf_op jit(solution)/shard_map/ppermute | solution.py:18
  36.4 1.2 %bitcast_add_fusion = f32[4,64,640]{2,1,0:T(8,128)S(1)} fusion(f32[4,64,640]{2,1,0:T(8,128)} %collective-permute-done.3, f32[4,2,64,640]{3,2,1,0:T(8,128)S(1)} %bitcast.66, s32[]{:T(128)S(6)} %select_n.78), kind=kLoop, calls=%fused_computation.14 | loop fusion | flops 163840 | bytes 1966084 | tf_op jit(solution)/shard_map/add | solution.py:41
  37.6 0.8 copy-done.1
  38.4 1.5 %collective-permute-start.4 = (f32[1,64,640]{2,1,0:T(8,128)S(1)}, f32[1,64,640]{2,1,0:T(8,128)S(1)}, u32[]{:S(2)}, u32[]{:S(2)}) collective-permute-start(f32[1,64,640]{2,1,0:T(8,128)S(1)} %get-tuple-element.17), channel_id=1, source_target_pairs={{0,8},{4,12},{8,0},{12,4},{16,24},{20,28},{24,16},{28,20},{1,9},{5... | collective-permute-start | bytes 491528 | tf_op jit(solution)/shard_map/ppermute | solution.py:18
  40.0 1.5 %collective-permute-start.5 = (f32[1,64,640]{2,1,0:T(8,128)S(1)}, f32[1,64,640]{2,1,0:T(8,128)S(1)}, u32[]{:S(2)}, u32[]{:S(2)}) collective-permute-start(f32[1,64,640]{2,1,0:T(8,128)S(1)} %get-tuple-element.19), channel_id=1, source_target_pairs={{0,16},{4,20},{8,24},{12,28},{16,0},{20,4},{24,8},{28,12},{1,17},{... | collective-permute-start | bytes 491528 | tf_op jit(solution)/shard_map/ppermute | solution.py:18
  41.5 0.5 collective-permute-start.6
  42.0 3.6 %collective-permute-done.4 = f32[1,64,640]{2,1,0:T(8,128)S(1)} collective-permute-done((f32[1,64,640]{2,1,0:T(8,128)S(1)}, f32[1,64,640]{2,1,0:T(8,128)S(1)}, u32[]{:S(2)}, u32[]{:S(2)}) %collective-permute-start.4) | collective-permute-done | bytes 163872 | tf_op jit(solution)/shard_map/ppermute | solution.py:18
  45.6 3.9 %collective-permute-done.5 = f32[1,64,640]{2,1,0:T(8,128)S(1)} collective-permute-done((f32[1,64,640]{2,1,0:T(8,128)S(1)}, f32[1,64,640]{2,1,0:T(8,128)S(1)}, u32[]{:S(2)}, u32[]{:S(2)}) %collective-permute-start.5) | collective-permute-done | bytes 163872 | tf_op jit(solution)/shard_map/ppermute | solution.py:18
  49.5 0.9 add_bitcast_fusion.1
  50.5 3.0 %collective-permute-start.8 = (f32[64,640]{1,0:T(8,128)S(1)}, f32[64,640]{1,0:T(8,128)S(1)}, u32[]{:S(2)}, u32[]{:S(2)}) collective-permute-start(f32[64,640]{1,0:T(8,128)S(1)} %add_bitcast_fusion.1), channel_id=1, source_target_pairs={{0,2},{1,3},{2,0},{3,1},{4,6},{5,7},{6,4},{7,5},{8,10},{9,11},{10,... | collective-permute-start | bytes 491528 | tf_op jit(solution)/shard_map/ppermute | solution.py:18
  53.5 0.4 collective-permute-start.9
  54.0 3.6 %collective-permute-done.7 = f32[64,640]{1,0:T(8,128)S(1)} collective-permute-done((f32[64,640]{1,0:T(8,128)S(1)}, f32[64,640]{1,0:T(8,128)S(1)}, u32[]{:S(2)}, u32[]{:S(2)}) %collective-permute-start.7) | collective-permute-done | bytes 163872 | tf_op jit(solution)/shard_map/ppermute | solution.py:18
  57.6 6.7 %collective-permute-done.8 = f32[64,640]{1,0:T(8,128)S(1)} collective-permute-done((f32[64,640]{1,0:T(8,128)S(1)}, f32[64,640]{1,0:T(8,128)S(1)}, u32[]{:S(2)}, u32[]{:S(2)}) %collective-permute-start.8) | collective-permute-done | bytes 163872 | tf_op jit(solution)/shard_map/ppermute | solution.py:18
  64.3 3.2 %collective-permute-done.9 = f32[64,640]{1,0:T(8,128)S(1)} collective-permute-done((f32[64,640]{1,0:T(8,128)S(1)}, f32[64,640]{1,0:T(8,128)S(1)}, u32[]{:S(2)}, u32[]{:S(2)}) %collective-permute-start.9) | collective-permute-done | bytes 163872 | tf_op jit(solution)/shard_map/ppermute | solution.py:18
  67.6 1.5 %collective-permute-start.10 = (f32[1,64,640]{2,1,0:T(8,128)S(1)}, f32[1,64,640]{2,1,0:T(8,128)S(1)}, u32[]{:S(2)}, u32[]{:S(2)}) collective-permute-start(f32[1,64,640]{2,1,0:T(8,128)S(1)} %get-tuple-element.6), channel_id=1, source_target_pairs={{0,8},{4,12},{8,0},{12,4},{16,24},{20,28},{24,16},{28,20},{1,9},{5... | collective-permute-start | bytes 491528 | tf_op jit(solution)/shard_map/ppermute | solution.py:18
  69.1 0.5 collective-permute-start.11
  69.6 1.5 %collective-permute-start.12 = (f32[1,64,640]{2,1,0:T(8,128)S(1)}, f32[1,64,640]{2,1,0:T(8,128)S(1)}, u32[]{:S(2)}, u32[]{:S(2)}) collective-permute-start(f32[1,64,640]{2,1,0:T(8,128)S(1)} %get-tuple-element.6), channel_id=1, source_target_pairs={{0,24},{4,28},{8,16},{12,20},{16,8},{20,12},{24,0},{28,4},{1,25},{... | collective-permute-start | bytes 491528 | tf_op jit(solution)/shard_map/ppermute | solution.py:18
  71.1 3.0 %collective-permute-done.10 = f32[1,64,640]{2,1,0:T(8,128)S(1)} collective-permute-done((f32[1,64,640]{2,1,0:T(8,128)S(1)}, f32[1,64,640]{2,1,0:T(8,128)S(1)}, u32[]{:S(2)}, u32[]{:S(2)}) %collective-permute-start.10) | collective-permute-done | bytes 163872 | tf_op jit(solution)/shard_map/ppermute | solution.py:18
  74.1 2.3 %collective-permute-done.11 = f32[1,64,640]{2,1,0:T(8,128)S(1)} collective-permute-done((f32[1,64,640]{2,1,0:T(8,128)S(1)}, f32[1,64,640]{2,1,0:T(8,128)S(1)}, u32[]{:S(2)}, u32[]{:S(2)}) %collective-permute-start.11) | collective-permute-done | bytes 163872 | tf_op jit(solution)/shard_map/ppermute | solution.py:18
  76.5 0.1 collective-permute-start.13
  76.6 0.1 broadcast_in_dim.55
  76.7 1.9 %collective-permute-done.13 = f32[4,64,640]{2,1,0:T(8,128)S(1)} collective-permute-done((f32[4,64,640]{2,1,0:T(8,128)S(1)}, f32[4,64,640]{2,1,0:T(8,128)S(1)}, u32[]{:S(2)}, u32[]{:S(2)}) %collective-permute-start.13) | collective-permute-done | bytes 655392 | tf_op jit(solution)/shard_map/ppermute | solution.py:18
  78.7 0.5 convolution_subtract_fusion.1
  79.2 1.1 convolution_subtract_fusion
  80.2 0.1 constant_dynamic-slice_fusion.5
  80.4 0.1 collective-permute-start.14
  80.4 3.8 %collective-permute-start.15 = (f32[512,128]{1,0:T(8,128)S(1)}, f32[512,128]{1,0:T(8,128)S(1)}, u32[]{:S(2)}, u32[]{:S(2)}) collective-permute-start(f32[512,128]{1,0:T(8,128)S(1)} %get-tuple-element.10), channel_id=1, source_target_pairs={{0,2},{1,3},{2,0},{3,1},{4,6},{5,7},{6,4},{7,5},{8,10},{9,11},{10,... | collective-permute-start | bytes 786440 | tf_op jit(solution)/shard_map/ppermute | solution.py:18
  84.4 7.6 %collective-permute-done.14 = f32[512,128]{1,0:T(8,128)S(1)} collective-permute-done((f32[512,128]{1,0:T(8,128)S(1)}, f32[512,128]{1,0:T(8,128)S(1)}, u32[]{:S(2)}, u32[]{:S(2)}) %collective-permute-start.14) | collective-permute-done | bytes 262176 | tf_op jit(solution)/shard_map/ppermute | solution.py:18
  92.0 10.2 %collective-permute-done.15 = f32[512,128]{1,0:T(8,128)S(1)} collective-permute-done((f32[512,128]{1,0:T(8,128)S(1)}, f32[512,128]{1,0:T(8,128)S(1)}, u32[]{:S(2)}, u32[]{:S(2)}) %collective-permute-start.15) | collective-permute-done | bytes 262176 | tf_op jit(solution)/shard_map/ppermute | solution.py:18
  102.2 4.7 %collective-permute-done.16 = f32[512,128]{1,0:T(8,128)S(1)} collective-permute-done((f32[512,128]{1,0:T(8,128)S(1)}, f32[512,128]{1,0:T(8,128)S(1)}, u32[]{:S(2)}, u32[]{:S(2)}) %collective-permute-start.16) | collective-permute-done | bytes 262176 | tf_op jit(solution)/shard_map/ppermute | solution.py:18
  106.9 1.0 copy-done.2
  (29 shorter events, 0.7 us)
Async XLA Ops:
  1.2 10.8 %collective-permute-start = (f32[2,64,512]{2,1,0:T(8,128)S(1)}, f32[2,64,512]{2,1,0:T(8,128)S(1)}, u32[]{:S(2)}, u32[]{:S(2)}) collective-permute-start(f32[2,64,512]{2,1,0:T(8,128)S(1)} %get-tuple-element.15), channel_id=1, source_target_pairs={{0,1},{1,0},{2,3},{3,2},{4,5},{5,4},{6,7},{7,6},{8,9},{9,8},{10,11... | collective-permute-start | bytes 786440 | tf_op jit(solution)/shard_map/ppermute | solution.py:18
  1.3 21.0 %collective-permute-start.1 = (f32[2,64,512]{2,1,0:T(8,128)S(1)}, f32[2,64,512]{2,1,0:T(8,128)S(1)}, u32[]{:S(2)}, u32[]{:S(2)}) collective-permute-start(f32[2,64,512]{2,1,0:T(8,128)S(1)} %get-tuple-element.16), channel_id=1, source_target_pairs={{0,2},{1,3},{2,0},{3,1},{4,6},{5,7},{6,4},{7,5},{8,10},{9,11},{10,... | collective-permute-start | bytes 786440 | tf_op jit(solution)/shard_map/ppermute | solution.py:18
  4.3 23.1 %collective-permute-start.2 = (f32[2,64,512]{2,1,0:T(8,128)S(1)}, f32[2,64,512]{2,1,0:T(8,128)S(1)}, u32[]{:S(2)}, u32[]{:S(2)}) collective-permute-start(f32[2,64,512]{2,1,0:T(8,128)S(1)} %get-tuple-element.14), channel_id=1, source_target_pairs={{0,3},{1,2},{2,1},{3,0},{4,7},{5,6},{6,5},{7,4},{8,11},{9,10},{10,... | collective-permute-start | bytes 786440 | tf_op jit(solution)/shard_map/ppermute | solution.py:18
  22.3 5.2 %copy-start.3 = (f32[2,256,256]{2,1,0:T(8,128)S(1)}, f32[2,256,256]{2,1,0:T(8,128)}, u32[]{:S(2)}) copy-start(f32[2,256,256]{2,1,0:T(8,128)} %param.5) | copy-start | bytes 1572868
  27.9 1.2 %copy-start = (f32[512,512]{1,0:T(8,128)S(1)}, f32[512,512]{1,0:T(8,128)}, u32[]{:S(2)}) copy-start(f32[512,512]{1,0:T(8,128)} %param.3) | copy-start | bytes 3145732
  34.0 2.4 %collective-permute-start.3 = (f32[4,64,640]{2,1,0:T(8,128)}, f32[4,64,640]{2,1,0:T(8,128)}, u32[]{:S(2)}, u32[]{:S(2)}) collective-permute-start(f32[4,64,640]{2,1,0:T(8,128)} %dynamic-slice_bitcast_fusion), channel_id=1, source_target_pairs={{0,4},{4,0},{8,12},{12,8},{16,20},{20,16},{24,28},{28,24},{1,5},{5... | collective-permute-start | bytes 1966088 | tf_op jit(solution)/shard_map/ppermute | solution.py:18
  37.6 0.8 copy-start.1
  38.4 7.1 %collective-permute-start.4 = (f32[1,64,640]{2,1,0:T(8,128)S(1)}, f32[1,64,640]{2,1,0:T(8,128)S(1)}, u32[]{:S(2)}, u32[]{:S(2)}) collective-permute-start(f32[1,64,640]{2,1,0:T(8,128)S(1)} %get-tuple-element.17), channel_id=1, source_target_pairs={{0,8},{4,12},{8,0},{12,4},{16,24},{20,28},{24,16},{28,20},{1,9},{5... | collective-permute-start | bytes 491528 | tf_op jit(solution)/shard_map/ppermute | solution.py:18
  40.0 9.5 %collective-permute-start.5 = (f32[1,64,640]{2,1,0:T(8,128)S(1)}, f32[1,64,640]{2,1,0:T(8,128)S(1)}, u32[]{:S(2)}, u32[]{:S(2)}) collective-permute-start(f32[1,64,640]{2,1,0:T(8,128)S(1)} %get-tuple-element.19), channel_id=1, source_target_pairs={{0,16},{4,20},{8,24},{12,28},{16,0},{20,4},{24,8},{28,12},{1,17},{... | collective-permute-start | bytes 491528 | tf_op jit(solution)/shard_map/ppermute | solution.py:18
  41.5 7.9 %collective-permute-start.6 = (f32[1,64,640]{2,1,0:T(8,128)S(1)}, f32[1,64,640]{2,1,0:T(8,128)S(1)}, u32[]{:S(2)}, u32[]{:S(2)}) collective-permute-start(f32[1,64,640]{2,1,0:T(8,128)S(1)} %get-tuple-element.18), channel_id=1, source_target_pairs={{0,24},{4,28},{8,16},{12,20},{16,8},{20,12},{24,0},{28,4},{1,25},{... | collective-permute-start | bytes 491528 | tf_op jit(solution)/shard_map/ppermute | solution.py:18
  50.4 7.2 %collective-permute-start.7 = (f32[64,640]{1,0:T(8,128)S(1)}, f32[64,640]{1,0:T(8,128)S(1)}, u32[]{:S(2)}, u32[]{:S(2)}) collective-permute-start(f32[64,640]{1,0:T(8,128)S(1)} %add_bitcast_fusion.1), channel_id=1, source_target_pairs={{0,1},{1,0},{2,3},{3,2},{4,5},{5,4},{6,7},{7,6},{8,9},{9,8},{10,11... | collective-permute-start | bytes 491528 | tf_op jit(solution)/shard_map/ppermute | solution.py:18
  50.5 13.8 %collective-permute-start.8 = (f32[64,640]{1,0:T(8,128)S(1)}, f32[64,640]{1,0:T(8,128)S(1)}, u32[]{:S(2)}, u32[]{:S(2)}) collective-permute-start(f32[64,640]{1,0:T(8,128)S(1)} %add_bitcast_fusion.1), channel_id=1, source_target_pairs={{0,2},{1,3},{2,0},{3,1},{4,6},{5,7},{6,4},{7,5},{8,10},{9,11},{10,... | collective-permute-start | bytes 491528 | tf_op jit(solution)/shard_map/ppermute | solution.py:18
  53.5 13.9 %collective-permute-start.9 = (f32[64,640]{1,0:T(8,128)S(1)}, f32[64,640]{1,0:T(8,128)S(1)}, u32[]{:S(2)}, u32[]{:S(2)}) collective-permute-start(f32[64,640]{1,0:T(8,128)S(1)} %add_bitcast_fusion.1), channel_id=1, source_target_pairs={{0,3},{1,2},{2,1},{3,0},{4,7},{5,6},{6,5},{7,4},{8,11},{9,10},{10,... | collective-permute-start | bytes 491528 | tf_op jit(solution)/shard_map/ppermute | solution.py:18
  67.6 6.5 %collective-permute-start.10 = (f32[1,64,640]{2,1,0:T(8,128)S(1)}, f32[1,64,640]{2,1,0:T(8,128)S(1)}, u32[]{:S(2)}, u32[]{:S(2)}) collective-permute-start(f32[1,64,640]{2,1,0:T(8,128)S(1)} %get-tuple-element.6), channel_id=1, source_target_pairs={{0,8},{4,12},{8,0},{12,4},{16,24},{20,28},{24,16},{28,20},{1,9},{5... | collective-permute-start | bytes 491528 | tf_op jit(solution)/shard_map/ppermute | solution.py:18
  69.1 7.4 %collective-permute-start.11 = (f32[1,64,640]{2,1,0:T(8,128)S(1)}, f32[1,64,640]{2,1,0:T(8,128)S(1)}, u32[]{:S(2)}, u32[]{:S(2)}) collective-permute-start(f32[1,64,640]{2,1,0:T(8,128)S(1)} %get-tuple-element.6), channel_id=1, source_target_pairs={{0,16},{4,20},{8,24},{12,28},{16,0},{20,4},{24,8},{28,12},{1,17},{... | collective-permute-start | bytes 491528 | tf_op jit(solution)/shard_map/ppermute | solution.py:18
  69.6 6.8 %collective-permute-start.12 = (f32[1,64,640]{2,1,0:T(8,128)S(1)}, f32[1,64,640]{2,1,0:T(8,128)S(1)}, u32[]{:S(2)}, u32[]{:S(2)}) collective-permute-start(f32[1,64,640]{2,1,0:T(8,128)S(1)} %get-tuple-element.6), channel_id=1, source_target_pairs={{0,24},{4,28},{8,16},{12,20},{16,8},{20,12},{24,0},{28,4},{1,25},{... | collective-permute-start | bytes 491528 | tf_op jit(solution)/shard_map/ppermute | solution.py:18
  76.5 2.2 %collective-permute-start.13 = (f32[4,64,640]{2,1,0:T(8,128)S(1)}, f32[4,64,640]{2,1,0:T(8,128)S(1)}, u32[]{:S(2)}, u32[]{:S(2)}) collective-permute-start(f32[4,64,640]{2,1,0:T(8,128)S(1)} %constant_dynamic-update-slice_fusion), channel_id=1, source_target_pairs={{0,4},{4,0},{8,12},{12,8},{16,20},{20,16},{24,28},{28,24},{1,5},{5... | collective-permute-start | bytes 1966088 | tf_op jit(solution)/shard_map/ppermute | solution.py:18
  80.4 11.6 %collective-permute-start.14 = (f32[512,128]{1,0:T(8,128)S(1)}, f32[512,128]{1,0:T(8,128)S(1)}, u32[]{:S(2)}, u32[]{:S(2)}) collective-permute-start(f32[512,128]{1,0:T(8,128)S(1)} %get-tuple-element.11), channel_id=1, source_target_pairs={{0,1},{1,0},{2,3},{3,2},{4,5},{5,4},{6,7},{7,6},{8,9},{9,8},{10,11... | collective-permute-start | bytes 786440 | tf_op jit(solution)/shard_map/ppermute | solution.py:18
  80.4 21.7 %collective-permute-start.15 = (f32[512,128]{1,0:T(8,128)S(1)}, f32[512,128]{1,0:T(8,128)S(1)}, u32[]{:S(2)}, u32[]{:S(2)}) collective-permute-start(f32[512,128]{1,0:T(8,128)S(1)} %get-tuple-element.10), channel_id=1, source_target_pairs={{0,2},{1,3},{2,0},{3,1},{4,6},{5,7},{6,4},{7,5},{8,10},{9,11},{10,... | collective-permute-start | bytes 786440 | tf_op jit(solution)/shard_map/ppermute | solution.py:18
  84.2 22.6 %collective-permute-start.16 = (f32[512,128]{1,0:T(8,128)S(1)}, f32[512,128]{1,0:T(8,128)S(1)}, u32[]{:S(2)}, u32[]{:S(2)}) collective-permute-start(f32[512,128]{1,0:T(8,128)S(1)} %get-tuple-element.9), channel_id=1, source_target_pairs={{0,3},{1,2},{2,1},{3,0},{4,7},{5,6},{6,5},{7,4},{8,11},{9,10},{10,... | collective-permute-start | bytes 786440 | tf_op jit(solution)/shard_map/ppermute | solution.py:18
  106.9 1.0 copy-start.2

commit v2 on v0

v2 whole, which is shorter than its diff:
```python
import functools

import jax
import jax.numpy as jnp
from jax import lax
from jax.experimental import pallas as pl
from jax.experimental.pallas import tpu as pltpu
from jax.sharding import PartitionSpec as P

PLAIN = ((1,), (0,))
BY_TRANSPOSE = ((1,), (1,))
FROM_TRANSPOSE = ((0,), (0,))


def split(value):
    high = value.astype(jnp.bfloat16)
    return high, (value - high.astype(jnp.float32)).astype(jnp.bfloat16)


def product(left, right, contract):
    def one(a, b):
        return lax.dot_general(a, b, (contract, ((), ())), preferred_element_type=jnp.float32)

    return one(left[0], right[0]) + (one(left[0], right[1]) + one(left[1], right[0]))


def kernel_call(body, shapes, *args, scratch=()):
    specs = [pl.BlockSpec(memory_space=pltpu.SMEM)]
    specs += [pl.BlockSpec(memory_space=pltpu.VMEM)] * (len(args) - 1)
    return pl.pallas_call(
        body,
        out_shape=[jax.ShapeDtypeStruct(shape, jnp.float32) for shape in shapes],
        in_specs=specs,
        out_specs=[pl.BlockSpec(memory_space=pltpu.VMEM)] * len(shapes),
        scratch_shapes=list(scratch),
        compiler_params=pltpu.CompilerParams(vmem_limit_bytes=32 * 1024 * 1024),
    )(*args)


def swap(block, axis, size, mask):
    return lax.ppermute(block, axis, [(i, i ^ mask) for i in range(size)])


def row_stages(size):
    stages = []
    shift = 0
    while (1 << shift) < size:
        bits = 1 if shift == 0 or (2 << shift) == size else 2
        stages.append((shift, 1 << bits))
        shift += bits
    return stages


def exchange_order(group):
    return [3, 1, 2] if group == 4 else list(range(1, group))


def cut_parts(parts, core, results, keep, send):
    rows = keep.shape[1]
    for j in range(parts // 2):
        at = 0
        for result in results:
            cut = pl.ds(at, result.shape[1])
            even = result[2 * j * rows : (2 * j + 1) * rows]
            odd = result[(2 * j + 1) * rows : (2 * j + 2) * rows]
            keep[j, :, cut] = jnp.where(core == 0, even, odd)
            send[j, :, cut] = jnp.where(core == 0, odd, even)
            at += result.shape[1]


def near_kernel(parts, *refs):
    place, pieces, field, keep, send, house = refs[0], refs[1:-4], refs[-4], refs[-3], refs[-2], refs[-1]
    col, core = place[0], place[1] & 1
    own, near = pieces[0].shape[1], len(pieces)
    for k, piece in enumerate(pieces):
        at = pl.multiple_of(((col ^ k) & (near - 1)) * own, own)
        house[pl.ds(at, own), :] = piece[0]
        house[pl.ds(near * own + at, own), :] = piece[1]
    result = product(split(house[...]), split(field[...]), PLAIN)
    cut_parts(parts, core, [result], keep, send)


def far_kernel(parts, *refs):
    place, pieces, field, keep, send, house, far = refs[0], refs[1:-5], refs[-5], refs[-4], refs[-3], refs[-2], refs[-1]
    col, core = place[0], place[1] & 1
    own, near = pieces[0].shape[1], len(pieces) // 2
    for k, piece in enumerate(pieces):
        at = pl.ds(pl.multiple_of((col ^ k) * own, own), own)
        house[0, at, :] = piece[0]
        house[1, at, :] = piece[1]
        if k >= near:
            at = pl.multiple_of(((col ^ k) & (near - 1)) * own, own)
            far[pl.ds(at, own), :] = piece[0]
            far[pl.ds(near * own + at, own), :] = piece[1]
    result = product(split(far[...]), split(field[...]), PLAIN)
    cross = product(split(house[1]), split(house[0]), BY_TRANSPOSE)
    cut_parts(parts, core, [result, cross], keep, send)


def merge_kernel(near, *refs):
    place, sources, same, out = refs[0], refs[1:-2], refs[-2], refs[-1]
    total = sources[0][0]
    for source in sources[1:]:
        total = total + source[0]
    eigvecs = same.shape[2]
    low = place[0] < near
    near_w, far_w = same[0], total[:, :eigvecs]
    out[0, :, :eigvecs] = jnp.where(low, near_w, far_w)
    out[0, :, eigvecs : 2 * eigvecs] = jnp.where(low, far_w, near_w)
    out[0, :, 2 * eigvecs :] = total[:, 2 * eigvecs - eigvecs :]


def add_split_kernel(shift, group, *refs):
    place, sources, outs = refs[0], refs[1:-group], refs[-group:]
    me = (place[1] >> shift) & (group - 1)
    for a in range(outs[0].shape[0]):
        for k, out in enumerate(outs):
            at = a * group + (me ^ k)
            total = sources[0][at]
            for source in sources[1:]:
                total = total + source[at]
            out[a] = total


def tail_kernel(cols_size, *refs):
    place, mine, other, factors, field, house = refs[:6]
    outs, scratch = refs[6:-1], refs[-1]
    col, core = place[0], place[1] & 1
    rows = mine.shape[1]
    for j in range(mine.shape[0]):
        a, b = mine[j], other[j]
        scratch[2 * j * rows : (2 * j + 1) * rows, :] = jnp.where(core == 0, a, b)
        scratch[(2 * j + 1) * rows : (2 * j + 2) * rows, :] = jnp.where(core == 0, b, a)
    eigvecs = field.shape[1]
    half = scratch.shape[0] // 2

    def weights(panel):
        rows = slice(panel * half, (panel + 1) * half)
        return jnp.concatenate([scratch[rows, :eigvecs], scratch[rows, eigvecs : 2 * eigvecs]], 0)

    first = product(split(factors[0]), split(weights(0)), PLAIN)
    first = split(first)
    cross = split(scratch[:, 2 * eigvecs :])
    second = weights(1) - product(cross, first, PLAIN)
    second = split(product(split(factors[1]), split(second), PLAIN))
    result = field[...] - (
        product(split(house[0]), first, FROM_TRANSPOSE)
        + product(split(house[1]), second, FROM_TRANSPOSE)
    )
    width = outs[0].shape[1]
    scratch_cols = [result[:, c * width : (c + 1) * width] for c in range(cols_size)]
    for c in range(cols_size):
        for k in range(cols_size):

            @pl.when(col == (c ^ k))
            def _(c=c, k=k):
                outs[k][...] = scratch_cols[c]


def all_reduce_cols(part, rows_size, cols_size):
    bits = cols_size.bit_length() - 1
    for step in range(bits):
        pairs = []
        for row in range(rows_size):
            mask = 1 << (bits - 1 - step if row & 1 else step)
            for col in range(cols_size):
                pairs.append((row * cols_size + col, row * cols_size + (col ^ mask)))
        part = part + lax.ppermute(part, ("row", "col"), pairs)
    return part


def make_per_device(rows_size, cols_size):
    stages = row_stages(rows_size)

    def per_device(vectors, panels, tfactors):
        col, row = lax.axis_index("col"), lax.axis_index("row")
        place = jnp.stack([col, row]).astype(jnp.int32)
        local_rows, eigvecs = vectors.shape
        own = panels.shape[2]
        width = own * cols_size
        out_cols = eigvecs // cols_size
        rows = width // rows_size
        wide = 2 * eigvecs + width

        vt = panels.transpose(0, 2, 1)
        pieces = [None] * cols_size
        for k in list(range(cols_size - 1, 0, -1)) + [0]:
            piece = lax.dynamic_slice_in_dim(vt, (col ^ k) * local_rows, local_rows, 2)
            pieces[k] = swap(piece, "col", cols_size, k) if k else piece

        near = cols_size // 2
        half = rows_size // 2

        def scatter(place, sources):
            for shift, group in stages[1:]:
                shape = (sources[0].shape[0] // group,) + sources[0].shape[1:]
                body = functools.partial(add_split_kernel, shift, group)
                cuts = kernel_call(body, [shape] * group, place, *sources)
                sources = [cuts[0]]
                for k in exchange_order(group):
                    sources.append(swap(cuts[k], "row", rows_size, k << shift))
            return sources

        def near_part(i, carry):
            at = place + i
            keep, send = kernel_call(
                functools.partial(near_kernel, rows_size),
                [(half, rows, eigvecs)] * 2,
                at,
                *pieces[:near],
                vectors,
                scratch=[pltpu.VMEM((width, local_rows), jnp.float32)],
            )
            first, *others = scatter(at, [keep, swap(send, "row", rows_size, 1)])
            for other in others:
                first = first + other
            return first

        same = lax.fori_loop(
            0, 1 + (row >> 10), near_part, jnp.zeros((1, rows, eigvecs), jnp.float32)
        )
        (pieces[near:], same) = lax.optimization_barrier((pieces[near:], same))
        keep, send, house = kernel_call(
            functools.partial(far_kernel, rows_size),
            [(half, rows, eigvecs + width)] * 2 + [(2, width, local_rows)],
            place,
            *pieces,
            vectors,
            scratch=[pltpu.VMEM((width, local_rows), jnp.float32)],
        )
        sources = scatter(place, [keep, swap(send, "row", rows_size, 1)])
        (part,) = kernel_call(
            functools.partial(merge_kernel, near), [(1, rows, wide)], place, *sources, same
        )
        current = all_reduce_cols(part, rows_size, cols_size)
        for shift, group in reversed(stages[1:]):
            me = (row >> shift) & (group - 1)
            whole = jnp.zeros((current.shape[0], group) + current.shape[1:], current.dtype)
            whole = lax.dynamic_update_index_in_dim(whole, current, me, 1)
            for k in exchange_order(group):
                block = swap(current, "row", rows_size, k << shift)
                whole = lax.dynamic_update_index_in_dim(whole, block, me ^ k, 1)
            current = whole.reshape((current.shape[0] * group,) + current.shape[1:])
        other = swap(current, "row", rows_size, 1)

        blocks = pl.pallas_call(
            functools.partial(tail_kernel, cols_size),
            out_shape=[jax.ShapeDtypeStruct((local_rows, out_cols), jnp.float32)] * cols_size,
            in_specs=[pl.BlockSpec(memory_space=pltpu.SMEM)]
            + [pl.BlockSpec(memory_space=pltpu.VMEM)] * 5,
            out_specs=[pl.BlockSpec(memory_space=pltpu.VMEM)] * cols_size,
            scratch_shapes=[pltpu.VMEM((width, wide), jnp.float32)],
            compiler_params=pltpu.CompilerParams(vmem_limit_bytes=32 * 1024 * 1024),
        )(place, current, other, tfactors, vectors, house)
        out = jnp.zeros((cols_size, local_rows, out_cols), jnp.float32)
        for k in list(range(1, cols_size)) + [0]:
            block = swap(blocks[k], "col", cols_size, k) if k else blocks[0]
            out = lax.dynamic_update_index_in_dim(out, block, col ^ k, 0)
        return out.reshape((cols_size * local_rows, out_cols))

    return per_device


def solution(mesh):
    in_specs = (P(("row", "col"), None), P(None, "row", "col"), P())
    out_specs = P("row", "col")
    per_device = make_per_device(mesh.shape["row"], mesh.shape["col"])
    return jax.shard_map(
        per_device, mesh=mesh, in_specs=in_specs, out_specs=out_specs, check_vma=False
    )
```

time: 237 us -> 95.9 us (0.40)
  waiting for transfers between devices: 149 us -> 63.9 us
  blocking collectives: 54.4 us -> 0 us
  starting transfers between devices: 0.08 us -> 19.3 us
  matrix products: 15.3 us -> 0 us
  between operations: 13.2 us -> 0.14 us
  Pallas kernels: 0 us -> 7.64 us
    psum x2 -> x0, waiting for transfers between devices: 108 us -> none  [the longest x1 55.2 us: per_device(): first_w = lax.psum(panel_product(first_vecs, field), 'row')]
    ppermute x0 -> x20, waiting for transfers between devices: none -> 63.9 us  [the longest x18 52.4 us: swap(): return lax.ppermute(block, axis, [(i, i ^ mask) for i in range(size)])]
    all_to_all x1 -> x0, blocking collectives: 54.4 us -> none  [per_device(): lax.all_to_all(vectors, 'col', split_axis=1, concat_axis=0, tiled=True)]
    all_gather x1 -> x0, waiting for transfers between devices: 40.8 us -> none  [per_device(): gathered = lax.all_gather(panels, 'col', axis=2, tiled=True)]
    ppermute x0 -> x20, starting transfers between devices: none -> 19.3 us  [the longest x18 18.1 us: swap(): return lax.ppermute(block, axis, [(i, i ^ mask) for i in range(size)])]
    dot_general x6 -> x0, matrix products: 15.3 us -> none  [the longest x4 8.39 us: matmul(): jnp.dot(left, right, precision=lax.Precision.HIGHEST, preferred_element_t...]
    pallas_call x0 -> x6, Pallas kernels: none -> 7.64 us  [the longest x5 4.41 us: kernel_call(): pl.pallas_call(body, out_shape=[jax.ShapeDtypeStruct(shape, jnp.float32)...]
  transfers between devices with their start and end apart: 3 -> 20, of which waited for: 3 -> 19; matrix products, arithmetic and copies ran while one was open for 1% -> 2% of each run, Pallas kernels for 0% -> 2%
where the time goes in v2:
time: 95.9 us; the launch traced here: 95.7 us
  waiting for transfers between devices  63.9 us (67%)
  starting transfers between devices  19.3 us (20%)
  Pallas kernels  7.64 us (8%)
  local copies, waits for them, and re-layouts  3.93 us (4%)
    ppermute x18, waiting for transfers between devices, swap(): return lax.ppermute(block, axis, [(i, i ^ mask) for i in range(size)])  52.4 us
    ppermute x18, starting transfers between devices, swap(): return lax.ppermute(block, axis, [(i, i ^ mask) for i in range(size)])  18.1 us
    ppermute x2, waiting for transfers between devices, all_reduce_cols(): part = part + lax.ppermute(part, ('row', 'col'), pairs)  11.5 us
    pallas_call x5, Pallas kernels, kernel_call(): pl.pallas_call(body, out_shape=[jax.ShapeDtypeStruct(shape, jnp.float32)...  4.41 us
    pallas_call x1, Pallas kernels, per_device(): pl.pallas_call(functools.partial(tail_kernel, cols_size), out_shape=[jax....  3.23 us
    dynamic_slice x1, local copies, waits for them, and re-layouts, per_device(): piece = lax.dynamic_slice_in_dim(vt, (col ^ k) * local_rows, local_rows, 2)  2.09 us
  transfers between devices with their start and end apart: 20, of which 19 were waited for; matrix products, arithmetic and copies ran while one was open for 2% of the time, Pallas kernels for 2%

profile of v2, /device:TPU:8, one launch (start us, length us, event | category | flops | bytes accessed | tf_op | source)
XLA Modules:
  0.0 95.7 jit_solution(7361326723017727275)
XLA Ops:
  0.0 2.1 %dynamic-slice_bitcast_fusion = (f32[2,64,512]{2,1,0:T(8,128)S(1)}, f32[2,64,512]{2,1,0:T(8,128)S(1)}, f32[2,64,512]{2,1,0:T(8,128)S(1)}, f32[2,64,512]{2,1,0:T(8,128)}) fusion(f32[2,2048,64]{1,2,0:T(8,128)} %param.6, s32[]{:T(128)S(6)} %select_n.41, s32[]{:T(128)S(6)} %select_n.39, s32[]{:T(128)S(6)} %select_n.38, s32[]{:T(128)S(6)} %select_n.40), kind=kLoop, calls=%fused_computation.6 | loop fusion | bytes 2097168 | tf_op jit(solution)/shard_map/dynamic_slice | solution.py:188
  2.1 3.0 %collective-permute-start.5 = (f32[2,64,512]{2,1,0:T(8,128)}, f32[2,64,512]{2,1,0:T(8,128)S(1)}, u32[]{:S(2)}, u32[]{:S(2)}) collective-permute-start(f32[2,64,512]{2,1,0:T(8,128)} %get-tuple-element.96), channel_id=1, source_target_pairs={{0,2},{1,3},{2,0},{3,1},{4,6},{5,7},{6,4},{7,5},{8,10},{9,11},{10,... | collective-permute-start | bytes 786440 | tf_op jit(solution)/shard_map/ppermute | solution.py:41
  5.1 0.5 collective-permute-start.6
  5.6 0.1 pad_add_fusion.refs_0_
  5.7 7.0 %collective-permute-done.4.refs_2_ = f32[2,64,512]{2,1,0:T(8,128)S(1)} collective-permute-done((f32[2,64,512]{2,1,0:T(8,128)S(1)}, f32[2,64,512]{2,1,0:T(8,128)S(1)}, u32[]{:S(2)}, u32[]{:S(2)}) %collective-permute-start.4) | collective-permute-done | bytes 262176 | tf_op jit(solution)/shard_map/ppermute | solution.py:41
  12.7 0.6 broadcast_in_dim.26
  13.3 12.5 %while.10 = (s32[]{:T(128)}, f32[1,32,512]{2,1,0:T(8,128)}, s32[]{:T(128)}, s32[2]{0:T(128)S(1)}, f32[2,64,512]{2,1,0:T(8,128)S(1)}, /*index=5*/f32[2,64,512]{2,1,0:T(8,128)S(1)}, f32[512,512]{1,0:T(8,128)S(1)}, s32[]{:T(128)}) while((s32[]{:T(128)}, f32[1,32,512]{2,1,0:T(8,128)}, s32[]{:T(128)}, s32[2]{0:T(128)S(1)}, ...), condition=%wide.region_1.0_spmd, body=%wide.region_0.0_spmd.sunk | while | flops 49156 | bytes 2162953 | solution.py:219
  13.3 1.2 %body.2 = (f32[4,32,512]{2,1,0:T(8,128)S(1)}, f32[4,32,512]{2,1,0:T(8,128)S(1)}) custom-call(s32[2]{0:T(128)S(1)} %broadcast_add_fusion.2.refs_0_, f32[2,64,512]{2,1,0:T(8,128)S(1)} %get-tuple-element.171.refs_1_, f32[2,64,512]{2,1,0:T(8,128)S(1)} %get-tuple-element.172.refs_2_, f32[512,512]{1,0:T(8,128)S(1)} %get-tuple-element.173.refs_3_), custom_call_target="tpu_custom_call" | custom-call | tf_op jit(solution)/shard_map/while/body/pallas_call | solution.py:30
  14.5 0.1 collective-permute-start
  14.6 1.5 %collective-permute-done.refs_2_ = f32[4,32,512]{2,1,0:T(8,128)S(1)} collective-permute-done((f32[4,32,512]{2,1,0:T(8,128)S(1)}, f32[4,32,512]{2,1,0:T(8,128)S(1)}, u32[]{:S(2)}, u32[]{:S(2)}) %collective-permute-start) | collective-permute-done | bytes 262176 | tf_op jit(solution)/shard_map/while/body/ppermute | solution.py:41
  16.1 0.6 body.3
  16.7 1.8 %collective-permute-start.1 = (f32[1,32,512]{2,1,0:T(8,128)S(1)}, f32[1,32,512]{2,1,0:T(8,128)S(1)}, u32[]{:S(2)}, u32[]{:S(2)}) collective-permute-start(f32[1,32,512]{2,1,0:T(8,128)S(1)} %get-tuple-element.147), channel_id=1, source_target_pairs={{0,16},{4,20},{8,24},{12,28},{16,0},{20,4},{24,8},{28,12},{1,17},{... | collective-permute-start | bytes 196616 | tf_op jit(solution)/shard_map/while/body/ppermute | solution.py:41
  18.5 1.5 %collective-permute-start.2 = (f32[1,32,512]{2,1,0:T(8,128)S(1)}, f32[1,32,512]{2,1,0:T(8,128)S(1)}, u32[]{:S(2)}, u32[]{:S(2)}) collective-permute-start(f32[1,32,512]{2,1,0:T(8,128)S(1)} %get-tuple-element.148), channel_id=1, source_target_pairs={{0,8},{4,12},{8,0},{12,4},{16,24},{20,28},{24,16},{28,20},{1,9},{5... | collective-permute-start | bytes 196616 | tf_op jit(solution)/shard_map/while/body/ppermute | solution.py:41
  20.0 0.3 collective-permute-start.3
  20.3 0.8 collective-permute-done.1
  21.1 2.3 %collective-permute-done.2 = f32[1,32,512]{2,1,0:T(8,128)S(1)} collective-permute-done((f32[1,32,512]{2,1,0:T(8,128)S(1)}, f32[1,32,512]{2,1,0:T(8,128)S(1)}, u32[]{:S(2)}, u32[]{:S(2)}) %collective-permute-start.2) | collective-permute-done | bytes 65568 | tf_op jit(solution)/shard_map/while/body/ppermute | solution.py:41
  23.4 1.7 %collective-permute-done.3 = f32[1,32,512]{2,1,0:T(8,128)S(1)} collective-permute-done((f32[1,32,512]{2,1,0:T(8,128)S(1)}, f32[1,32,512]{2,1,0:T(8,128)S(1)}, u32[]{:S(2)}, u32[]{:S(2)}) %collective-permute-start.3) | collective-permute-done | bytes 65568 | tf_op jit(solution)/shard_map/while/body/ppermute | solution.py:41
  25.1 0.6 add_add_fusion.2
  25.8 2.6 %collective-permute-done.6.refs_4_ = f32[2,64,512]{2,1,0:T(8,128)S(1)} collective-permute-done((f32[2,64,512]{2,1,0:T(8,128)S(1)}, f32[2,64,512]{2,1,0:T(8,128)S(1)}, u32[]{:S(2)}, u32[]{:S(2)}) %collective-permute-start.6) | collective-permute-done | bytes 262176 | tf_op jit(solution)/shard_map/ppermute | solution.py:41
  28.4 1.4 %shard_map.37 = (f32[4,32,768]{2,1,0:T(8,128)S(1)}, f32[4,32,768]{2,1,0:T(8,128)S(1)}, f32[2,256,512]{2,1,0:T(8,128)S(1)}) custom-call(s32[2]{0:T(128)S(1)} %get-tuple-element.217, f32[2,64,512]{2,1,0:T(8,128)S(1)} %get-tuple-element.197, f32[2,64,512]{2,1,0:T(8,128)S(1)} %get-tuple-element.199, f32[2,64,512]{2,1,0:T(8,128)S(1)} %collective-permute-done.5.refs_3_, ...), custom_call_target="tpu_custom_call" | custom-call | tf_op jit(solution)/shard_map/pallas_call | solution.py:30
  29.9 0.1 collective-permute-start.7
  30.0 1.7 %collective-permute-done.7.refs_2_ = f32[4,32,768]{2,1,0:T(8,128)S(1)} collective-permute-done((f32[4,32,768]{2,1,0:T(8,128)S(1)}, f32[4,32,768]{2,1,0:T(8,128)S(1)}, u32[]{:S(2)}, u32[]{:S(2)}) %collective-permute-start.7) | collective-permute-done | bytes 393248 | tf_op jit(solution)/shard_map/ppermute | solution.py:41
  31.7 0.6 shard_map.38
  32.3 1.6 %collective-permute-start.10 = (f32[1,32,768]{2,1,0:T(8,128)S(1)}, f32[1,32,768]{2,1,0:T(8,128)S(1)}, u32[]{:S(2)}, u32[]{:S(2)}) collective-permute-start(f32[1,32,768]{2,1,0:T(8,128)S(1)} %get-tuple-element.70), channel_id=1, source_target_pairs={{0,16},{4,20},{8,24},{12,28},{16,0},{20,4},{24,8},{28,12},{1,17},{... | collective-permute-start | bytes 294920 | tf_op jit(solution)/shard_map/ppermute | solution.py:41
  33.9 1.4 %collective-permute-start.8 = (f32[1,32,768]{2,1,0:T(8,128)S(1)}, f32[1,32,768]{2,1,0:T(8,128)S(1)}, u32[]{:S(2)}, u32[]{:S(2)}) collective-permute-start(f32[1,32,768]{2,1,0:T(8,128)S(1)} %get-tuple-element.68), channel_id=1, source_target_pairs={{0,24},{4,28},{8,16},{12,20},{16,8},{20,12},{24,0},{28,4},{1,25},{... | collective-permute-start | bytes 294920 | tf_op jit(solution)/shard_map/ppermute | solution.py:41
  35.3 0.5 collective-permute-start.9
  35.8 2.3 %collective-permute-done.10.refs_4_ = f32[1,32,768]{2,1,0:T(8,128)S(1)} collective-permute-done((f32[1,32,768]{2,1,0:T(8,128)S(1)}, f32[1,32,768]{2,1,0:T(8,128)S(1)}, u32[]{:S(2)}, u32[]{:S(2)}) %collective-permute-start.10) | collective-permute-done | bytes 98336 | tf_op jit(solution)/shard_map/ppermute | solution.py:41
  38.1 2.2 %collective-permute-done.8.refs_2_ = f32[1,32,768]{2,1,0:T(8,128)S(1)} collective-permute-done((f32[1,32,768]{2,1,0:T(8,128)S(1)}, f32[1,32,768]{2,1,0:T(8,128)S(1)}, u32[]{:S(2)}, u32[]{:S(2)}) %collective-permute-start.8) | collective-permute-done | bytes 98336 | tf_op jit(solution)/shard_map/ppermute | solution.py:41
  40.3 0.2 collective-permute-done.9.refs_3_
  40.5 0.6 shard_map.39
  41.2 6.3 %collective-permute-done.11 = f32[1,32,1280]{2,1,0:T(8,128)S(1)} collective-permute-done((f32[1,32,1280]{2,1,0:T(8,128)S(1)}, f32[1,32,1280]{2,1,0:T(8,128)S(1)}, u32[]{:S(2)}, u32[]{:S(2)}) %collective-permute-start.11) | collective-permute-done | bytes 163872 | tf_op jit(solution)/shard_map/ppermute | solution.py:168
  47.5 1.1 %collective-permute-start.12 = (f32[1,32,1280]{2,1,0:T(8,128)S(1)}, f32[1,32,1280]{2,1,0:T(8,128)S(1)}, u32[]{:S(2)}, u32[]{:S(2)}) collective-permute-start(f32[1,32,1280]{2,1,0:T(8,128)S(1)} %add.70), channel_id=1, source_target_pairs={{0,2},{1,3},{2,0},{3,1},{4,5},{5,4},{6,7},{7,6},{8,10},{9,11},{10,... | collective-permute-start | bytes 491528 | tf_op jit(solution)/shard_map/ppermute | solution.py:168
  48.6 5.2 %collective-permute-done.12 = f32[1,32,1280]{2,1,0:T(8,128)S(1)} collective-permute-done((f32[1,32,1280]{2,1,0:T(8,128)S(1)}, f32[1,32,1280]{2,1,0:T(8,128)S(1)}, u32[]{:S(2)}, u32[]{:S(2)}) %collective-permute-start.12) | collective-permute-done | bytes 163872 | tf_op jit(solution)/shard_map/ppermute | solution.py:168
  53.9 2.3 %collective-permute-start.13 = (f32[1,32,1280]{2,1,0:T(8,128)S(1)}, f32[1,32,1280]{2,1,0:T(8,128)S(1)}, u32[]{:S(2)}, u32[]{:S(2)}) collective-permute-start(f32[1,32,1280]{2,1,0:T(8,128)S(1)} %get-tuple-element.92), channel_id=1, source_target_pairs={{0,24},{4,28},{8,16},{12,20},{16,8},{20,12},{24,0},{28,4},{1,25},{... | collective-permute-start | bytes 491528 | tf_op jit(solution)/shard_map/ppermute | solution.py:41
  56.2 0.8 collective-permute-start.14
  56.9 0.5 collective-permute-start.15
  57.4 2.7 %collective-permute-done.13 = f32[1,32,1280]{2,1,0:T(8,128)S(1)} collective-permute-done((f32[1,32,1280]{2,1,0:T(8,128)S(1)}, f32[1,32,1280]{2,1,0:T(8,128)S(1)}, u32[]{:S(2)}, u32[]{:S(2)}) %collective-permute-start.13) | collective-permute-done | bytes 163872 | tf_op jit(solution)/shard_map/ppermute | solution.py:41
  60.2 1.8 %collective-permute-done.14 = f32[1,32,1280]{2,1,0:T(8,128)S(1)} collective-permute-done((f32[1,32,1280]{2,1,0:T(8,128)S(1)}, f32[1,32,1280]{2,1,0:T(8,128)S(1)}, u32[]{:S(2)}, u32[]{:S(2)}) %collective-permute-start.14) | collective-permute-done | bytes 163872 | tf_op jit(solution)/shard_map/ppermute | solution.py:41
  62.0 0.3 collective-permute-done.15
  62.3 2.1 %collective-permute-done.16.refs_2_ = f32[4,32,1280]{2,1,0:T(8,128)S(1)} collective-permute-done((f32[4,32,1280]{2,1,0:T(8,128)S(1)}, f32[4,32,1280]{2,1,0:T(8,128)S(1)}, u32[]{:S(2)}, u32[]{:S(2)}) %collective-permute-start.16) | collective-permute-done | bytes 655392 | tf_op jit(solution)/shard_map/ppermute | solution.py:41
  64.4 3.2 %shard_map.40 = (f32[512,128]{1,0:T(8,128)S(1)}, f32[512,128]{1,0:T(8,128)S(1)}, f32[512,128]{1,0:T(8,128)S(1)}, f32[512,128]{1,0:T(8,128)S(1)}) custom-call(s32[2]{0:T(128)S(1)} %get-tuple-element.217, f32[4,32,1280]{2,1,0:T(8,128)S(1)} %constant_dynamic-update-slice_fusion.refs_1_, f32[4,32,1280]{2,1,0:T(8,128)S(1)} %collective-permute-done.16.refs_2_, ...), custom_call_target="tpu_custom_call" | custom-call | tf_op jit(solution)/shard_map/pallas_call | solution.py:246
  67.7 2.2 %collective-permute-start.17 = (f32[512,128]{1,0:T(8,128)S(1)}, f32[512,128]{1,0:T(8,128)S(1)}, u32[]{:S(2)}, u32[]{:S(2)}) collective-permute-start(f32[512,128]{1,0:T(8,128)S(1)} %get-tuple-element.73), channel_id=1, source_target_pairs={{0,1},{1,0},{2,3},{3,2},{4,5},{5,4},{6,7},{7,6},{8,9},{9,8},{10,11... | collective-permute-start | bytes 786440 | tf_op jit(solution)/shard_map/ppermute | solution.py:41
  69.9 0.4 collective-permute-start.18
  70.3 1.2 %collective-permute-start.19 = (f32[512,128]{1,0:T(8,128)S(1)}, f32[512,128]{1,0:T(8,128)S(1)}, u32[]{:S(2)}, u32[]{:S(2)}) collective-permute-start(f32[512,128]{1,0:T(8,128)S(1)} %get-tuple-element.75), channel_id=1, source_target_pairs={{0,3},{1,2},{2,1},{3,0},{4,7},{5,6},{6,5},{7,4},{8,11},{9,10},{10,... | collective-permute-start | bytes 786440 | tf_op jit(solution)/shard_map/ppermute | solution.py:41
  71.4 9.0 %collective-permute-done.17 = f32[512,128]{1,0:T(8,128)S(1)} collective-permute-done((f32[512,128]{1,0:T(8,128)S(1)}, f32[512,128]{1,0:T(8,128)S(1)}, u32[]{:S(2)}, u32[]{:S(2)}) %collective-permute-start.17) | collective-permute-done | bytes 262176 | tf_op jit(solution)/shard_map/ppermute | solution.py:41
  80.6 7.7 %collective-permute-done.18 = f32[512,128]{1,0:T(8,128)S(1)} collective-permute-done((f32[512,128]{1,0:T(8,128)S(1)}, f32[512,128]{1,0:T(8,128)S(1)}, u32[]{:S(2)}, u32[]{:S(2)}) %collective-permute-start.18) | collective-permute-done | bytes 262176 | tf_op jit(solution)/shard_map/ppermute | solution.py:41
  88.3 6.4 %collective-permute-done.19 = f32[512,128]{1,0:T(8,128)S(1)} collective-permute-done((f32[512,128]{1,0:T(8,128)S(1)}, f32[512,128]{1,0:T(8,128)S(1)}, u32[]{:S(2)}, u32[]{:S(2)}) %collective-permute-start.19) | collective-permute-done | bytes 262176 | tf_op jit(solution)/shard_map/ppermute | solution.py:41
  94.7 1.0 %copy-done.2 = f32[4,512,128]{2,1,0:T(8,128)} copy-done((f32[4,512,128]{2,1,0:T(8,128)}, f32[4,512,128]{2,1,0:T(8,128)S(1)}, u32[]{:S(2)}) %copy-start.2) | copy-done | bytes 1048600
  (23 shorter events, 0.5 us)
Async XLA Ops:
  0.0 13.3 %copy-start.1 = (f32[512,512]{1,0:T(8,128)S(1)}, f32[512,512]{1,0:T(8,128)}, u32[]{:S(2)}) copy-start(f32[512,512]{1,0:T(8,128)} %refs_4_.1) | copy-start | bytes 3145732
  2.1 10.6 %collective-permute-start.4 = (f32[2,64,512]{2,1,0:T(8,128)S(1)}, f32[2,64,512]{2,1,0:T(8,128)S(1)}, u32[]{:S(2)}, u32[]{:S(2)}) collective-permute-start(f32[2,64,512]{2,1,0:T(8,128)S(1)} %get-tuple-element.94), channel_id=1, source_target_pairs={{0,1},{1,0},{2,3},{3,2},{4,5},{5,4},{6,7},{7,6},{8,9},{9,8},{10,11... | collective-permute-start | bytes 786440 | tf_op jit(solution)/shard_map/ppermute | solution.py:41
  2.1 23.7 %collective-permute-start.5 = (f32[2,64,512]{2,1,0:T(8,128)}, f32[2,64,512]{2,1,0:T(8,128)S(1)}, u32[]{:S(2)}, u32[]{:S(2)}) collective-permute-start(f32[2,64,512]{2,1,0:T(8,128)} %get-tuple-element.96), channel_id=1, source_target_pairs={{0,2},{1,3},{2,0},{3,1},{4,6},{5,7},{6,4},{7,5},{8,10},{9,11},{10,... | collective-permute-start | bytes 786440 | tf_op jit(solution)/shard_map/ppermute | solution.py:41
  5.1 23.3 %collective-permute-start.6 = (f32[2,64,512]{2,1,0:T(8,128)S(1)}, f32[2,64,512]{2,1,0:T(8,128)S(1)}, u32[]{:S(2)}, u32[]{:S(2)}) collective-permute-start(f32[2,64,512]{2,1,0:T(8,128)S(1)} %get-tuple-element.93), channel_id=1, source_target_pairs={{0,3},{1,2},{2,1},{3,0},{4,7},{5,6},{6,5},{7,4},{8,11},{9,10},{10,... | collective-permute-start | bytes 786440 | tf_op jit(solution)/shard_map/ppermute | solution.py:41
  14.5 1.6 %collective-permute-start = (f32[4,32,512]{2,1,0:T(8,128)S(1)}, f32[4,32,512]{2,1,0:T(8,128)S(1)}, u32[]{:S(2)}, u32[]{:S(2)}) collective-permute-start(f32[4,32,512]{2,1,0:T(8,128)S(1)} %get-tuple-element.146), channel_id=1, source_target_pairs={{0,4},{4,0},{8,12},{12,8},{16,20},{20,16},{24,28},{28,24},{1,5},{5... | collective-permute-start | bytes 786440 | tf_op jit(solution)/shard_map/while/body/ppermute | solution.py:41
  16.7 4.3 %collective-permute-start.1 = (f32[1,32,512]{2,1,0:T(8,128)S(1)}, f32[1,32,512]{2,1,0:T(8,128)S(1)}, u32[]{:S(2)}, u32[]{:S(2)}) collective-permute-start(f32[1,32,512]{2,1,0:T(8,128)S(1)} %get-tuple-element.147), channel_id=1, source_target_pairs={{0,16},{4,20},{8,24},{12,28},{16,0},{20,4},{24,8},{28,12},{1,17},{... | collective-permute-start | bytes 196616 | tf_op jit(solution)/shard_map/while/body/ppermute | solution.py:41
  18.5 4.9 %collective-permute-start.2 = (f32[1,32,512]{2,1,0:T(8,128)S(1)}, f32[1,32,512]{2,1,0:T(8,128)S(1)}, u32[]{:S(2)}, u32[]{:S(2)}) collective-permute-start(f32[1,32,512]{2,1,0:T(8,128)S(1)} %get-tuple-element.148), channel_id=1, source_target_pairs={{0,8},{4,12},{8,0},{12,4},{16,24},{20,28},{24,16},{28,20},{1,9},{5... | collective-permute-start | bytes 196616 | tf_op jit(solution)/shard_map/while/body/ppermute | solution.py:41
  20.0 5.2 %collective-permute-start.3 = (f32[1,32,512]{2,1,0:T(8,128)S(1)}, f32[1,32,512]{2,1,0:T(8,128)S(1)}, u32[]{:S(2)}, u32[]{:S(2)}) collective-permute-start(f32[1,32,512]{2,1,0:T(8,128)S(1)} %get-tuple-element.150), channel_id=1, source_target_pairs={{0,24},{4,28},{8,16},{12,20},{16,8},{20,12},{24,0},{28,4},{1,25},{... | collective-permute-start | bytes 196616 | tf_op jit(solution)/shard_map/while/body/ppermute | solution.py:41
  29.9 1.8 %collective-permute-start.7 = (f32[4,32,768]{2,1,0:T(8,128)S(1)}, f32[4,32,768]{2,1,0:T(8,128)S(1)}, u32[]{:S(2)}, u32[]{:S(2)}) collective-permute-start(f32[4,32,768]{2,1,0:T(8,128)S(1)} %get-tuple-element.66), channel_id=1, source_target_pairs={{0,4},{4,0},{8,12},{12,8},{16,20},{20,16},{24,28},{28,24},{1,5},{5... | collective-permute-start | bytes 1179656 | tf_op jit(solution)/shard_map/ppermute | solution.py:41
  31.7 8.9 %copy-start.3 = (f32[1,32,512]{2,1,0:T(8,128)S(1)}, f32[1,32,512]{2,1,0:T(8,128)}, u32[]{:S(2)}) copy-start(f32[1,32,512]{2,1,0:T(8,128)} %get-tuple-element.71.refs_5_) | copy-start | bytes 196612
  32.3 5.9 %collective-permute-start.10 = (f32[1,32,768]{2,1,0:T(8,128)S(1)}, f32[1,32,768]{2,1,0:T(8,128)S(1)}, u32[]{:S(2)}, u32[]{:S(2)}) collective-permute-start(f32[1,32,768]{2,1,0:T(8,128)S(1)} %get-tuple-element.70), channel_id=1, source_target_pairs={{0,16},{4,20},{8,24},{12,28},{16,0},{20,4},{24,8},{28,12},{1,17},{... | collective-permute-start | bytes 294920 | tf_op jit(solution)/shard_map/ppermute | solution.py:41
  33.9 6.5 %collective-permute-start.8 = (f32[1,32,768]{2,1,0:T(8,128)S(1)}, f32[1,32,768]{2,1,0:T(8,128)S(1)}, u32[]{:S(2)}, u32[]{:S(2)}) collective-permute-start(f32[1,32,768]{2,1,0:T(8,128)S(1)} %get-tuple-element.68), channel_id=1, source_target_pairs={{0,24},{4,28},{8,16},{12,20},{16,8},{20,12},{24,0},{28,4},{1,25},{... | collective-permute-start | bytes 294920 | tf_op jit(solution)/shard_map/ppermute | solution.py:41
  35.3 5.2 %collective-permute-start.9 = (f32[1,32,768]{2,1,0:T(8,128)S(1)}, f32[1,32,768]{2,1,0:T(8,128)S(1)}, u32[]{:S(2)}, u32[]{:S(2)}) collective-permute-start(f32[1,32,768]{2,1,0:T(8,128)S(1)} %get-tuple-element.69), channel_id=1, source_target_pairs={{0,8},{4,12},{8,0},{12,4},{16,24},{20,28},{24,16},{28,20},{1,9},{5... | collective-permute-start | bytes 294920 | tf_op jit(solution)/shard_map/ppermute | solution.py:41
  41.1 6.3 %collective-permute-start.11 = (f32[1,32,1280]{2,1,0:T(8,128)S(1)}, f32[1,32,1280]{2,1,0:T(8,128)S(1)}, u32[]{:S(2)}, u32[]{:S(2)}) collective-permute-start(f32[1,32,1280]{2,1,0:T(8,128)S(1)} %shard_map.39), channel_id=1, source_target_pairs={{0,1},{1,0},{2,3},{3,2},{4,6},{5,7},{6,4},{7,5},{8,9},{9,8},{10,11... | collective-permute-start | bytes 491528 | tf_op jit(solution)/shard_map/ppermute | solution.py:168
  47.5 6.3 %collective-permute-start.12 = (f32[1,32,1280]{2,1,0:T(8,128)S(1)}, f32[1,32,1280]{2,1,0:T(8,128)S(1)}, u32[]{:S(2)}, u32[]{:S(2)}) collective-permute-start(f32[1,32,1280]{2,1,0:T(8,128)S(1)} %add.70), channel_id=1, source_target_pairs={{0,2},{1,3},{2,0},{3,1},{4,5},{5,4},{6,7},{7,6},{8,10},{9,11},{10,... | collective-permute-start | bytes 491528 | tf_op jit(solution)/shard_map/ppermute | solution.py:168
  53.9 10.6 %copy-start = (f32[2,256,256]{2,1,0:T(8,128)S(1)}, f32[2,256,256]{2,1,0:T(8,128)}, u32[]{:S(2)}) copy-start(f32[2,256,256]{2,1,0:T(8,128)} %refs_3_.1) | copy-start | bytes 1572868
  53.9 6.3 %collective-permute-start.13 = (f32[1,32,1280]{2,1,0:T(8,128)S(1)}, f32[1,32,1280]{2,1,0:T(8,128)S(1)}, u32[]{:S(2)}, u32[]{:S(2)}) collective-permute-start(f32[1,32,1280]{2,1,0:T(8,128)S(1)} %get-tuple-element.92), channel_id=1, source_target_pairs={{0,24},{4,28},{8,16},{12,20},{16,8},{20,12},{24,0},{28,4},{1,25},{... | collective-permute-start | bytes 491528 | tf_op jit(solution)/shard_map/ppermute | solution.py:41
  56.2 5.8 %collective-permute-start.14 = (f32[1,32,1280]{2,1,0:T(8,128)S(1)}, f32[1,32,1280]{2,1,0:T(8,128)S(1)}, u32[]{:S(2)}, u32[]{:S(2)}) collective-permute-start(f32[1,32,1280]{2,1,0:T(8,128)S(1)} %get-tuple-element.92), channel_id=1, source_target_pairs={{0,8},{4,12},{8,0},{12,4},{16,24},{20,28},{24,16},{28,20},{1,9},{5... | collective-permute-start | bytes 491528 | tf_op jit(solution)/shard_map/ppermute | solution.py:41
  56.9 5.3 %collective-permute-start.15 = (f32[1,32,1280]{2,1,0:T(8,128)S(1)}, f32[1,32,1280]{2,1,0:T(8,128)S(1)}, u32[]{:S(2)}, u32[]{:S(2)}) collective-permute-start(f32[1,32,1280]{2,1,0:T(8,128)S(1)} %get-tuple-element.92), channel_id=1, source_target_pairs={{0,16},{4,20},{8,24},{12,28},{16,0},{20,4},{24,8},{28,12},{1,17},{... | collective-permute-start | bytes 491528 | tf_op jit(solution)/shard_map/ppermute | solution.py:41
  62.3 2.2 %collective-permute-start.16 = (f32[4,32,1280]{2,1,0:T(8,128)S(1)}, f32[4,32,1280]{2,1,0:T(8,128)S(1)}, u32[]{:S(2)}, u32[]{:S(2)}) collective-permute-start(f32[4,32,1280]{2,1,0:T(8,128)S(1)} %constant_dynamic-update-slice_fusion.refs_1_), channel_id=1, source_target_pairs={{0,4},{4,0},{8,12},{12,8},{16,20},{20,16},{24,28},{28,24},{1,5},{5... | collective-permute-start | bytes 1966088 | tf_op jit(solution)/shard_map/ppermute | solution.py:41
  67.7 12.8 %collective-permute-start.17 = (f32[512,128]{1,0:T(8,128)S(1)}, f32[512,128]{1,0:T(8,128)S(1)}, u32[]{:S(2)}, u32[]{:S(2)}) collective-permute-start(f32[512,128]{1,0:T(8,128)S(1)} %get-tuple-element.73), channel_id=1, source_target_pairs={{0,1},{1,0},{2,3},{3,2},{4,5},{5,4},{6,7},{7,6},{8,9},{9,8},{10,11... | collective-permute-start | bytes 786440 | tf_op jit(solution)/shard_map/ppermute | solution.py:41
  69.9 18.3 %collective-permute-start.18 = (f32[512,128]{1,0:T(8,128)S(1)}, f32[512,128]{1,0:T(8,128)S(1)}, u32[]{:S(2)}, u32[]{:S(2)}) collective-permute-start(f32[512,128]{1,0:T(8,128)S(1)} %get-tuple-element.74), channel_id=1, source_target_pairs={{0,2},{1,3},{2,0},{3,1},{4,6},{5,7},{6,4},{7,5},{8,10},{9,11},{10,... | collective-permute-start | bytes 786440 | tf_op jit(solution)/shard_map/ppermute | solution.py:41
  70.3 24.4 %collective-permute-start.19 = (f32[512,128]{1,0:T(8,128)S(1)}, f32[512,128]{1,0:T(8,128)S(1)}, u32[]{:S(2)}, u32[]{:S(2)}) collective-permute-start(f32[512,128]{1,0:T(8,128)S(1)} %get-tuple-element.75), channel_id=1, source_target_pairs={{0,3},{1,2},{2,1},{3,0},{4,7},{5,6},{6,5},{7,4},{8,11},{9,10},{10,... | collective-permute-start | bytes 786440 | tf_op jit(solution)/shard_map/ppermute | solution.py:41
  94.7 1.0 %copy-start.2 = (f32[4,512,128]{2,1,0:T(8,128)}, f32[4,512,128]{2,1,0:T(8,128)S(1)}, u32[]{:S(2)}) copy-start(f32[4,512,128]{2,1,0:T(8,128)S(1)} %bitcast_dynamic-update-slice_fusion) | copy-start | bytes 3145732

commit v3 on v0

v3 whole, which is shorter than its diff:
```python
import functools

import jax
import jax.numpy as jnp
from jax import lax
from jax.experimental import pallas as pl
from jax.experimental.pallas import tpu as pltpu
from jax.sharding import PartitionSpec as P

PLAIN = ((1,), (0,))
BY_TRANSPOSE = ((1,), (1,))
FROM_TRANSPOSE = ((0,), (0,))


def split(value):
    high = value.astype(jnp.bfloat16)
    return high, (value - high.astype(jnp.float32)).astype(jnp.bfloat16)


def product(left, right, contract=PLAIN):
    def one(a, b):
        return lax.dot_general(a, b, (contract, ((), ())), preferred_element_type=jnp.float32)

    return one(left[0], right[0]) + (one(left[0], right[1]) + one(left[1], right[0]))


def kernel_call(body, shapes, place, *args, scratch=()):
    specs = [pl.BlockSpec(memory_space=pltpu.SMEM)]
    specs += [pl.BlockSpec(memory_space=pltpu.VMEM)] * len(args)
    return pl.pallas_call(
        body,
        out_shape=[jax.ShapeDtypeStruct(shape, jnp.float32) for shape in shapes],
        in_specs=specs,
        out_specs=[pl.BlockSpec(memory_space=pltpu.VMEM)] * len(shapes),
        scratch_shapes=[pltpu.VMEM(shape, kind) for shape, kind in scratch],
        compiler_params=pltpu.CompilerParams(vmem_limit_bytes=24 * 1024 * 1024),
    )(place, *args)


def swap(block, axis, size, mask):
    return lax.ppermute(block, axis, [(i, i ^ mask) for i in range(size)])


def row_stages(size):
    stages = []
    shift = 0
    while (1 << shift) < size:
        bits = 1 if shift == 0 or (2 << shift) == size else 2
        stages.append((shift, 1 << bits))
        shift += bits
    return stages


def exchange_order(group):
    return [2, 1, 3] if group == 4 else list(range(1, group))


def join_kernel(steps, cols_size, *refs):
    place, blocks, out, sem = refs[0], refs[1 : 1 + len(steps)], refs[-2], refs[-1]
    copies = []
    for i, (step, block) in enumerate(zip(steps, blocks)):
        source = turn(place[0], -step, cols_size)
        copies.append(pltpu.make_async_copy(block, out.at[source], sem.at[i]))
    for copy in copies:
        copy.start()
    for copy in copies:
        copy.wait()


def turn(col, step, size):
    bits = size.bit_length() - 1

    def reverse(value):
        return sum(((value >> i) & 1) << (bits - 1 - i) for i in range(bits))

    return reverse((reverse(col) + step) & (size - 1))


def near_kernel(parts, groups, cols_size, *refs):
    place, pieces, (field, keep, send, high, low) = refs[0], refs[1:-5], refs[-5:]
    col, core = place[0], place[1] & 1
    own, near = pieces[0].shape[1], len(pieces)
    for i, piece in enumerate(pieces):
        at = pl.multiple_of((turn(col, -i * groups, cols_size) & (near - 1)) * own, own)
        for panel in range(2):
            rows = pl.ds(panel * near * own + at, own)
            high[rows, :], low[rows, :] = split(piece[panel])
    result = product((high[...], low[...]), split(field[...]))
    for j in range(parts // 2):
        rows = keep.shape[1]
        even = result[2 * j * rows : (2 * j + 1) * rows]
        odd = result[(2 * j + 1) * rows : (2 * j + 2) * rows]
        keep[j] = jnp.where(core == 0, even, odd)
        send[j] = jnp.where(core == 0, odd, even)


def far_kernel(parts, steps, groups, *refs):
    place, pieces = refs[0], refs[1:-8]
    field, keep, send, house, high, low, far_h, far_l = refs[-8:]
    col, core = place[0], place[1] & 1
    cols_size = len(pieces)
    own, near = pieces[0].shape[1], cols_size // groups
    mine = col // near
    for step, piece in zip(steps, pieces):
        block = turn(col, -step, cols_size)
        group = block // near
        at = pl.multiple_of(block * own, own)
        slot = group - jnp.where(group > mine, 1, 0)
        inside = pl.multiple_of((slot * 2 * near + (block & (near - 1))) * own, own)
        for panel in range(2):
            value = piece[panel]
            rows = pl.ds(at, own)
            house[panel, rows, :] = value
            value_h, value_l = split(value)
            high[panel, rows, :], low[panel, rows, :] = value_h, value_l
            if step % groups:
                rows = pl.ds(inside + panel * near * own, own)
                far_h[rows, :], far_l[rows, :] = value_h, value_l
    result = product((far_h[...], far_l[...]), split(field[...]))
    cross = product((high[1], low[1]), (high[0], low[0]), BY_TRANSPOSE)
    height = 2 * near * own
    count = height // parts
    rows = cross.shape[0] // parts
    side = keep.shape[2] // cross.shape[1]
    packed = -(-rows // side)
    for j in range(parts // 2):
        for out, odd in ((keep, core), (send, 1 - core)):

            def chosen(value, first, number, stride):
                even = value[first : first + number]
                return jnp.where(odd == 0, even, value[first + stride : first + stride + number])

            for slot in range(groups - 1):
                at = slot * count
                block = chosen(result, slot * height + 2 * j * count, count, count)
                out[j, at : at + count, :] = block
            at = (groups - 1) * count
            if packed * side != rows:
                out[j, at:, :] = jnp.zeros((packed, keep.shape[2]), jnp.float32)
            for i in range(rows // packed):
                block = chosen(cross, 2 * j * rows + i * packed, packed, rows)
                out[j, at:, i * cross.shape[1] : (i + 1) * cross.shape[1]] = block


def add_split_kernel(shift, group, *refs):
    place, sources, outs = refs[0], refs[1:-group], refs[-group:]
    me = (place[1] >> shift) & (group - 1)
    for a in range(outs[0].shape[0]):
        for k, out in enumerate(outs):
            at = a * group + (me ^ k)
            total = sources[0][at]
            for source in sources[1:]:
                total = total + source[at]
            out[a] = total


def assemble_kernel(shift, group, *refs):
    place, blocks, out = refs[0], refs[1:-1], refs[-1]
    me = (place[1] >> shift) & (group - 1)
    for k, block in enumerate(blocks):
        for a in range(block.shape[0]):
            out[a * group + (me ^ k)] = block[a]


def tail_kernel(cols_size, groups, shift, ks, *refs):
    group = len(ks)
    place, blocks = refs[0], refs[1 : 1 + 2 * group]
    factors, house, field = refs[1 + 2 * group : 4 + 2 * group]
    outs, weights, cross = refs[4 + 2 * group : -2], refs[-2], refs[-1]
    col, core = place[0], place[1] & 1
    me = (place[1] >> shift) & (group - 1)
    width = house.shape[1]
    parts = 2 * group * blocks[0].shape[0]
    height = 2 * width // groups
    count = height // parts
    rows = width // parts
    packed = blocks[0].shape[1] - groups * count
    for i, block in enumerate(blocks):
        for a in range(block.shape[0]):
            p = 2 * (a * group + (me ^ ks[i % group])) + (core if i < group else 1 - core)
            start = p * count
            panel = start // (height // 2)
            start = panel * width + start - panel * (height // 2)
            for j in range(groups):
                at = pl.multiple_of(start + j * (height // 2), count)
                weights[pl.ds(at, count), :] = block[a, j * count : (j + 1) * count]
            for j in range(rows // packed):
                at = pl.multiple_of(p * rows + j * packed, packed)
                cut = slice(j * width, (j + 1) * width)
                cross[pl.ds(at, packed), :] = block[a, groups * count :, cut]

    first = split(product(split(factors[0]), split(weights[:width])))
    second = weights[width:] - product(split(cross[...]), first)
    second = split(product(split(factors[1]), split(second)))
    update = product(split(house[0]), first, FROM_TRANSPOSE)
    update = update + product(split(house[1]), second, FROM_TRANSPOSE)
    cols = outs[0].shape[1]
    result = field[...] - update
    for c in range(cols_size):
        for step, out in enumerate(outs):

            @pl.when(turn(col, step, cols_size) == c)
            def _(c=c, out=out):
                out[...] = result[:, c * cols : (c + 1) * cols]


def all_reduce_cols(part, rows_size, cols_size):
    bits = cols_size.bit_length() - 1
    for step in range(bits):
        pairs = []
        for row in range(rows_size):
            mask = 1 << (bits - 1 - step if row & 1 else step)
            for col in range(cols_size):
                pairs.append((row * cols_size + col, row * cols_size + (col ^ mask)))
        other = lax.ppermute(part, ("row", "col"), pairs)
        if step == bits - 1:
            return part, other
        part = part + other


def make_per_device(rows_size, cols_size):
    stages = row_stages(rows_size)
    bf16 = jnp.bfloat16

    def scatter(place, sources, stages):
        for shift, group in stages[1:]:
            shape = (sources[0].shape[0] // group,) + sources[0].shape[1:]
            body = functools.partial(add_split_kernel, shift, group)
            cuts = kernel_call(body, [shape] * group, place, *sources)
            sources = [cuts[0]]
            for k in exchange_order(group):
                sources.append(swap(cuts[k], "row", rows_size, k << shift))
        return functools.reduce(jnp.add, sources)

    def gather(place, current):
        for shift, group in reversed(stages[2:]):
            blocks = [current] * group
            for k in exchange_order(group):
                blocks[k] = swap(current, "row", rows_size, k << shift)
            body = functools.partial(assemble_kernel, shift, group)
            shape = (current.shape[0] * group,) + current.shape[1:]
            (current,) = kernel_call(body, [shape], place, *blocks)
        shift, group = stages[1]
        blocks = [current]
        for k in exchange_order(group):
            blocks.append(swap(current, "row", rows_size, k << shift))
        return blocks + [swap(block, "row", rows_size, 1) for block in blocks]

    def per_device(vectors, panels, tfactors):
        col, row = lax.axis_index("col"), lax.axis_index("row")
        place = jnp.stack([col, row]).astype(jnp.int32)
        always = (row >> 16) == 0
        local_rows, eigvecs = vectors.shape
        own = panels.shape[2]
        width = own * cols_size
        out_cols = eigvecs // cols_size
        half = rows_size // 2
        near = max(1, rows_size // (2 * own))
        groups = cols_size // near
        count = 2 * near * own // rows_size
        packed = -(-(width // rows_size) * width // eigvecs)

        vt = panels.transpose(0, 2, 1)
        pieces = [None] * cols_size
        steps = list(range(cols_size - 1, 0, -1))
        for batch in (steps[:1], steps[1:] + [0]):
            for k in batch:
                at = turn(col, k, cols_size) * local_rows
                pieces[k] = lax.dynamic_slice_in_dim(vt, at, local_rows, 2)
            cuts, vt = lax.optimization_barrier(([pieces[k] for k in batch], vt))
            for k, cut in zip(batch, cuts):
                pairs = [(i, turn(i, k, cols_size)) for i in range(cols_size)]
                pieces[k] = lax.ppermute(cut, "col", pairs) if k else cut

        def near_part():
            keep, send = kernel_call(
                functools.partial(near_kernel, rows_size, groups, cols_size),
                [(half, count, eigvecs)] * 2,
                place,
                *pieces[::groups],
                vectors,
                scratch=[((2 * near * own, local_rows), bf16)] * 2,
            )
            bits = [(i, 2) for i in range(rows_size.bit_length() - 1)]
            return scatter(place, [keep, swap(send, "row", rows_size, 1)], bits)

        same = lax.cond(
            always, near_part, lambda: jnp.zeros((1, count, eigvecs), jnp.float32)
        )
        steps = steps + [0]
        cuts, same = lax.optimization_barrier(([pieces[k] for k in steps], same))
        keep, send, house = kernel_call(
            functools.partial(far_kernel, rows_size, steps, groups),
            [(half, (groups - 1) * count + packed, eigvecs)] * 2 + [(2, width, local_rows)],
            place,
            *cuts,
            vectors,
            scratch=[((2, width, local_rows), bf16)] * 2
            + [((2 * (cols_size - near) * own, local_rows), bf16)] * 2,
        )
        rest = scatter(place, [keep, swap(send, "row", rows_size, 1)], stages)
        blocks = [rest[:, i * count : (i + 1) * count] for i in range(groups - 1)]
        mine = col // near
        part = []
        for group in range(groups):
            block = blocks[max(group - 1, 0)]
            if 0 < group < groups - 1:
                block = jnp.where(mine < group, block, blocks[group])
            part.append(jnp.where(mine == group, same, block))
        part = jnp.concatenate(part + [rest[:, (groups - 1) * count :]], 1)
        part, other = all_reduce_cols(part, rows_size, cols_size)

        blocks = kernel_call(
            functools.partial(
                tail_kernel, cols_size, groups, stages[1][0], [0] + exchange_order(stages[1][1])
            ),
            [(local_rows, out_cols)] * cols_size,
            place,
            *gather(place, part + other),
            tfactors,
            house,
            vectors,
            scratch=[((2 * width, eigvecs), jnp.float32), ((width, width), jnp.float32)],
        )
        blocks = list(blocks)
        for k in [3, 1, 2]:
            pairs = [(i, turn(i, k, cols_size)) for i in range(cols_size)]
            blocks[k] = lax.ppermute(blocks[k], "col", pairs)
        steps = [0, *range(cols_size - 1, 0, -2), *range(2, cols_size, 2)]
        out = pl.pallas_call(
            functools.partial(join_kernel, steps, cols_size),
            out_shape=jax.ShapeDtypeStruct((cols_size, local_rows, out_cols), jnp.float32),
            in_specs=[pl.BlockSpec(memory_space=pltpu.SMEM)]
            + [pl.BlockSpec(memory_space=pltpu.VMEM)] * cols_size,
            out_specs=pl.BlockSpec(memory_space=pl.ANY),
            scratch_shapes=[pltpu.SemaphoreType.DMA((cols_size,))],
            compiler_params=pltpu.CompilerParams(vmem_limit_bytes=4 * 1024 * 1024),
        )(place, *[blocks[k] for k in steps])
        return out.reshape((cols_size * local_rows, out_cols))

    return per_device


def solution(mesh):
    in_specs = (P(("row", "col"), None), P(None, "row", "col"), P())
    out_specs = P("row", "col")
    per_device = make_per_device(mesh.shape["row"], mesh.shape["col"])
    return jax.shard_map(
        per_device, mesh=mesh, in_specs=in_specs, out_specs=out_specs, check_vma=False
    )
```

time: 237 us -> 90.8 us (0.38)
  waiting for transfers between devices: 149 us -> 56.1 us
  blocking collectives: 54.4 us -> 0 us
  starting transfers between devices: 0.08 us -> 23.4 us
  matrix products: 15.3 us -> 0 us
  between operations: 13.2 us -> 0.13 us
  Pallas kernels: 0 us -> 8.51 us
    psum x2 -> x0, waiting for transfers between devices: 108 us -> none  [the longest x1 55.2 us: per_device(): first_w = lax.psum(panel_product(first_vecs, field), 'row')]
    ppermute x0 -> x22, waiting for transfers between devices: none -> 56.1 us  [the longest x14 20.1 us: swap(): return lax.ppermute(block, axis, [(i, i ^ mask) for i in range(size)])]
    all_to_all x1 -> x0, blocking collectives: 54.4 us -> none  [per_device(): lax.all_to_all(vectors, 'col', split_axis=1, concat_axis=0, tiled=True)]
    all_gather x1 -> x0, waiting for transfers between devices: 40.8 us -> none  [per_device(): gathered = lax.all_gather(panels, 'col', axis=2, tiled=True)]
    ppermute x0 -> x22, starting transfers between devices: none -> 23.4 us  [the longest x14 10.6 us: swap(): return lax.ppermute(block, axis, [(i, i ^ mask) for i in range(size)])]
    dot_general x6 -> x0, matrix products: 15.3 us -> none  [the longest x4 8.39 us: matmul(): jnp.dot(left, right, precision=lax.Precision.HIGHEST, preferred_element_t...]
    pallas_call x0 -> x7, Pallas kernels: none -> 8.51 us  [the longest x6 6.97 us: kernel_call(): pl.pallas_call(body, out_shape=[jax.ShapeDtypeStruct(shape, jnp.float32)...]
  transfers between devices with their start and end apart: 3 -> 22, of which waited for: 3 -> 18; matrix products, arithmetic and copies ran while one was open for 1% -> 1% of each run, Pallas kernels for 0% -> 2%
where the time goes in v3:
time: 90.8 us; the launch traced here: 90.6 us
  waiting for transfers between devices  56.1 us (62%)
  starting transfers between devices  23.4 us (26%)
  Pallas kernels  8.51 us (9%)
  local copies, waits for them, and re-layouts  2.23 us (2%)
    ppermute x14, waiting for transfers between devices, swap(): return lax.ppermute(block, axis, [(i, i ^ mask) for i in range(size)])  20.1 us
    ppermute x3, waiting for transfers between devices, per_device(): blocks[k] = lax.ppermute(blocks[k], 'col', pairs)  19.6 us
    ppermute x14, starting transfers between devices, swap(): return lax.ppermute(block, axis, [(i, i ^ mask) for i in range(size)])  10.6 us
    ppermute x2, waiting for transfers between devices, all_reduce_cols(): other = lax.ppermute(part, ('row', 'col'), pairs)  8.88 us
    ppermute x3, waiting for transfers between devices, per_device(): pieces[k] = lax.ppermute(cut, 'col', pairs) if k else cut  7.59 us
    pallas_call x6, Pallas kernels, kernel_call(): pl.pallas_call(body, out_shape=[jax.ShapeDtypeStruct(shape, jnp.float32)...  6.97 us
    ppermute x3, starting transfers between devices, per_device(): blocks[k] = lax.ppermute(blocks[k], 'col', pairs)  4.9 us
    ppermute x3, starting transfers between devices, per_device(): pieces[k] = lax.ppermute(cut, 'col', pairs) if k else cut  4.17 us
  transfers between devices with their start and end apart: 22, of which 18 were waited for; matrix products, arithmetic and copies ran while one was open for 1% of the time, Pallas kernels for 2%

profile of v3, /device:TPU:8, one launch (start us, length us, event | category | flops | bytes accessed | tf_op | source)
XLA Modules:
  0.0 90.6 jit_solution(12788943183166170962)
XLA Ops:
  0.0 1.1 %dynamic-slice_bitcast_fusion = f32[2,64,512]{2,1,0:T(8,128)S(1)} fusion(f32[2,2048,64]{1,2,0:T(8,128)} %param.6, s32[]{:T(128)S(6)} %select_n.54), kind=kLoop, calls=%fused_computation | loop fusion | bytes 524292 | tf_op jit(solution)/shard_map/dynamic_slice | solution.py:269
  1.1 1.6 %collective-permute-start.3 = (f32[2,64,512]{2,1,0:T(8,128)S(1)}, f32[2,64,512]{2,1,0:T(8,128)S(1)}, u32[]{:S(2)}, u32[]{:S(2)}) collective-permute-start(f32[2,64,512]{2,1,0:T(8,128)S(1)} %dynamic-slice_bitcast_fusion), channel_id=1, source_target_pairs={{0,3},{1,2},{2,0},{3,1},{4,7},{5,6},{6,4},{7,5},{8,11},{9,10},{10,... | collective-permute-start | bytes 786440 | tf_op jit(solution)/shard_map/ppermute | solution.py:273
  2.7 1.2 %constant_dynamic-slice_fusion = (f32[2,64,512]{2,1,0:T(8,128)S(1)}, f32[2,64,512]{2,1,0:T(8,128)S(1)}, f32[2,64,512]{2,1,0:T(8,128)S(1)}) fusion(f32[2,64,2048]{2,1,0:T(8,128)} %bitcast.6, s32[]{:T(128)S(6)} %select_n.57, s32[]{:T(128)S(6)} %select_n.56, s32[]{:T(128)S(6)} %select_n.55), kind=kLoop, calls=%fused_computation.7 | loop fusion | bytes 1572876 | tf_op jit(solution)/shard_map/dynamic_slice | solution.py:269
  3.9 2.5 %collective-permute-start.4 = (f32[2,64,512]{2,1,0:T(8,128)S(1)}, f32[2,64,512]{2,1,0:T(8,128)S(1)}, u32[]{:S(2)}, u32[]{:S(2)}) collective-permute-start(f32[2,64,512]{2,1,0:T(8,128)S(1)} %get-tuple-element.46), channel_id=1, source_target_pairs={{0,1},{1,0},{2,3},{3,2},{4,5},{5,4},{6,7},{7,6},{8,9},{9,8},{10,11... | collective-permute-start | bytes 786440 | tf_op jit(solution)/shard_map/ppermute | solution.py:273
  6.4 0.1 pad_add_fusion.refs_0_
  6.5 11.8 %conditional.1 = (f32[1,16,512]{2,1,0:T(8,128)S(1)}) conditional(s32[]{:T(128)} %convert_element_type.3, () %tuple.16, (s32[2]{0:T(128)S(1)}, f32[2,64,512]{2,1,0:T(8,128)S(1)}, f32[512,512]{1,0:T(8,128)S(1)}) %tuple.23), branch_computations={%region_0.0_spmd, %region_1.0_spmd} | conditional | flops 8192 | bytes 1015936 | solution.py:287
  6.5 1.0 %branch_1_fun.3 = (f32[4,16,512]{2,1,0:T(8,128)S(1)}, f32[4,16,512]{2,1,0:T(8,128)S(1)}) custom-call(s32[2]{0:T(128)S(1)} %get-tuple-element.14.refs_0_, f32[2,64,512]{2,1,0:T(8,128)S(1)} %get-tuple-element.15.refs_1_, f32[512,512]{1,0:T(8,128)S(1)} %get-tuple-element.16.refs_2_), custom_call_target="tpu_custom_call" | custom-call | tf_op jit(solution)/shard_map/cond/branch_1_fun/pallas_call | solution.py:30
  7.4 0.1 collective-permute-start
  7.5 1.3 %collective-permute-done.refs_2_ = f32[4,16,512]{2,1,0:T(8,128)S(1)} collective-permute-done((f32[4,16,512]{2,1,0:T(8,128)S(1)}, f32[4,16,512]{2,1,0:T(8,128)S(1)}, u32[]{:S(2)}, u32[]{:S(2)}) %collective-permute-start) | collective-permute-done | bytes 131104 | tf_op jit(solution)/shard_map/cond/branch_1_fun/ppermute | solution.py:41
  8.9 0.6 branch_1_fun.4
  9.4 1.6 %collective-permute-start.1 = (f32[2,16,512]{2,1,0:T(8,128)S(1)}, f32[2,16,512]{2,1,0:T(8,128)S(1)}, u32[]{:S(2)}, u32[]{:S(2)}) collective-permute-start(f32[2,16,512]{2,1,0:T(8,128)S(1)} %get-tuple-element.20), channel_id=1, source_target_pairs={{0,8},{4,12},{8,0},{12,4},{16,24},{20,28},{24,16},{28,20},{1,9},{5... | collective-permute-start | bytes 196616 | tf_op jit(solution)/shard_map/cond/branch_1_fun/ppermute | solution.py:41
  11.0 2.8 %collective-permute-done.1.refs_2_ = f32[2,16,512]{2,1,0:T(8,128)S(1)} collective-permute-done((f32[2,16,512]{2,1,0:T(8,128)S(1)}, f32[2,16,512]{2,1,0:T(8,128)S(1)}, u32[]{:S(2)}, u32[]{:S(2)}) %collective-permute-start.1) | collective-permute-done | bytes 65568 | tf_op jit(solution)/shard_map/cond/branch_1_fun/ppermute | solution.py:41
  13.8 0.6 branch_1_fun.5
  14.3 1.6 %collective-permute-start.2 = (f32[1,16,512]{2,1,0:T(8,128)S(1)}, f32[1,16,512]{2,1,0:T(8,128)S(1)}, u32[]{:S(2)}, u32[]{:S(2)}) collective-permute-start(f32[1,16,512]{2,1,0:T(8,128)S(1)} %get-tuple-element.22), channel_id=1, source_target_pairs={{0,16},{4,20},{8,24},{12,28},{16,0},{20,4},{24,8},{28,12},{1,17},{... | collective-permute-start | bytes 98312 | tf_op jit(solution)/shard_map/cond/branch_1_fun/ppermute | solution.py:41
  15.9 2.4 %collective-permute-done.2 = f32[1,16,512]{2,1,0:T(8,128)S(1)} collective-permute-done((f32[1,16,512]{2,1,0:T(8,128)S(1)}, f32[1,16,512]{2,1,0:T(8,128)S(1)}, u32[]{:S(2)}, u32[]{:S(2)}) %collective-permute-start.2) | collective-permute-done | bytes 32800 | tf_op jit(solution)/shard_map/cond/branch_1_fun/ppermute | solution.py:41
  18.3 3.4 %collective-permute-done.4.refs_2_ = f32[2,64,512]{2,1,0:T(8,128)S(1)} collective-permute-done((f32[2,64,512]{2,1,0:T(8,128)S(1)}, f32[2,64,512]{2,1,0:T(8,128)S(1)}, u32[]{:S(2)}, u32[]{:S(2)}) %collective-permute-start.4) | collective-permute-done | bytes 262176 | tf_op jit(solution)/shard_map/ppermute | solution.py:273
  21.8 4.1 %collective-permute-done.5.refs_3_ = f32[2,64,512]{2,1,0:T(8,128)S(1)} collective-permute-done((f32[2,64,512]{2,1,0:T(8,128)S(1)}, f32[2,64,512]{2,1,0:T(8,128)S(1)}, u32[]{:S(2)}, u32[]{:S(2)}) %collective-permute-start.5) | collective-permute-done | bytes 262176 | tf_op jit(solution)/shard_map/ppermute | solution.py:273
  25.9 1.6 %shard_map.37 = (f32[4,64,512]{2,1,0:T(8,128)S(1)}, f32[4,64,512]{2,1,0:T(8,128)S(1)}, f32[2,256,512]{2,1,0:T(8,128)S(1)}) custom-call(s32[2]{0:T(128)S(1)} %pad_add_fusion.refs_0_, f32[2,64,512]{2,1,0:T(8,128)S(1)} %collective-permute-done.3.refs_1_, f32[2,64,512]{2,1,0:T(8,128)S(1)} %collective-permute-done.4.refs_2_, ...), custom_call_target="tpu_custom_call" | custom-call | tf_op jit(solution)/shard_map/pallas_call | solution.py:30
  27.5 0.1 collective-permute-start.6
  27.6 1.9 %collective-permute-done.6.refs_2_ = f32[4,64,512]{2,1,0:T(8,128)S(1)} collective-permute-done((f32[4,64,512]{2,1,0:T(8,128)S(1)}, f32[4,64,512]{2,1,0:T(8,128)S(1)}, u32[]{:S(2)}, u32[]{:S(2)}) %collective-permute-start.6) | collective-permute-done | bytes 524320 | tf_op jit(solution)/shard_map/ppermute | solution.py:41
  29.5 0.6 shard_map.38
  30.1 1.6 %collective-permute-start.7 = (f32[1,64,512]{2,1,0:T(8,128)S(1)}, f32[1,64,512]{2,1,0:T(8,128)S(1)}, u32[]{:S(2)}, u32[]{:S(2)}) collective-permute-start(f32[1,64,512]{2,1,0:T(8,128)S(1)} %get-tuple-element.57), channel_id=1, source_target_pairs={{0,16},{4,20},{8,24},{12,28},{16,0},{20,4},{24,8},{28,12},{1,17},{... | collective-permute-start | bytes 393224 | tf_op jit(solution)/shard_map/ppermute | solution.py:41
  31.8 1.5 %collective-permute-start.8 = (f32[1,64,512]{2,1,0:T(8,128)S(1)}, f32[1,64,512]{2,1,0:T(8,128)S(1)}, u32[]{:S(2)}, u32[]{:S(2)}) collective-permute-start(f32[1,64,512]{2,1,0:T(8,128)S(1)} %get-tuple-element.58), channel_id=1, source_target_pairs={{0,8},{4,12},{8,0},{12,4},{16,24},{20,28},{24,16},{28,20},{1,9},{5... | collective-permute-start | bytes 393224 | tf_op jit(solution)/shard_map/ppermute | solution.py:41
  33.3 0.4 collective-permute-start.9
  33.7 2.0 %collective-permute-done.7 = f32[1,64,512]{2,1,0:T(8,128)S(1)} collective-permute-done((f32[1,64,512]{2,1,0:T(8,128)S(1)}, f32[1,64,512]{2,1,0:T(8,128)S(1)}, u32[]{:S(2)}, u32[]{:S(2)}) %collective-permute-start.7) | collective-permute-done | bytes 131104 | tf_op jit(solution)/shard_map/ppermute | solution.py:41
  35.7 2.4 %collective-permute-done.8 = f32[1,64,512]{2,1,0:T(8,128)S(1)} collective-permute-done((f32[1,64,512]{2,1,0:T(8,128)S(1)}, f32[1,64,512]{2,1,0:T(8,128)S(1)}, u32[]{:S(2)}, u32[]{:S(2)}) %collective-permute-start.8) | collective-permute-done | bytes 131104 | tf_op jit(solution)/shard_map/ppermute | solution.py:41
  38.1 1.6 %collective-permute-done.9 = f32[1,64,512]{2,1,0:T(8,128)S(1)} collective-permute-done((f32[1,64,512]{2,1,0:T(8,128)S(1)}, f32[1,64,512]{2,1,0:T(8,128)S(1)}, u32[]{:S(2)}, u32[]{:S(2)}) %collective-permute-start.9) | collective-permute-done | bytes 131104 | tf_op jit(solution)/shard_map/ppermute | solution.py:41
  39.8 0.0 copy-start
  39.9 0.1 collective-permute-start.10
  39.9 5.3 %collective-permute-done.10 = f32[1,80,512]{2,1,0:T(8,128)S(1)} collective-permute-done((f32[1,80,512]{2,1,0:T(8,128)S(1)}, f32[1,80,512]{2,1,0:T(8,128)S(1)}, u32[]{:S(2)}, u32[]{:S(2)}) %collective-permute-start.10) | collective-permute-done | bytes 163872 | tf_op jit(solution)/shard_map/ppermute | solution.py:215
  45.3 3.6 %collective-permute-start.11 = (f32[1,80,512]{2,1,0:T(8,128)S(1)}, f32[1,80,512]{2,1,0:T(8,128)S(1)}, u32[]{:S(2)}, u32[]{:S(2)}) collective-permute-start(f32[1,80,512]{2,1,0:T(8,128)S(1)} %add.73), channel_id=1, source_target_pairs={{0,2},{1,3},{2,0},{3,1},{4,5},{5,4},{6,7},{7,6},{8,10},{9,11},{10,... | collective-permute-start | bytes 491528 | tf_op jit(solution)/shard_map/ppermute | solution.py:215
  48.9 3.6 %collective-permute-done.11 = f32[1,80,512]{2,1,0:T(8,128)S(1)} collective-permute-done((f32[1,80,512]{2,1,0:T(8,128)S(1)}, f32[1,80,512]{2,1,0:T(8,128)S(1)}, u32[]{:S(2)}, u32[]{:S(2)}) %collective-permute-start.11) | collective-permute-done | bytes 163872 | tf_op jit(solution)/shard_map/ppermute | solution.py:215
  52.5 2.2 %collective-permute-start.14 = (f32[1,80,512]{2,1,0:T(8,128)S(1)}, f32[1,80,512]{2,1,0:T(8,128)S(1)}, u32[]{:S(2)}, u32[]{:S(2)}) collective-permute-start(f32[1,80,512]{2,1,0:T(8,128)S(1)} %add.74.refs_1_), channel_id=1, source_target_pairs={{0,24},{4,28},{8,16},{12,20},{16,8},{20,12},{24,0},{28,4},{1,25},{... | collective-permute-start | bytes 491528 | tf_op jit(solution)/shard_map/ppermute | solution.py:41
  54.7 0.5 collective-permute-start.13
  55.2 0.8 collective-permute-start.12
  56.1 2.7 %collective-permute-done.14.refs_4_ = f32[1,80,512]{2,1,0:T(8,128)S(1)} collective-permute-done((f32[1,80,512]{2,1,0:T(8,128)S(1)}, f32[1,80,512]{2,1,0:T(8,128)S(1)}, u32[]{:S(2)}, u32[]{:S(2)}) %collective-permute-start.14) | collective-permute-done | bytes 163872 | tf_op jit(solution)/shard_map/ppermute | solution.py:41
  58.8 1.5 %collective-permute-done.13.refs_3_ = f32[1,80,512]{2,1,0:T(8,128)S(1)} collective-permute-done((f32[1,80,512]{2,1,0:T(8,128)S(1)}, f32[1,80,512]{2,1,0:T(8,128)S(1)}, u32[]{:S(2)}, u32[]{:S(2)}) %collective-permute-start.13) | collective-permute-done | bytes 163872 | tf_op jit(solution)/shard_map/ppermute | solution.py:41
  60.3 0.3 collective-permute-done.12.refs_2_
  60.6 0.2 collective-permute-start.16
  60.8 0.9 collective-permute-done.17.refs_7_
  61.7 0.3 collective-permute-done.16.refs_6_
  62.0 2.7 %shard_map.39 = (f32[512,128]{1,0:T(8,128)S(1)}, f32[512,128]{1,0:T(8,128)S(1)}, f32[512,128]{1,0:T(8,128)S(1)}, f32[512,128]{1,0:T(8,128)S(1)}) custom-call(s32[2]{0:T(128)S(1)} %pad_add_fusion.refs_0_, f32[1,80,512]{2,1,0:T(8,128)S(1)} %add.74.refs_1_, f32[1,80,512]{2,1,0:T(8,128)S(1)} %collective-permute-done.12.refs_2_, ...), custom_call_target="tpu_custom_call" | custom-call | tf_op jit(solution)/shard_map/pallas_call | solution.py:30
  64.6 0.9 collective-permute-start.19
  65.5 2.6 %collective-permute-start.20 = (f32[512,128]{1,0:T(8,128)S(1)}, f32[512,128]{1,0:T(8,128)S(1)}, u32[]{:S(2)}, u32[]{:S(2)}) collective-permute-start(f32[512,128]{1,0:T(8,128)S(1)} %get-tuple-element.63), channel_id=1, source_target_pairs={{0,2},{1,3},{2,1},{3,0},{4,6},{5,7},{6,5},{7,4},{8,10},{9,11},{10,... | collective-permute-start | bytes 786440 | tf_op jit(solution)/shard_map/ppermute | solution.py:328
  68.1 1.4 %collective-permute-start.21 = (f32[512,128]{1,0:T(8,128)S(1)}, f32[512,128]{1,0:T(8,128)S(1)}, u32[]{:S(2)}, u32[]{:S(2)}) collective-permute-start(f32[512,128]{1,0:T(8,128)S(1)} %get-tuple-element.64), channel_id=1, source_target_pairs={{0,1},{1,0},{2,3},{3,2},{4,5},{5,4},{6,7},{7,6},{8,9},{9,8},{10,11... | collective-permute-start | bytes 786440 | tf_op jit(solution)/shard_map/ppermute | solution.py:328
  69.5 13.8 %collective-permute-done.19.refs_2_ = f32[512,128]{1,0:T(8,128)S(1)} collective-permute-done((f32[512,128]{1,0:T(8,128)S(1)}, f32[512,128]{1,0:T(8,128)S(1)}, u32[]{:S(2)}, u32[]{:S(2)}) %collective-permute-start.19) | collective-permute-done | bytes 262176 | tf_op jit(solution)/shard_map/ppermute | solution.py:328
  83.4 5.7 %collective-permute-done.20.refs_3_ = f32[512,128]{1,0:T(8,128)S(1)} collective-permute-done((f32[512,128]{1,0:T(8,128)S(1)}, f32[512,128]{1,0:T(8,128)S(1)}, u32[]{:S(2)}, u32[]{:S(2)}) %collective-permute-start.20) | collective-permute-done | bytes 262176 | tf_op jit(solution)/shard_map/ppermute | solution.py:328
  89.1 1.5 %shard_map.40 = f32[4,512,128]{2,1,0:T(8,128)} custom-call(s32[2]{0:T(128)S(1)} %pad_add_fusion.refs_0_, f32[512,128]{1,0:T(8,128)S(1)} %get-tuple-element.61.refs_1_, f32[512,128]{1,0:T(8,128)S(1)} %collective-permute-done.19.refs_2_, f32[512,128]{1,0:T(8,128)S(1)} %collective-permute-done.20.refs_3_, f32[512,128]{1,0:T(8,128)S(1)} %collective-permute-done.21.refs_4_), custom_call_target="tpu_custom_call" | custom-call | tf_op jit(solution)/shard_map/pallas_call | solution.py:330
  (20 shorter events, 0.2 us)
Async XLA Ops:
  0.0 6.5 %copy-start.1 = (f32[512,512]{1,0:T(8,128)S(1)}, f32[512,512]{1,0:T(8,128)}, u32[]{:S(2)}) copy-start(f32[512,512]{1,0:T(8,128)} %refs_11_.1) | copy-start | bytes 3145732
  1.1 17.2 %collective-permute-start.3 = (f32[2,64,512]{2,1,0:T(8,128)S(1)}, f32[2,64,512]{2,1,0:T(8,128)S(1)}, u32[]{:S(2)}, u32[]{:S(2)}) collective-permute-start(f32[2,64,512]{2,1,0:T(8,128)S(1)} %dynamic-slice_bitcast_fusion), channel_id=1, source_target_pairs={{0,3},{1,2},{2,0},{3,1},{4,7},{5,6},{6,4},{7,5},{8,11},{9,10},{10,... | collective-permute-start | bytes 786440 | tf_op jit(solution)/shard_map/ppermute | solution.py:273
  3.9 17.9 %collective-permute-start.4 = (f32[2,64,512]{2,1,0:T(8,128)S(1)}, f32[2,64,512]{2,1,0:T(8,128)S(1)}, u32[]{:S(2)}, u32[]{:S(2)}) collective-permute-start(f32[2,64,512]{2,1,0:T(8,128)S(1)} %get-tuple-element.46), channel_id=1, source_target_pairs={{0,1},{1,0},{2,3},{3,2},{4,5},{5,4},{6,7},{7,6},{8,9},{9,8},{10,11... | collective-permute-start | bytes 786440 | tf_op jit(solution)/shard_map/ppermute | solution.py:273
  6.4 19.5 %collective-permute-start.5 = (f32[2,64,512]{2,1,0:T(8,128)S(1)}, f32[2,64,512]{2,1,0:T(8,128)S(1)}, u32[]{:S(2)}, u32[]{:S(2)}) collective-permute-start(f32[2,64,512]{2,1,0:T(8,128)S(1)} %get-tuple-element.47), channel_id=1, source_target_pairs={{0,2},{1,3},{2,1},{3,0},{4,6},{5,7},{6,5},{7,4},{8,10},{9,11},{10,... | collective-permute-start | bytes 786440 | tf_op jit(solution)/shard_map/ppermute | solution.py:273
  7.4 1.4 %collective-permute-start = (f32[4,16,512]{2,1,0:T(8,128)S(1)}, f32[4,16,512]{2,1,0:T(8,128)S(1)}, u32[]{:S(2)}, u32[]{:S(2)}) collective-permute-start(f32[4,16,512]{2,1,0:T(8,128)S(1)} %get-tuple-element.18), channel_id=1, source_target_pairs={{0,4},{4,0},{8,12},{12,8},{16,20},{20,16},{24,28},{28,24},{1,5},{5... | collective-permute-start | bytes 393224 | tf_op jit(solution)/shard_map/cond/branch_1_fun/ppermute | solution.py:41
  9.4 4.3 %collective-permute-start.1 = (f32[2,16,512]{2,1,0:T(8,128)S(1)}, f32[2,16,512]{2,1,0:T(8,128)S(1)}, u32[]{:S(2)}, u32[]{:S(2)}) collective-permute-start(f32[2,16,512]{2,1,0:T(8,128)S(1)} %get-tuple-element.20), channel_id=1, source_target_pairs={{0,8},{4,12},{8,0},{12,4},{16,24},{20,28},{24,16},{28,20},{1,9},{5... | collective-permute-start | bytes 196616 | tf_op jit(solution)/shard_map/cond/branch_1_fun/ppermute | solution.py:41
  14.3 4.0 %collective-permute-start.2 = (f32[1,16,512]{2,1,0:T(8,128)S(1)}, f32[1,16,512]{2,1,0:T(8,128)S(1)}, u32[]{:S(2)}, u32[]{:S(2)}) collective-permute-start(f32[1,16,512]{2,1,0:T(8,128)S(1)} %get-tuple-element.22), channel_id=1, source_target_pairs={{0,16},{4,20},{8,24},{12,28},{16,0},{20,4},{24,8},{28,12},{1,17},{... | collective-permute-start | bytes 98312 | tf_op jit(solution)/shard_map/cond/branch_1_fun/ppermute | solution.py:41
  27.5 2.0 %collective-permute-start.6 = (f32[4,64,512]{2,1,0:T(8,128)S(1)}, f32[4,64,512]{2,1,0:T(8,128)S(1)}, u32[]{:S(2)}, u32[]{:S(2)}) collective-permute-start(f32[4,64,512]{2,1,0:T(8,128)S(1)} %get-tuple-element.55), channel_id=1, source_target_pairs={{0,4},{4,0},{8,12},{12,8},{16,20},{20,16},{24,28},{28,24},{1,5},{5... | collective-permute-start | bytes 1572872 | tf_op jit(solution)/shard_map/ppermute | solution.py:41
  30.1 5.6 %collective-permute-start.7 = (f32[1,64,512]{2,1,0:T(8,128)S(1)}, f32[1,64,512]{2,1,0:T(8,128)S(1)}, u32[]{:S(2)}, u32[]{:S(2)}) collective-permute-start(f32[1,64,512]{2,1,0:T(8,128)S(1)} %get-tuple-element.57), channel_id=1, source_target_pairs={{0,16},{4,20},{8,24},{12,28},{16,0},{20,4},{24,8},{28,12},{1,17},{... | collective-permute-start | bytes 393224 | tf_op jit(solution)/shard_map/ppermute | solution.py:41
  31.8 6.4 %collective-permute-start.8 = (f32[1,64,512]{2,1,0:T(8,128)S(1)}, f32[1,64,512]{2,1,0:T(8,128)S(1)}, u32[]{:S(2)}, u32[]{:S(2)}) collective-permute-start(f32[1,64,512]{2,1,0:T(8,128)S(1)} %get-tuple-element.58), channel_id=1, source_target_pairs={{0,8},{4,12},{8,0},{12,4},{16,24},{20,28},{24,16},{28,20},{1,9},{5... | collective-permute-start | bytes 393224 | tf_op jit(solution)/shard_map/ppermute | solution.py:41
  33.3 6.5 %collective-permute-start.9 = (f32[1,64,512]{2,1,0:T(8,128)S(1)}, f32[1,64,512]{2,1,0:T(8,128)S(1)}, u32[]{:S(2)}, u32[]{:S(2)}) collective-permute-start(f32[1,64,512]{2,1,0:T(8,128)S(1)} %get-tuple-element.59), channel_id=1, source_target_pairs={{0,24},{4,28},{8,16},{12,20},{16,8},{20,12},{24,0},{28,4},{1,25},{... | collective-permute-start | bytes 393224 | tf_op jit(solution)/shard_map/ppermute | solution.py:41
  39.8 22.1 %copy-start = (f32[2,256,256]{2,1,0:T(8,128)S(1)}, f32[2,256,256]{2,1,0:T(8,128)}, u32[]{:S(2)}) copy-start(f32[2,256,256]{2,1,0:T(8,128)} %refs_9_.1) | copy-start | bytes 1572868
  39.9 5.4 %collective-permute-start.10 = (f32[1,80,512]{2,1,0:T(8,128)S(1)}, f32[1,80,512]{2,1,0:T(8,128)S(1)}, u32[]{:S(2)}, u32[]{:S(2)}) collective-permute-start(f32[1,80,512]{2,1,0:T(8,128)S(1)} %slice_dynamic-update-slice_fusion), channel_id=1, source_target_pairs={{0,1},{1,0},{2,3},{3,2},{4,6},{5,7},{6,4},{7,5},{8,9},{9,8},{10,11... | collective-permute-start | bytes 491528 | tf_op jit(solution)/shard_map/ppermute | solution.py:215
  45.3 7.2 %collective-permute-start.11 = (f32[1,80,512]{2,1,0:T(8,128)S(1)}, f32[1,80,512]{2,1,0:T(8,128)S(1)}, u32[]{:S(2)}, u32[]{:S(2)}) collective-permute-start(f32[1,80,512]{2,1,0:T(8,128)S(1)} %add.73), channel_id=1, source_target_pairs={{0,2},{1,3},{2,0},{3,1},{4,5},{5,4},{6,7},{7,6},{8,10},{9,11},{10,... | collective-permute-start | bytes 491528 | tf_op jit(solution)/shard_map/ppermute | solution.py:215
  52.5 6.3 %collective-permute-start.14 = (f32[1,80,512]{2,1,0:T(8,128)S(1)}, f32[1,80,512]{2,1,0:T(8,128)S(1)}, u32[]{:S(2)}, u32[]{:S(2)}) collective-permute-start(f32[1,80,512]{2,1,0:T(8,128)S(1)} %add.74.refs_1_), channel_id=1, source_target_pairs={{0,24},{4,28},{8,16},{12,20},{16,8},{20,12},{24,0},{28,4},{1,25},{... | collective-permute-start | bytes 491528 | tf_op jit(solution)/shard_map/ppermute | solution.py:41
  54.7 5.6 %collective-permute-start.13 = (f32[1,80,512]{2,1,0:T(8,128)S(1)}, f32[1,80,512]{2,1,0:T(8,128)S(1)}, u32[]{:S(2)}, u32[]{:S(2)}) collective-permute-start(f32[1,80,512]{2,1,0:T(8,128)S(1)} %add.74.refs_1_), channel_id=1, source_target_pairs={{0,8},{4,12},{8,0},{12,4},{16,24},{20,28},{24,16},{28,20},{1,9},{5... | collective-permute-start | bytes 491528 | tf_op jit(solution)/shard_map/ppermute | solution.py:41
  55.2 5.3 %collective-permute-start.12 = (f32[1,80,512]{2,1,0:T(8,128)S(1)}, f32[1,80,512]{2,1,0:T(8,128)S(1)}, u32[]{:S(2)}, u32[]{:S(2)}) collective-permute-start(f32[1,80,512]{2,1,0:T(8,128)S(1)} %add.74.refs_1_), channel_id=1, source_target_pairs={{0,16},{4,20},{8,24},{12,28},{16,0},{20,4},{24,8},{28,12},{1,17},{... | collective-permute-start | bytes 491528 | tf_op jit(solution)/shard_map/ppermute | solution.py:41
  56.1 4.7 %collective-permute-start.15 = (f32[1,80,512]{2,1,0:T(8,128)S(1)}, f32[1,80,512]{2,1,0:T(8,128)S(1)}, u32[]{:S(2)}, u32[]{:S(2)}) collective-permute-start(f32[1,80,512]{2,1,0:T(8,128)S(1)} %add.74.refs_1_), channel_id=1, source_target_pairs={{0,4},{4,0},{8,12},{12,8},{16,20},{20,16},{24,28},{28,24},{1,5},{5... | collective-permute-start | bytes 491528 | tf_op jit(solution)/shard_map/ppermute | solution.py:41
  58.8 2.0 %collective-permute-start.18 = (f32[1,80,512]{2,1,0:T(8,128)S(1)}, f32[1,80,512]{2,1,0:T(8,128)S(1)}, u32[]{:S(2)}, u32[]{:S(2)}) collective-permute-start(f32[1,80,512]{2,1,0:T(8,128)S(1)} %collective-permute-done.14.refs_4_), channel_id=1, source_target_pairs={{0,4},{4,0},{8,12},{12,8},{16,20},{20,16},{24,28},{28,24},{1,5},{5... | collective-permute-start | bytes 491528 | tf_op jit(solution)/shard_map/ppermute | solution.py:41
  60.3 1.4 %collective-permute-start.17 = (f32[1,80,512]{2,1,0:T(8,128)S(1)}, f32[1,80,512]{2,1,0:T(8,128)S(1)}, u32[]{:S(2)}, u32[]{:S(2)}) collective-permute-start(f32[1,80,512]{2,1,0:T(8,128)S(1)} %collective-permute-done.13.refs_3_), channel_id=1, source_target_pairs={{0,4},{4,0},{8,12},{12,8},{16,20},{20,16},{24,28},{28,24},{1,5},{5... | collective-permute-start | bytes 491528 | tf_op jit(solution)/shard_map/ppermute | solution.py:41
  60.6 1.4 %collective-permute-start.16 = (f32[1,80,512]{2,1,0:T(8,128)S(1)}, f32[1,80,512]{2,1,0:T(8,128)S(1)}, u32[]{:S(2)}, u32[]{:S(2)}) collective-permute-start(f32[1,80,512]{2,1,0:T(8,128)S(1)} %collective-permute-done.12.refs_2_), channel_id=1, source_target_pairs={{0,4},{4,0},{8,12},{12,8},{16,20},{20,16},{24,28},{28,24},{1,5},{5... | collective-permute-start | bytes 491528 | tf_op jit(solution)/shard_map/ppermute | solution.py:41
  64.6 18.7 %collective-permute-start.19 = (f32[512,128]{1,0:T(8,128)S(1)}, f32[512,128]{1,0:T(8,128)S(1)}, u32[]{:S(2)}, u32[]{:S(2)}) collective-permute-start(f32[512,128]{1,0:T(8,128)S(1)} %get-tuple-element.62), channel_id=1, source_target_pairs={{0,3},{1,2},{2,0},{3,1},{4,7},{5,6},{6,4},{7,5},{8,11},{9,10},{10,... | collective-permute-start | bytes 786440 | tf_op jit(solution)/shard_map/ppermute | solution.py:328
  65.5 23.6 %collective-permute-start.20 = (f32[512,128]{1,0:T(8,128)S(1)}, f32[512,128]{1,0:T(8,128)S(1)}, u32[]{:S(2)}, u32[]{:S(2)}) collective-permute-start(f32[512,128]{1,0:T(8,128)S(1)} %get-tuple-element.63), channel_id=1, source_target_pairs={{0,2},{1,3},{2,1},{3,0},{4,6},{5,7},{6,5},{7,4},{8,10},{9,11},{10,... | collective-permute-start | bytes 786440 | tf_op jit(solution)/shard_map/ppermute | solution.py:328
  68.1 21.0 %collective-permute-start.21 = (f32[512,128]{1,0:T(8,128)S(1)}, f32[512,128]{1,0:T(8,128)S(1)}, u32[]{:S(2)}, u32[]{:S(2)}) collective-permute-start(f32[512,128]{1,0:T(8,128)S(1)} %get-tuple-element.64), channel_id=1, source_target_pairs={{0,1},{1,0},{2,3},{3,2},{4,5},{5,4},{6,7},{7,6},{8,9},{9,8},{10,11... | collective-permute-start | bytes 786440 | tf_op jit(solution)/shard_map/ppermute | solution.py:328

commit v4 on v3

--- a/solution.py
+++ b/solution.py
@@ -24,17 +24,19 @@
     return one(left[0], right[0]) + (one(left[0], right[1]) + one(left[1], right[0]))
 
 
-def kernel_call(body, shapes, place, *args, scratch=()):
-    specs = [pl.BlockSpec(memory_space=pltpu.SMEM)]
-    specs += [pl.BlockSpec(memory_space=pltpu.VMEM)] * len(args)
+def here():
+    return lax.axis_index("col"), lax.axis_index("row")
+
+
+def kernel_call(body, shapes, *args, scratch=()):
     return pl.pallas_call(
         body,
         out_shape=[jax.ShapeDtypeStruct(shape, jnp.float32) for shape in shapes],
-        in_specs=specs,
+        in_specs=[pl.BlockSpec(memory_space=pltpu.VMEM)] * len(args),
         out_specs=[pl.BlockSpec(memory_space=pltpu.VMEM)] * len(shapes),
         scratch_shapes=[pltpu.VMEM(shape, kind) for shape, kind in scratch],
         compiler_params=pltpu.CompilerParams(vmem_limit_bytes=24 * 1024 * 1024),
-    )(place, *args)
+    )(*args)
 
 
 def swap(block, axis, size, mask):
@@ -56,7 +58,7 @@
 
 
 def join_kernel(steps, cols_size, *refs):
-    place, blocks, out, sem = refs[0], refs[1 : 1 + len(steps)], refs[-2], refs[-1]
+    place, blocks, out, sem = here(), refs[: len(steps)], refs[-2], refs[-1]
     copies = []
     for i, (step, block) in enumerate(zip(steps, blocks)):
         source = turn(place[0], -step, cols_size)
@@ -77,7 +79,7 @@
 
 
 def near_kernel(parts, groups, cols_size, *refs):
-    place, pieces, (field, keep, send, high, low) = refs[0], refs[1:-5], refs[-5:]
+    place, pieces, (field, keep, send, high, low) = here(), refs[:-5], refs[-5:]
     col, core = place[0], place[1] & 1
     own, near = pieces[0].shape[1], len(pieces)
     for i, piece in enumerate(pieces):
@@ -95,7 +97,7 @@
 
 
 def far_kernel(parts, steps, groups, *refs):
-    place, pieces = refs[0], refs[1:-8]
+    place, pieces = here(), refs[:-8]
     field, keep, send, house, high, low, far_h, far_l = refs[-8:]
     col, core = place[0], place[1] & 1
     cols_size = len(pieces)
@@ -143,7 +145,7 @@
 
 
 def add_split_kernel(shift, group, *refs):
-    place, sources, outs = refs[0], refs[1:-group], refs[-group:]
+    place, sources, outs = here(), refs[:-group], refs[-group:]
     me = (place[1] >> shift) & (group - 1)
     for a in range(outs[0].shape[0]):
         for k, out in enumerate(outs):
@@ -155,7 +157,7 @@
 
 
 def assemble_kernel(shift, group, *refs):
-    place, blocks, out = refs[0], refs[1:-1], refs[-1]
+    place, blocks, out = here(), refs[:-1], refs[-1]
     me = (place[1] >> shift) & (group - 1)
     for k, block in enumerate(blocks):
         for a in range(block.shape[0]):
@@ -164,9 +166,9 @@
 
 def tail_kernel(cols_size, groups, shift, ks, *refs):
     group = len(ks)
-    place, blocks = refs[0], refs[1 : 1 + 2 * group]
-    factors, house, field = refs[1 + 2 * group : 4 + 2 * group]
-    outs, weights, cross = refs[4 + 2 * group : -2], refs[-2], refs[-1]
+    place, blocks = here(), refs[: 2 * group]
+    factors, house, field = refs[2 * group : 3 + 2 * group]
+    outs, weights, cross = refs[3 + 2 * group : -2], refs[-2], refs[-1]
     col, core = place[0], place[1] & 1
     me = (place[1] >> shift) & (group - 1)
     width = house.shape[1]
@@ -222,24 +224,24 @@
     stages = row_stages(rows_size)
     bf16 = jnp.bfloat16
 
-    def scatter(place, sources, stages):
+    def scatter(sources, stages):
         for shift, group in stages[1:]:
             shape = (sources[0].shape[0] // group,) + sources[0].shape[1:]
             body = functools.partial(add_split_kernel, shift, group)
-            cuts = kernel_call(body, [shape] * group, place, *sources)
+            cuts = kernel_call(body, [shape] * group, *sources)
             sources = [cuts[0]]
             for k in exchange_order(group):
                 sources.append(swap(cuts[k], "row", rows_size, k << shift))
         return functools.reduce(jnp.add, sources)
 
-    def gather(place, current):
+    def gather(current):
         for shift, group in reversed(stages[2:]):
             blocks = [current] * group
             for k in exchange_order(group):
                 blocks[k] = swap(current, "row", rows_size, k << shift)
             body = functools.partial(assemble_kernel, shift, group)
             shape = (current.shape[0] * group,) + current.shape[1:]
-            (current,) = kernel_call(body, [shape], place, *blocks)
+            (current,) = kernel_call(body, [shape], *blocks)
         shift, group = stages[1]
         blocks = [current]
         for k in exchange_order(group):
@@ -248,7 +250,6 @@
 
     def per_device(vectors, panels, tfactors):
         col, row = lax.axis_index("col"), lax.axis_index("row")
-        place = jnp.stack([col, row]).astype(jnp.int32)
         always = (row >> 16) == 0
         local_rows, eigvecs = vectors.shape
         own = panels.shape[2]
@@ -276,13 +277,12 @@
             keep, send = kernel_call(
                 functools.partial(near_kernel, rows_size, groups, cols_size),
                 [(half, count, eigvecs)] * 2,
-                place,
                 *pieces[::groups],
                 vectors,
                 scratch=[((2 * near * own, local_rows), bf16)] * 2,
             )
             bits = [(i, 2) for i in range(rows_size.bit_length() - 1)]
-            return scatter(place, [keep, swap(send, "row", rows_size, 1)], bits)
+            return scatter([keep, swap(send, "row", rows_size, 1)], bits)
 
         same = lax.cond(
             always, near_part, lambda: jnp.zeros((1, count, eigvecs), jnp.float32)
@@ -292,13 +292,12 @@
         keep, send, house = kernel_call(
             functools.partial(far_kernel, rows_size, steps, groups),
             [(half, (groups - 1) * count + packed, eigvecs)] * 2 + [(2, width, local_rows)],
-            place,
             *cuts,
             vectors,
             scratch=[((2, width, local_rows), bf16)] * 2
             + [((2 * (cols_size - near) * own, local_rows), bf16)] * 2,
         )
-        rest = scatter(place, [keep, swap(send, "row", rows_size, 1)], stages)
+        rest = scatter([keep, swap(send, "row", rows_size, 1)], stages)
         blocks = [rest[:, i * count : (i + 1) * count] for i in range(groups - 1)]
         mine = col // near
         part = []
@@ -315,8 +314,7 @@
                 tail_kernel, cols_size, groups, stages[1][0], [0] + exchange_order(stages[1][1])
             ),
             [(local_rows, out_cols)] * cols_size,
-            place,
-            *gather(place, part + other),
+            *gather(part + other),
             tfactors,
             house,
             vectors,
@@ -330,12 +328,11 @@
         out = pl.pallas_call(
             functools.partial(join_kernel, steps, cols_size),
             out_shape=jax.ShapeDtypeStruct((cols_size, local_rows, out_cols), jnp.float32),
-            in_specs=[pl.BlockSpec(memory_space=pltpu.SMEM)]
-            + [pl.BlockSpec(memory_space=pltpu.VMEM)] * cols_size,
+            in_specs=[pl.BlockSpec(memory_space=pltpu.VMEM)] * cols_size,
             out_specs=pl.BlockSpec(memory_space=pl.ANY),
             scratch_shapes=[pltpu.SemaphoreType.DMA((cols_size,))],
             compiler_params=pltpu.CompilerParams(vmem_limit_bytes=4 * 1024 * 1024),
-        )(place, *[blocks[k] for k in steps])
+        )(*[blocks[k] for k in steps])
         return out.reshape((cols_size * local_rows, out_cols))
 
     return per_device

time: 90.8 us -> 88.6 us (0.976)
  Pallas kernels: 8.51 us -> 4.72 us
  waiting for transfers between devices: 56.1 us -> 57.8 us
    pallas_call x6, Pallas kernels: 6.97 us -> 3.73 us  [kernel_call(): pl.pallas_call(body, out_shape=[jax.ShapeDtypeStruct(shape, jnp.float32)...]
    ppermute x3, waiting for transfers between devices: 7.59 us -> 9.3 us  [per_device(): pieces[k] = lax.ppermute(cut, 'col', pairs) if k else cut]
  transfers between devices with their start and end apart: 22 -> 22, of which waited for: 18 -> 18; matrix products, arithmetic and copies ran while one was open for 1% -> 1% of each run, Pallas kernels for 2% -> 1%
where the time goes in v4:
time: 88.6 us; the launch traced here: 88.5 us
  waiting for transfers between devices  57.8 us (65%)
  starting transfers between devices  23.4 us (26%)
  Pallas kernels  4.72 us (5%)
  local copies, waits for them, and re-layouts  2.23 us (3%)
    ppermute x14, waiting for transfers between devices, swap(): return lax.ppermute(block, axis, [(i, i ^ mask) for i in range(size)])  20.1 us
    ppermute x3, waiting for transfers between devices, per_device(): blocks[k] = lax.ppermute(blocks[k], 'col', pairs)  19.6 us
    ppermute x14, starting transfers between devices, swap(): return lax.ppermute(block, axis, [(i, i ^ mask) for i in range(size)])  10.6 us
    ppermute x3, waiting for transfers between devices, per_device(): pieces[k] = lax.ppermute(cut, 'col', pairs) if k else cut  9.3 us
    ppermute x2, waiting for transfers between devices, all_reduce_cols(): other = lax.ppermute(part, ('row', 'col'), pairs)  8.88 us
    ppermute x3, starting transfers between devices, per_device(): blocks[k] = lax.ppermute(blocks[k], 'col', pairs)  4.89 us
    ppermute x3, starting transfers between devices, per_device(): pieces[k] = lax.ppermute(cut, 'col', pairs) if k else cut  4.17 us
    pallas_call x6, Pallas kernels, kernel_call(): pl.pallas_call(body, out_shape=[jax.ShapeDtypeStruct(shape, jnp.float32)...  3.73 us
  transfers between devices with their start and end apart: 22, of which 18 were waited for; matrix products, arithmetic and copies ran while one was open for 1% of the time, Pallas kernels for 1%

profile of v4, /device:TPU:8, one launch (start us, length us, event | category | flops | bytes accessed | tf_op | source)
XLA Modules:
  0.0 88.5 jit_solution(7093389691767493612)
XLA Ops:
  0.0 1.1 %dynamic-slice_bitcast_fusion = f32[2,64,512]{2,1,0:T(8,128)S(1)} fusion(f32[2,2048,64]{1,2,0:T(8,128)} %param.6, s32[]{:T(128)S(6)} %select_n.54), kind=kLoop, calls=%fused_computation | loop fusion | bytes 524292 | tf_op jit(solution)/shard_map/dynamic_slice | solution.py:270
  1.1 1.6 %collective-permute-start.3 = (f32[2,64,512]{2,1,0:T(8,128)S(1)}, f32[2,64,512]{2,1,0:T(8,128)S(1)}, u32[]{:S(2)}, u32[]{:S(2)}) collective-permute-start(f32[2,64,512]{2,1,0:T(8,128)S(1)} %dynamic-slice_bitcast_fusion), channel_id=1, source_target_pairs={{0,3},{1,2},{2,0},{3,1},{4,7},{5,6},{6,4},{7,5},{8,11},{9,10},{10,... | collective-permute-start | bytes 786440 | tf_op jit(solution)/shard_map/ppermute | solution.py:274
  2.7 1.2 %constant_dynamic-slice_fusion = (f32[2,64,512]{2,1,0:T(8,128)S(1)}, f32[2,64,512]{2,1,0:T(8,128)S(1)}, f32[2,64,512]{2,1,0:T(8,128)S(1)}) fusion(f32[2,64,2048]{2,1,0:T(8,128)} %bitcast.4, s32[]{:T(128)S(6)} %select_n.57, s32[]{:T(128)S(6)} %select_n.56, s32[]{:T(128)S(6)} %select_n.55), kind=kLoop, calls=%fused_computation.7 | loop fusion | bytes 1572876 | tf_op jit(solution)/shard_map/dynamic_slice | solution.py:270
  3.9 2.5 %collective-permute-start.4 = (f32[2,64,512]{2,1,0:T(8,128)S(1)}, f32[2,64,512]{2,1,0:T(8,128)S(1)}, u32[]{:S(2)}, u32[]{:S(2)}) collective-permute-start(f32[2,64,512]{2,1,0:T(8,128)S(1)} %get-tuple-element.43), channel_id=1, source_target_pairs={{0,1},{1,0},{2,3},{3,2},{4,5},{5,4},{6,7},{7,6},{8,9},{9,8},{10,11... | collective-permute-start | bytes 786440 | tf_op jit(solution)/shard_map/ppermute | solution.py:274
  6.4 0.0 collective-permute-start.5
  6.4 10.2 %conditional.1 = (f32[1,16,512]{2,1,0:T(8,128)S(1)}) conditional(s32[]{:T(128)} %convert_element_type.3, () %tuple.16, (f32[2,64,512]{2,1,0:T(8,128)S(1)}, f32[512,512]{1,0:T(8,128)S(1)}) %tuple.23), branch_computations={%region_0.0_spmd, %region_1.0_spmd} | conditional | flops 8192 | bytes 1015936 | solution.py:287
  6.4 0.4 branch_1_fun.3
  6.8 0.1 collective-permute-start
  6.9 1.3 %collective-permute-done.refs_1_ = f32[4,16,512]{2,1,0:T(8,128)S(1)} collective-permute-done((f32[4,16,512]{2,1,0:T(8,128)S(1)}, f32[4,16,512]{2,1,0:T(8,128)S(1)}, u32[]{:S(2)}, u32[]{:S(2)}) %collective-permute-start) | collective-permute-done | bytes 131104 | tf_op jit(solution)/shard_map/cond/branch_1_fun/ppermute | solution.py:43
  8.3 1.5 %collective-permute-start.1 = (f32[2,16,512]{2,1,0:T(8,128)S(1)}, f32[2,16,512]{2,1,0:T(8,128)S(1)}, u32[]{:S(2)}, u32[]{:S(2)}) collective-permute-start(f32[2,16,512]{2,1,0:T(8,128)S(1)} %get-tuple-element.17), channel_id=1, source_target_pairs={{0,8},{4,12},{8,0},{12,4},{16,24},{20,28},{24,16},{28,20},{1,9},{5... | collective-permute-start | bytes 196616 | tf_op jit(solution)/shard_map/cond/branch_1_fun/ppermute | solution.py:43
  9.8 2.8 %collective-permute-done.1.refs_1_ = f32[2,16,512]{2,1,0:T(8,128)S(1)} collective-permute-done((f32[2,16,512]{2,1,0:T(8,128)S(1)}, f32[2,16,512]{2,1,0:T(8,128)S(1)}, u32[]{:S(2)}, u32[]{:S(2)}) %collective-permute-start.1) | collective-permute-done | bytes 65568 | tf_op jit(solution)/shard_map/cond/branch_1_fun/ppermute | solution.py:43
  12.6 1.6 %collective-permute-start.2 = (f32[1,16,512]{2,1,0:T(8,128)S(1)}, f32[1,16,512]{2,1,0:T(8,128)S(1)}, u32[]{:S(2)}, u32[]{:S(2)}) collective-permute-start(f32[1,16,512]{2,1,0:T(8,128)S(1)} %get-tuple-element.19), channel_id=1, source_target_pairs={{0,16},{4,20},{8,24},{12,28},{16,0},{20,4},{24,8},{28,12},{1,17},{... | collective-permute-start | bytes 98312 | tf_op jit(solution)/shard_map/cond/branch_1_fun/ppermute | solution.py:43
  14.2 2.4 %collective-permute-done.2 = f32[1,16,512]{2,1,0:T(8,128)S(1)} collective-permute-done((f32[1,16,512]{2,1,0:T(8,128)S(1)}, f32[1,16,512]{2,1,0:T(8,128)S(1)}, u32[]{:S(2)}, u32[]{:S(2)}) %collective-permute-start.2) | collective-permute-done | bytes 32800 | tf_op jit(solution)/shard_map/cond/branch_1_fun/ppermute | solution.py:43
  16.6 0.0 collective-permute-done.3.refs_0_
  16.6 5.2 %collective-permute-done.4.refs_1_ = f32[2,64,512]{2,1,0:T(8,128)S(1)} collective-permute-done((f32[2,64,512]{2,1,0:T(8,128)S(1)}, f32[2,64,512]{2,1,0:T(8,128)S(1)}, u32[]{:S(2)}, u32[]{:S(2)}) %collective-permute-start.4) | collective-permute-done | bytes 262176 | tf_op jit(solution)/shard_map/ppermute | solution.py:274
  21.8 4.1 %collective-permute-done.5.refs_2_ = f32[2,64,512]{2,1,0:T(8,128)S(1)} collective-permute-done((f32[2,64,512]{2,1,0:T(8,128)S(1)}, f32[2,64,512]{2,1,0:T(8,128)S(1)}, u32[]{:S(2)}, u32[]{:S(2)}) %collective-permute-start.5) | collective-permute-done | bytes 262176 | tf_op jit(solution)/shard_map/ppermute | solution.py:274
  25.9 1.1 %shard_map.37 = (f32[4,64,512]{2,1,0:T(8,128)S(1)}, f32[4,64,512]{2,1,0:T(8,128)S(1)}, f32[2,256,512]{2,1,0:T(8,128)S(1)}) custom-call(f32[2,64,512]{2,1,0:T(8,128)S(1)} %collective-permute-done.3.refs_0_, f32[2,64,512]{2,1,0:T(8,128)S(1)} %collective-permute-done.4.refs_1_, f32[2,64,512]{2,1,0:T(8,128)S(1)} %collective-permute-done.5.refs_2_, ...), custom_call_target="tpu_custom_call" | custom-call | tf_op jit(solution)/shard_map/pallas_call | solution.py:32
  27.0 0.1 collective-permute-start.6
  27.1 1.9 %collective-permute-done.6.refs_1_ = f32[4,64,512]{2,1,0:T(8,128)S(1)} collective-permute-done((f32[4,64,512]{2,1,0:T(8,128)S(1)}, f32[4,64,512]{2,1,0:T(8,128)S(1)}, u32[]{:S(2)}, u32[]{:S(2)}) %collective-permute-start.6) | collective-permute-done | bytes 524320 | tf_op jit(solution)/shard_map/ppermute | solution.py:43
  29.0 0.1 shard_map.38
  29.0 1.6 %collective-permute-start.7 = (f32[1,64,512]{2,1,0:T(8,128)S(1)}, f32[1,64,512]{2,1,0:T(8,128)S(1)}, u32[]{:S(2)}, u32[]{:S(2)}) collective-permute-start(f32[1,64,512]{2,1,0:T(8,128)S(1)} %get-tuple-element.54), channel_id=1, source_target_pairs={{0,16},{4,20},{8,24},{12,28},{16,0},{20,4},{24,8},{28,12},{1,17},{... | collective-permute-start | bytes 393224 | tf_op jit(solution)/shard_map/ppermute | solution.py:43
  30.7 1.5 %collective-permute-start.8 = (f32[1,64,512]{2,1,0:T(8,128)S(1)}, f32[1,64,512]{2,1,0:T(8,128)S(1)}, u32[]{:S(2)}, u32[]{:S(2)}) collective-permute-start(f32[1,64,512]{2,1,0:T(8,128)S(1)} %get-tuple-element.55), channel_id=1, source_target_pairs={{0,8},{4,12},{8,0},{12,4},{16,24},{20,28},{24,16},{28,20},{1,9},{5... | collective-permute-start | bytes 393224 | tf_op jit(solution)/shard_map/ppermute | solution.py:43
  32.2 0.4 collective-permute-start.9
  32.6 2.0 %collective-permute-done.7 = f32[1,64,512]{2,1,0:T(8,128)S(1)} collective-permute-done((f32[1,64,512]{2,1,0:T(8,128)S(1)}, f32[1,64,512]{2,1,0:T(8,128)S(1)}, u32[]{:S(2)}, u32[]{:S(2)}) %collective-permute-start.7) | collective-permute-done | bytes 131104 | tf_op jit(solution)/shard_map/ppermute | solution.py:43
  34.6 2.4 %collective-permute-done.8 = f32[1,64,512]{2,1,0:T(8,128)S(1)} collective-permute-done((f32[1,64,512]{2,1,0:T(8,128)S(1)}, f32[1,64,512]{2,1,0:T(8,128)S(1)}, u32[]{:S(2)}, u32[]{:S(2)}) %collective-permute-start.8) | collective-permute-done | bytes 131104 | tf_op jit(solution)/shard_map/ppermute | solution.py:43
  37.1 1.6 %collective-permute-done.9 = f32[1,64,512]{2,1,0:T(8,128)S(1)} collective-permute-done((f32[1,64,512]{2,1,0:T(8,128)S(1)}, f32[1,64,512]{2,1,0:T(8,128)S(1)}, u32[]{:S(2)}, u32[]{:S(2)}) %collective-permute-start.9) | collective-permute-done | bytes 131104 | tf_op jit(solution)/shard_map/ppermute | solution.py:43
  38.7 0.0 copy-start
  38.8 0.1 collective-permute-start.10
  38.8 5.3 %collective-permute-done.10 = f32[1,80,512]{2,1,0:T(8,128)S(1)} collective-permute-done((f32[1,80,512]{2,1,0:T(8,128)S(1)}, f32[1,80,512]{2,1,0:T(8,128)S(1)}, u32[]{:S(2)}, u32[]{:S(2)}) %collective-permute-start.10) | collective-permute-done | bytes 163872 | tf_op jit(solution)/shard_map/ppermute | solution.py:217
  44.2 3.6 %collective-permute-start.11 = (f32[1,80,512]{2,1,0:T(8,128)S(1)}, f32[1,80,512]{2,1,0:T(8,128)S(1)}, u32[]{:S(2)}, u32[]{:S(2)}) collective-permute-start(f32[1,80,512]{2,1,0:T(8,128)S(1)} %add.73), channel_id=1, source_target_pairs={{0,2},{1,3},{2,0},{3,1},{4,5},{5,4},{6,7},{7,6},{8,10},{9,11},{10,... | collective-permute-start | bytes 491528 | tf_op jit(solution)/shard_map/ppermute | solution.py:217
  47.8 3.6 %collective-permute-done.11 = f32[1,80,512]{2,1,0:T(8,128)S(1)} collective-permute-done((f32[1,80,512]{2,1,0:T(8,128)S(1)}, f32[1,80,512]{2,1,0:T(8,128)S(1)}, u32[]{:S(2)}, u32[]{:S(2)}) %collective-permute-start.11) | collective-permute-done | bytes 163872 | tf_op jit(solution)/shard_map/ppermute | solution.py:217
  51.4 2.2 %collective-permute-start.14 = (f32[1,80,512]{2,1,0:T(8,128)S(1)}, f32[1,80,512]{2,1,0:T(8,128)S(1)}, u32[]{:S(2)}, u32[]{:S(2)}) collective-permute-start(f32[1,80,512]{2,1,0:T(8,128)S(1)} %add.74.refs_0_), channel_id=1, source_target_pairs={{0,24},{4,28},{8,16},{12,20},{16,8},{20,12},{24,0},{28,4},{1,25},{... | collective-permute-start | bytes 491528 | tf_op jit(solution)/shard_map/ppermute | solution.py:43
  53.6 0.5 collective-permute-start.13
  54.1 0.8 collective-permute-start.12
  55.0 2.7 %collective-permute-done.14.refs_3_ = f32[1,80,512]{2,1,0:T(8,128)S(1)} collective-permute-done((f32[1,80,512]{2,1,0:T(8,128)S(1)}, f32[1,80,512]{2,1,0:T(8,128)S(1)}, u32[]{:S(2)}, u32[]{:S(2)}) %collective-permute-start.14) | collective-permute-done | bytes 163872 | tf_op jit(solution)/shard_map/ppermute | solution.py:43
  57.7 1.5 %collective-permute-done.13.refs_2_ = f32[1,80,512]{2,1,0:T(8,128)S(1)} collective-permute-done((f32[1,80,512]{2,1,0:T(8,128)S(1)}, f32[1,80,512]{2,1,0:T(8,128)S(1)}, u32[]{:S(2)}, u32[]{:S(2)}) %collective-permute-start.13) | collective-permute-done | bytes 163872 | tf_op jit(solution)/shard_map/ppermute | solution.py:43
  59.2 0.0 collective-permute-start.17
  59.2 0.3 collective-permute-done.12.refs_1_
  59.5 0.2 collective-permute-start.16
  59.7 0.9 collective-permute-done.17.refs_6_
  60.6 0.3 collective-permute-done.16.refs_5_
  60.9 2.1 %shard_map.39 = (f32[512,128]{1,0:T(8,128)S(1)}, f32[512,128]{1,0:T(8,128)S(1)}, f32[512,128]{1,0:T(8,128)S(1)}, f32[512,128]{1,0:T(8,128)S(1)}) custom-call(f32[1,80,512]{2,1,0:T(8,128)S(1)} %add.74.refs_0_, f32[1,80,512]{2,1,0:T(8,128)S(1)} %collective-permute-done.12.refs_1_, f32[1,80,512]{2,1,0:T(8,128)S(1)} %collective-permute-done.13.refs_2_, ...), custom_call_target="tpu_custom_call" | custom-call | tf_op jit(solution)/shard_map/pallas_call | solution.py:32
  63.0 0.9 collective-permute-start.19
  63.9 2.6 %collective-permute-start.20 = (f32[512,128]{1,0:T(8,128)S(1)}, f32[512,128]{1,0:T(8,128)S(1)}, u32[]{:S(2)}, u32[]{:S(2)}) collective-permute-start(f32[512,128]{1,0:T(8,128)S(1)} %get-tuple-element.60), channel_id=1, source_target_pairs={{0,2},{1,3},{2,1},{3,0},{4,6},{5,7},{6,5},{7,4},{8,10},{9,11},{10,... | collective-permute-start | bytes 786440 | tf_op jit(solution)/shard_map/ppermute | solution.py:326
  66.5 1.4 %collective-permute-start.21 = (f32[512,128]{1,0:T(8,128)S(1)}, f32[512,128]{1,0:T(8,128)S(1)}, u32[]{:S(2)}, u32[]{:S(2)}) collective-permute-start(f32[512,128]{1,0:T(8,128)S(1)} %get-tuple-element.61), channel_id=1, source_target_pairs={{0,1},{1,0},{2,3},{3,2},{4,5},{5,4},{6,7},{7,6},{8,9},{9,8},{10,11... | collective-permute-start | bytes 786440 | tf_op jit(solution)/shard_map/ppermute | solution.py:326
  67.9 13.9 %collective-permute-done.19.refs_1_ = f32[512,128]{1,0:T(8,128)S(1)} collective-permute-done((f32[512,128]{1,0:T(8,128)S(1)}, f32[512,128]{1,0:T(8,128)S(1)}, u32[]{:S(2)}, u32[]{:S(2)}) %collective-permute-start.19) | collective-permute-done | bytes 262176 | tf_op jit(solution)/shard_map/ppermute | solution.py:326
  81.8 5.7 %collective-permute-done.20.refs_2_ = f32[512,128]{1,0:T(8,128)S(1)} collective-permute-done((f32[512,128]{1,0:T(8,128)S(1)}, f32[512,128]{1,0:T(8,128)S(1)}, u32[]{:S(2)}, u32[]{:S(2)}) %collective-permute-start.20) | collective-permute-done | bytes 262176 | tf_op jit(solution)/shard_map/ppermute | solution.py:326
  87.5 1.0 %shard_map.40 = f32[4,512,128]{2,1,0:T(8,128)} custom-call(f32[512,128]{1,0:T(8,128)S(1)} %get-tuple-element.58.refs_0_, f32[512,128]{1,0:T(8,128)S(1)} %collective-permute-done.19.refs_1_, f32[512,128]{1,0:T(8,128)S(1)} %collective-permute-done.20.refs_2_, f32[512,128]{1,0:T(8,128)S(1)} %collective-permute-done.21.refs_3_), custom_call_target="tpu_custom_call" | custom-call | tf_op jit(solution)/shard_map/pallas_call | solution.py:328
  (19 shorter events, 0.2 us)
Async XLA Ops:
  0.0 6.4 %copy-start.1 = (f32[512,512]{1,0:T(8,128)S(1)}, f32[512,512]{1,0:T(8,128)}, u32[]{:S(2)}) copy-start(f32[512,512]{1,0:T(8,128)} %refs_10_.1) | copy-start | bytes 3145732
  1.1 15.5 %collective-permute-start.3 = (f32[2,64,512]{2,1,0:T(8,128)S(1)}, f32[2,64,512]{2,1,0:T(8,128)S(1)}, u32[]{:S(2)}, u32[]{:S(2)}) collective-permute-start(f32[2,64,512]{2,1,0:T(8,128)S(1)} %dynamic-slice_bitcast_fusion), channel_id=1, source_target_pairs={{0,3},{1,2},{2,0},{3,1},{4,7},{5,6},{6,4},{7,5},{8,11},{9,10},{10,... | collective-permute-start | bytes 786440 | tf_op jit(solution)/shard_map/ppermute | solution.py:274
  3.9 17.9 %collective-permute-start.4 = (f32[2,64,512]{2,1,0:T(8,128)S(1)}, f32[2,64,512]{2,1,0:T(8,128)S(1)}, u32[]{:S(2)}, u32[]{:S(2)}) collective-permute-start(f32[2,64,512]{2,1,0:T(8,128)S(1)} %get-tuple-element.43), channel_id=1, source_target_pairs={{0,1},{1,0},{2,3},{3,2},{4,5},{5,4},{6,7},{7,6},{8,9},{9,8},{10,11... | collective-permute-start | bytes 786440 | tf_op jit(solution)/shard_map/ppermute | solution.py:274
  6.4 19.5 %collective-permute-start.5 = (f32[2,64,512]{2,1,0:T(8,128)S(1)}, f32[2,64,512]{2,1,0:T(8,128)S(1)}, u32[]{:S(2)}, u32[]{:S(2)}) collective-permute-start(f32[2,64,512]{2,1,0:T(8,128)S(1)} %get-tuple-element.44), channel_id=1, source_target_pairs={{0,2},{1,3},{2,1},{3,0},{4,6},{5,7},{6,5},{7,4},{8,10},{9,11},{10,... | collective-permute-start | bytes 786440 | tf_op jit(solution)/shard_map/ppermute | solution.py:274
  6.8 1.4 %collective-permute-start = (f32[4,16,512]{2,1,0:T(8,128)S(1)}, f32[4,16,512]{2,1,0:T(8,128)S(1)}, u32[]{:S(2)}, u32[]{:S(2)}) collective-permute-start(f32[4,16,512]{2,1,0:T(8,128)S(1)} %get-tuple-element.15), channel_id=1, source_target_pairs={{0,4},{4,0},{8,12},{12,8},{16,20},{20,16},{24,28},{28,24},{1,5},{5... | collective-permute-start | bytes 393224 | tf_op jit(solution)/shard_map/cond/branch_1_fun/ppermute | solution.py:43
  8.3 4.3 %collective-permute-start.1 = (f32[2,16,512]{2,1,0:T(8,128)S(1)}, f32[2,16,512]{2,1,0:T(8,128)S(1)}, u32[]{:S(2)}, u32[]{:S(2)}) collective-permute-start(f32[2,16,512]{2,1,0:T(8,128)S(1)} %get-tuple-element.17), channel_id=1, source_target_pairs={{0,8},{4,12},{8,0},{12,4},{16,24},{20,28},{24,16},{28,20},{1,9},{5... | collective-permute-start | bytes 196616 | tf_op jit(solution)/shard_map/cond/branch_1_fun/ppermute | solution.py:43
  12.6 4.0 %collective-permute-start.2 = (f32[1,16,512]{2,1,0:T(8,128)S(1)}, f32[1,16,512]{2,1,0:T(8,128)S(1)}, u32[]{:S(2)}, u32[]{:S(2)}) collective-permute-start(f32[1,16,512]{2,1,0:T(8,128)S(1)} %get-tuple-element.19), channel_id=1, source_target_pairs={{0,16},{4,20},{8,24},{12,28},{16,0},{20,4},{24,8},{28,12},{1,17},{... | collective-permute-start | bytes 98312 | tf_op jit(solution)/shard_map/cond/branch_1_fun/ppermute | solution.py:43
  27.0 2.0 %collective-permute-start.6 = (f32[4,64,512]{2,1,0:T(8,128)S(1)}, f32[4,64,512]{2,1,0:T(8,128)S(1)}, u32[]{:S(2)}, u32[]{:S(2)}) collective-permute-start(f32[4,64,512]{2,1,0:T(8,128)S(1)} %get-tuple-element.52), channel_id=1, source_target_pairs={{0,4},{4,0},{8,12},{12,8},{16,20},{20,16},{24,28},{28,24},{1,5},{5... | collective-permute-start | bytes 1572872 | tf_op jit(solution)/shard_map/ppermute | solution.py:43
  29.0 5.6 %collective-permute-start.7 = (f32[1,64,512]{2,1,0:T(8,128)S(1)}, f32[1,64,512]{2,1,0:T(8,128)S(1)}, u32[]{:S(2)}, u32[]{:S(2)}) collective-permute-start(f32[1,64,512]{2,1,0:T(8,128)S(1)} %get-tuple-element.54), channel_id=1, source_target_pairs={{0,16},{4,20},{8,24},{12,28},{16,0},{20,4},{24,8},{28,12},{1,17},{... | collective-permute-start | bytes 393224 | tf_op jit(solution)/shard_map/ppermute | solution.py:43
  30.7 6.4 %collective-permute-start.8 = (f32[1,64,512]{2,1,0:T(8,128)S(1)}, f32[1,64,512]{2,1,0:T(8,128)S(1)}, u32[]{:S(2)}, u32[]{:S(2)}) collective-permute-start(f32[1,64,512]{2,1,0:T(8,128)S(1)} %get-tuple-element.55), channel_id=1, source_target_pairs={{0,8},{4,12},{8,0},{12,4},{16,24},{20,28},{24,16},{28,20},{1,9},{5... | collective-permute-start | bytes 393224 | tf_op jit(solution)/shard_map/ppermute | solution.py:43
  32.2 6.5 %collective-permute-start.9 = (f32[1,64,512]{2,1,0:T(8,128)S(1)}, f32[1,64,512]{2,1,0:T(8,128)S(1)}, u32[]{:S(2)}, u32[]{:S(2)}) collective-permute-start(f32[1,64,512]{2,1,0:T(8,128)S(1)} %get-tuple-element.56), channel_id=1, source_target_pairs={{0,24},{4,28},{8,16},{12,20},{16,8},{20,12},{24,0},{28,4},{1,25},{... | collective-permute-start | bytes 393224 | tf_op jit(solution)/shard_map/ppermute | solution.py:43
  38.7 22.1 %copy-start = (f32[2,256,256]{2,1,0:T(8,128)S(1)}, f32[2,256,256]{2,1,0:T(8,128)}, u32[]{:S(2)}) copy-start(f32[2,256,256]{2,1,0:T(8,128)} %refs_8_.1) | copy-start | bytes 1572868
  38.8 5.4 %collective-permute-start.10 = (f32[1,80,512]{2,1,0:T(8,128)S(1)}, f32[1,80,512]{2,1,0:T(8,128)S(1)}, u32[]{:S(2)}, u32[]{:S(2)}) collective-permute-start(f32[1,80,512]{2,1,0:T(8,128)S(1)} %slice_dynamic-update-slice_fusion), channel_id=1, source_target_pairs={{0,1},{1,0},{2,3},{3,2},{4,6},{5,7},{6,4},{7,5},{8,9},{9,8},{10,11... | collective-permute-start | bytes 491528 | tf_op jit(solution)/shard_map/ppermute | solution.py:217
  44.2 7.2 %collective-permute-start.11 = (f32[1,80,512]{2,1,0:T(8,128)S(1)}, f32[1,80,512]{2,1,0:T(8,128)S(1)}, u32[]{:S(2)}, u32[]{:S(2)}) collective-permute-start(f32[1,80,512]{2,1,0:T(8,128)S(1)} %add.73), channel_id=1, source_target_pairs={{0,2},{1,3},{2,0},{3,1},{4,5},{5,4},{6,7},{7,6},{8,10},{9,11},{10,... | collective-permute-start | bytes 491528 | tf_op jit(solution)/shard_map/ppermute | solution.py:217
  51.4 6.3 %collective-permute-start.14 = (f32[1,80,512]{2,1,0:T(8,128)S(1)}, f32[1,80,512]{2,1,0:T(8,128)S(1)}, u32[]{:S(2)}, u32[]{:S(2)}) collective-permute-start(f32[1,80,512]{2,1,0:T(8,128)S(1)} %add.74.refs_0_), channel_id=1, source_target_pairs={{0,24},{4,28},{8,16},{12,20},{16,8},{20,12},{24,0},{28,4},{1,25},{... | collective-permute-start | bytes 491528 | tf_op jit(solution)/shard_map/ppermute | solution.py:43
  53.6 5.6 %collective-permute-start.13 = (f32[1,80,512]{2,1,0:T(8,128)S(1)}, f32[1,80,512]{2,1,0:T(8,128)S(1)}, u32[]{:S(2)}, u32[]{:S(2)}) collective-permute-start(f32[1,80,512]{2,1,0:T(8,128)S(1)} %add.74.refs_0_), channel_id=1, source_target_pairs={{0,8},{4,12},{8,0},{12,4},{16,24},{20,28},{24,16},{28,20},{1,9},{5... | collective-permute-start | bytes 491528 | tf_op jit(solution)/shard_map/ppermute | solution.py:43
  54.1 5.3 %collective-permute-start.12 = (f32[1,80,512]{2,1,0:T(8,128)S(1)}, f32[1,80,512]{2,1,0:T(8,128)S(1)}, u32[]{:S(2)}, u32[]{:S(2)}) collective-permute-start(f32[1,80,512]{2,1,0:T(8,128)S(1)} %add.74.refs_0_), channel_id=1, source_target_pairs={{0,16},{4,20},{8,24},{12,28},{16,0},{20,4},{24,8},{28,12},{1,17},{... | collective-permute-start | bytes 491528 | tf_op jit(solution)/shard_map/ppermute | solution.py:43
  55.0 4.7 %collective-permute-start.15 = (f32[1,80,512]{2,1,0:T(8,128)S(1)}, f32[1,80,512]{2,1,0:T(8,128)S(1)}, u32[]{:S(2)}, u32[]{:S(2)}) collective-permute-start(f32[1,80,512]{2,1,0:T(8,128)S(1)} %add.74.refs_0_), channel_id=1, source_target_pairs={{0,4},{4,0},{8,12},{12,8},{16,20},{20,16},{24,28},{28,24},{1,5},{5... | collective-permute-start | bytes 491528 | tf_op jit(solution)/shard_map/ppermute | solution.py:43
  57.7 2.0 %collective-permute-start.18 = (f32[1,80,512]{2,1,0:T(8,128)S(1)}, f32[1,80,512]{2,1,0:T(8,128)S(1)}, u32[]{:S(2)}, u32[]{:S(2)}) collective-permute-start(f32[1,80,512]{2,1,0:T(8,128)S(1)} %collective-permute-done.14.refs_3_), channel_id=1, source_target_pairs={{0,4},{4,0},{8,12},{12,8},{16,20},{20,16},{24,28},{28,24},{1,5},{5... | collective-permute-start | bytes 491528 | tf_op jit(solution)/shard_map/ppermute | solution.py:43
  59.2 1.4 %collective-permute-start.17 = (f32[1,80,512]{2,1,0:T(8,128)S(1)}, f32[1,80,512]{2,1,0:T(8,128)S(1)}, u32[]{:S(2)}, u32[]{:S(2)}) collective-permute-start(f32[1,80,512]{2,1,0:T(8,128)S(1)} %collective-permute-done.13.refs_2_), channel_id=1, source_target_pairs={{0,4},{4,0},{8,12},{12,8},{16,20},{20,16},{24,28},{28,24},{1,5},{5... | collective-permute-start | bytes 491528 | tf_op jit(solution)/shard_map/ppermute | solution.py:43
  59.5 1.4 %collective-permute-start.16 = (f32[1,80,512]{2,1,0:T(8,128)S(1)}, f32[1,80,512]{2,1,0:T(8,128)S(1)}, u32[]{:S(2)}, u32[]{:S(2)}) collective-permute-start(f32[1,80,512]{2,1,0:T(8,128)S(1)} %collective-permute-done.12.refs_1_), channel_id=1, source_target_pairs={{0,4},{4,0},{8,12},{12,8},{16,20},{20,16},{24,28},{28,24},{1,5},{5... | collective-permute-start | bytes 491528 | tf_op jit(solution)/shard_map/ppermute | solution.py:43
  63.0 18.8 %collective-permute-start.19 = (f32[512,128]{1,0:T(8,128)S(1)}, f32[512,128]{1,0:T(8,128)S(1)}, u32[]{:S(2)}, u32[]{:S(2)}) collective-permute-start(f32[512,128]{1,0:T(8,128)S(1)} %get-tuple-element.59), channel_id=1, source_target_pairs={{0,3},{1,2},{2,0},{3,1},{4,7},{5,6},{6,4},{7,5},{8,11},{9,10},{10,... | collective-permute-start | bytes 786440 | tf_op jit(solution)/shard_map/ppermute | solution.py:326
  63.9 23.6 %collective-permute-start.20 = (f32[512,128]{1,0:T(8,128)S(1)}, f32[512,128]{1,0:T(8,128)S(1)}, u32[]{:S(2)}, u32[]{:S(2)}) collective-permute-start(f32[512,128]{1,0:T(8,128)S(1)} %get-tuple-element.60), channel_id=1, source_target_pairs={{0,2},{1,3},{2,1},{3,0},{4,6},{5,7},{6,5},{7,4},{8,10},{9,11},{10,... | collective-permute-start | bytes 786440 | tf_op jit(solution)/shard_map/ppermute | solution.py:326
  66.5 21.0 %collective-permute-start.21 = (f32[512,128]{1,0:T(8,128)S(1)}, f32[512,128]{1,0:T(8,128)S(1)}, u32[]{:S(2)}, u32[]{:S(2)}) collective-permute-start(f32[512,128]{1,0:T(8,128)S(1)} %get-tuple-element.61), channel_id=1, source_target_pairs={{0,1},{1,0},{2,3},{3,2},{4,5},{5,4},{6,7},{7,6},{8,9},{9,8},{10,11... | collective-permute-start | bytes 786440 | tf_op jit(solution)/shard_map/ppermute | solution.py:326

commit v5 on v4

--- a/solution.py
+++ b/solution.py
@@ -69,21 +69,21 @@
         copy.wait()
 
 
+def reverse(value, size):
+    bits = size.bit_length() - 1
+    return sum(((value >> i) & 1) << (bits - 1 - i) for i in range(bits))
+
+
 def turn(col, step, size):
-    bits = size.bit_length() - 1
-
-    def reverse(value):
-        return sum(((value >> i) & 1) << (bits - 1 - i) for i in range(bits))
-
-    return reverse((reverse(col) + step) & (size - 1))
-
-
-def near_kernel(parts, groups, cols_size, *refs):
+    return reverse((reverse(col, size) + step) & (size - 1), size)
+
+
+def near_kernel(parts, steps, cols_size, *refs):
     place, pieces, (field, keep, send, high, low) = here(), refs[:-5], refs[-5:]
     col, core = place[0], place[1] & 1
     own, near = pieces[0].shape[1], len(pieces)
-    for i, piece in enumerate(pieces):
-        at = pl.multiple_of((turn(col, -i * groups, cols_size) & (near - 1)) * own, own)
+    for step, piece in zip(steps, pieces):
+        at = pl.multiple_of((turn(col, -step, cols_size) & (near - 1)) * own, own)
         for panel in range(2):
             rows = pl.ds(panel * near * own + at, own)
             high[rows, :], low[rows, :] = split(piece[panel])
@@ -96,35 +96,38 @@
         send[j] = jnp.where(core == 0, odd, even)
 
 
-def far_kernel(parts, steps, groups, *refs):
-    place, pieces = here(), refs[:-8]
-    field, keep, send, house, high, low, far_h, far_l = refs[-8:]
+def far_kernel(parts, steps, groups, rest, last, cols_size, *refs):
+    place, pieces, refs = here(), refs[: len(steps)], refs[len(steps) :]
+    if last:
+        field, keep, send, house, high, low, far_h, far_l = refs
+    else:
+        field, keep, send, far_h, far_l = refs
     col, core = place[0], place[1] & 1
-    cols_size = len(pieces)
     own, near = pieces[0].shape[1], cols_size // groups
-    mine = col // near
     for step, piece in zip(steps, pieces):
         block = turn(col, -step, cols_size)
-        group = block // near
         at = pl.multiple_of(block * own, own)
-        slot = group - jnp.where(group > mine, 1, 0)
-        inside = pl.multiple_of((slot * 2 * near + (block & (near - 1))) * own, own)
+        inside = pl.multiple_of((block & (near - 1)) * own, own)
         for panel in range(2):
             value = piece[panel]
             rows = pl.ds(at, own)
-            house[panel, rows, :] = value
             value_h, value_l = split(value)
-            high[panel, rows, :], low[panel, rows, :] = value_h, value_l
-            if step % groups:
-                rows = pl.ds(inside + panel * near * own, own)
+            if last:
+                house[panel, rows, :] = value
+                high[panel, rows, :], low[panel, rows, :] = value_h, value_l
+            if step % groups in rest:
+                slot = 2 * rest.index(step % groups) + panel
+                rows = pl.ds(inside + slot * near * own, own)
                 far_h[rows, :], far_l[rows, :] = value_h, value_l
-    result = product((far_h[...], far_l[...]), split(field[...]))
-    cross = product((high[1], low[1]), (high[0], low[0]), BY_TRANSPOSE)
+    if rest:
+        result = product((far_h[...], far_l[...]), split(field[...]))
     height = 2 * near * own
     count = height // parts
-    rows = cross.shape[0] // parts
-    side = keep.shape[2] // cross.shape[1]
-    packed = -(-rows // side)
+    if last:
+        cross = product((high[1], low[1]), (high[0], low[0]), BY_TRANSPOSE)
+        rows = cross.shape[0] // parts
+        side = keep.shape[2] // cross.shape[1]
+        packed = -(-rows // side)
     for j in range(parts // 2):
         for out, odd in ((keep, core), (send, 1 - core)):
 
@@ -132,11 +135,13 @@
                 even = value[first : first + number]
                 return jnp.where(odd == 0, even, value[first + stride : first + stride + number])
 
-            for slot in range(groups - 1):
+            for slot in range(len(rest)):
                 at = slot * count
                 block = chosen(result, slot * height + 2 * j * count, count, count)
                 out[j, at : at + count, :] = block
-            at = (groups - 1) * count
+            if not last:
+                continue
+            at = len(rest) * count
             if packed * side != rows:
                 out[j, at:, :] = jnp.zeros((packed, keep.shape[2]), jnp.float32)
             for i in range(rows // packed):
@@ -144,16 +149,38 @@
                 out[j, at:, i * cross.shape[1] : (i + 1) * cross.shape[1]] = block
 
 
-def add_split_kernel(shift, group, *refs):
+def add_split_kernel(shift, group, terms, *refs):
     place, sources, outs = here(), refs[:-group], refs[-group:]
     me = (place[1] >> shift) & (group - 1)
-    for a in range(outs[0].shape[0]):
-        for k, out in enumerate(outs):
-            at = a * group + (me ^ k)
-            total = sources[0][at]
-            for source in sources[1:]:
-                total = total + source[at]
-            out[a] = total
+    first = 0
+    for i in range(0, len(sources), terms):
+        rows = slice(first, first + sources[i].shape[1])
+        first += sources[i].shape[1]
+        for a in range(outs[0].shape[0]):
+            for k, out in enumerate(outs):
+                at = a * group + (me ^ k)
+                total = sources[i][at]
+                for source in sources[i + 1 : i + terms]:
+                    total = total + source[at]
+                out[a, rows] = total
+
+
+def merge_kernel(cols_size, groups, order, *refs):
+    place, early, sources = here(), refs[: groups - len(order)], refs[groups - len(order) : -2]
+    out, scratch = refs[-2:]
+    count = early[0].shape[1]
+    total = sources[0][0]
+    for source in sources[1:]:
+        total = total + source[0]
+    for distance, block in zip([d for d in range(groups) if d not in order], early):
+        scratch[distance] = block[0]
+    for i, distance in enumerate(order):
+        scratch[distance] = total[i * count : (i + 1) * count]
+    mine = reverse(place[0] // (cols_size // groups), groups)
+    for group in range(groups):
+        distance = (mine - reverse(group, groups)) & (groups - 1)
+        out[0, group * count : (group + 1) * count] = scratch[distance]
+    out[0, groups * count :] = total[len(order) * count :]
 
 
 def assemble_kernel(shift, group, *refs):
@@ -224,15 +251,21 @@
     stages = row_stages(rows_size)
     bf16 = jnp.bfloat16
 
-    def scatter(sources, stages):
+    def exchanged(sources, stages):
+        terms = 2
         for shift, group in stages[1:]:
-            shape = (sources[0].shape[0] // group,) + sources[0].shape[1:]
-            body = functools.partial(add_split_kernel, shift, group)
+            rows = sum(source.shape[1] for source in sources[::terms])
+            shape = (sources[0].shape[0] // group, rows, sources[0].shape[2])
+            body = functools.partial(add_split_kernel, shift, group, terms)
             cuts = kernel_call(body, [shape] * group, *sources)
             sources = [cuts[0]]
             for k in exchange_order(group):
                 sources.append(swap(cuts[k], "row", rows_size, k << shift))
-        return functools.reduce(jnp.add, sources)
+            terms = len(sources)
+        return sources
+
+    def scatter(sources, stages):
+        return functools.reduce(jnp.add, exchanged(sources, stages))
 
     def gather(current):
         for shift, group in reversed(stages[2:]):
@@ -273,40 +306,60 @@
                 pairs = [(i, turn(i, k, cols_size)) for i in range(cols_size)]
                 pieces[k] = lax.ppermute(cut, "col", pairs) if k else cut
 
-        def near_part():
+        def early(distance, stages):
+            part = [k for k in range(cols_size) if k % groups == distance]
             keep, send = kernel_call(
-                functools.partial(near_kernel, rows_size, groups, cols_size),
+                functools.partial(near_kernel, rows_size, part, cols_size),
                 [(half, count, eigvecs)] * 2,
-                *pieces[::groups],
+                *[pieces[k] for k in part],
                 vectors,
                 scratch=[((2 * near * own, local_rows), bf16)] * 2,
             )
-            bits = [(i, 2) for i in range(rows_size.bit_length() - 1)]
-            return scatter([keep, swap(send, "row", rows_size, 1)], bits)
-
+            return scatter([keep, swap(send, "row", rows_size, 1)], stages)
+
+        bits = [(i, 2) for i in range(rows_size.bit_length() - 1)]
         same = lax.cond(
-            always, near_part, lambda: jnp.zeros((1, count, eigvecs), jnp.float32)
+            always,
+            functools.partial(early, 0, bits),
+            lambda: jnp.zeros((1, count, eigvecs), jnp.float32),
         )
-        steps = steps + [0]
-        cuts, same = lax.optimization_barrier(([pieces[k] for k in steps], same))
-        keep, send, house = kernel_call(
-            functools.partial(far_kernel, rows_size, steps, groups),
-            [(half, (groups - 1) * count + packed, eigvecs)] * 2 + [(2, width, local_rows)],
-            *cuts,
-            vectors,
-            scratch=[((2, width, local_rows), bf16)] * 2
-            + [((2 * (cols_size - near) * own, local_rows), bf16)] * 2,
+
+        def far(steps, rest, last):
+            body = functools.partial(far_kernel, rows_size, steps, groups, rest, last, cols_size)
+            rows = len(rest) * count + (packed if last else 0)
+            keep, send, *house = kernel_call(
+                body,
+                [(half, rows, eigvecs)] * 2 + [(2, width, local_rows)] * last,
+                *[pieces[k] for k in steps],
+                vectors,
+                scratch=[((2, width, local_rows), bf16)] * (2 * last)
+                + [((2 * max(1, len(rest)) * near * own, local_rows), bf16)] * 2,
+            )
+            return [keep, swap(send, "row", rows_size, 1)], *house
+
+        order = [k for k in range(groups - 1, groups // 2, -1)]
+        sources = []
+        others = [k for k in range(groups // 2, 0, -1)]
+        for rest in (order, others):
+            wanted = [k for k in range(1, cols_size) if k % groups in rest]
+            cuts, (same, sources) = lax.optimization_barrier(
+                ([pieces[k] for k in wanted], (same, sources))
+            )
+            for k, cut in zip(wanted, cuts):
+                pieces[k] = cut
+            if rest == order and order:
+                (sources,) = far(wanted, rest, False)
+        pair, house = far(steps + [0], others, True)
+        order = order + others
+        sources = exchanged(sources + pair, stages)
+        sums = [same]
+        (part,) = kernel_call(
+            functools.partial(merge_kernel, cols_size, groups, order),
+            [(1, groups * count + packed, eigvecs)],
+            *sums,
+            *sources,
+            scratch=[((groups, count, eigvecs), jnp.float32)],
         )
-        rest = scatter([keep, swap(send, "row", rows_size, 1)], stages)
-        blocks = [rest[:, i * count : (i + 1) * count] for i in range(groups - 1)]
-        mine = col // near
-        part = []
-        for group in range(groups):
-            block = blocks[max(group - 1, 0)]
-            if 0 < group < groups - 1:
-                block = jnp.where(mine < group, block, blocks[group])
-            part.append(jnp.where(mine == group, same, block))
-        part = jnp.concatenate(part + [rest[:, (groups - 1) * count :]], 1)
         part, other = all_reduce_cols(part, rows_size, cols_size)
 
         blocks = kernel_call(

time: 88.6 us -> 88.2 us (level)
    pallas_call x6 -> x8, Pallas kernels: 3.73 us -> 3.96 us  [kernel_call(): pl.pallas_call(body, out_shape=[jax.ShapeDtypeStruct(shape, jnp.float32)...]
    ppermute x14 -> x15, waiting for transfers between devices: 20.1 us -> 19.9 us  [swap(): return lax.ppermute(block, axis, [(i, i ^ mask) for i in range(size)])]
    ppermute x14 -> x15, starting transfers between devices: 10.6 us -> 10.7 us  [swap(): return lax.ppermute(block, axis, [(i, i ^ mask) for i in range(size)])]
  transfers between devices with their start and end apart: 22 -> 23, of which waited for: 18 -> 18; matrix products, arithmetic and copies ran while one was open for 1% -> 1% of each run, Pallas kernels for 1% -> 1%
where the time goes in v5:
time: 88.2 us; the launch traced here: 88 us
  waiting for transfers between devices  57.1 us (65%)
  starting transfers between devices  23.6 us (27%)
  Pallas kernels  4.96 us (6%)
  local copies, waits for them, and re-layouts  2.23 us (3%)
    ppermute x15, waiting for transfers between devices, swap(): return lax.ppermute(block, axis, [(i, i ^ mask) for i in range(size)])  19.9 us
    ppermute x3, waiting for transfers between devices, per_device(): blocks[k] = lax.ppermute(blocks[k], 'col', pairs)  19.6 us
    ppermute x15, starting transfers between devices, swap(): return lax.ppermute(block, axis, [(i, i ^ mask) for i in range(size)])  10.7 us
    ppermute x2, waiting for transfers between devices, all_reduce_cols(): other = lax.ppermute(part, ('row', 'col'), pairs)  8.88 us
    ppermute x3, waiting for transfers between devices, per_device(): pieces[k] = lax.ppermute(cut, 'col', pairs) if k else cut  8.74 us
    ppermute x3, starting transfers between devices, per_device(): blocks[k] = lax.ppermute(blocks[k], 'col', pairs)  4.9 us
    ppermute x3, starting transfers between devices, per_device(): pieces[k] = lax.ppermute(cut, 'col', pairs) if k else cut  4.23 us
    pallas_call x8, Pallas kernels, kernel_call(): pl.pallas_call(body, out_shape=[jax.ShapeDtypeStruct(shape, jnp.float32)...  3.96 us
  transfers between devices with their start and end apart: 23, of which 18 were waited for; matrix products, arithmetic and copies ran while one was open for 1% of the time, Pallas kernels for 1%

profile of v5, /device:TPU:8, one launch (start us, length us, event | category | flops | bytes accessed | tf_op | source)
XLA Modules:
  0.0 88.0 jit_solution(4752871958418637881)
XLA Ops:
  0.0 1.1 %dynamic-slice_bitcast_fusion = f32[2,64,512]{2,1,0:T(8,128)S(1)} fusion(f32[2,2048,64]{1,2,0:T(8,128)} %param.6, s32[]{:T(128)S(6)} %select_n.12), kind=kLoop, calls=%fused_computation | loop fusion | bytes 524292 | tf_op jit(solution)/shard_map/dynamic_slice | solution.py:303
  1.1 1.6 %collective-permute-start.5 = (f32[2,64,512]{2,1,0:T(8,128)S(1)}, f32[2,64,512]{2,1,0:T(8,128)S(1)}, u32[]{:S(2)}, u32[]{:S(2)}) collective-permute-start(f32[2,64,512]{2,1,0:T(8,128)S(1)} %dynamic-slice_bitcast_fusion), channel_id=1, source_target_pairs={{0,3},{1,2},{2,0},{3,1},{4,7},{5,6},{6,4},{7,5},{8,11},{9,10},{10,... | collective-permute-start | bytes 786440 | tf_op jit(solution)/shard_map/ppermute | solution.py:307
  2.7 1.2 %constant_dynamic-slice_fusion = (f32[2,64,512]{2,1,0:T(8,128)S(1)}, f32[2,64,512]{2,1,0:T(8,128)S(1)}, f32[2,64,512]{2,1,0:T(8,128)S(1)}) fusion(f32[2,64,2048]{2,1,0:T(8,128)} %bitcast.4, s32[]{:T(128)S(6)} %select_n.15, s32[]{:T(128)S(6)} %select_n.14, s32[]{:T(128)S(6)} %select_n.13), kind=kLoop, calls=%fused_computation.1 | loop fusion | bytes 1572876 | tf_op jit(solution)/shard_map/dynamic_slice | solution.py:303
  3.9 1.4 %collective-permute-start.3 = (f32[2,64,512]{2,1,0:T(8,128)S(1)}, f32[2,64,512]{2,1,0:T(8,128)S(1)}, u32[]{:S(2)}, u32[]{:S(2)}) collective-permute-start(f32[2,64,512]{2,1,0:T(8,128)S(1)} %get-tuple-element.46), channel_id=1, source_target_pairs={{0,2},{1,3},{2,1},{3,0},{4,6},{5,7},{6,5},{7,4},{8,10},{9,11},{10,... | collective-permute-start | bytes 786440 | tf_op jit(solution)/shard_map/ppermute | solution.py:307
  5.3 1.2 %collective-permute-start.4 = (f32[2,64,512]{2,1,0:T(8,128)S(1)}, f32[2,64,512]{2,1,0:T(8,128)S(1)}, u32[]{:S(2)}, u32[]{:S(2)}) collective-permute-start(f32[2,64,512]{2,1,0:T(8,128)S(1)} %get-tuple-element.47), channel_id=1, source_target_pairs={{0,1},{1,0},{2,3},{3,2},{4,5},{5,4},{6,7},{7,6},{8,9},{9,8},{10,11... | collective-permute-start | bytes 786440 | tf_op jit(solution)/shard_map/ppermute | solution.py:307
  6.5 10.2 %conditional.1 = (f32[1,16,512]{2,1,0:T(8,128)S(1)}) conditional(s32[]{:T(128)} %convert_element_type.3, () %tuple.17, (f32[2,64,512]{2,1,0:T(8,128)S(1)}, f32[512,512]{1,0:T(8,128)S(1)}) %tuple.25), branch_computations={%region_0.0_spmd, %region_1.0_spmd} | conditional | flops 8192 | bytes 1015936 | solution.py:321
  6.5 0.4 branch_1_fun.3
  6.9 0.1 collective-permute-start
  7.0 1.3 %collective-permute-done.refs_1_ = f32[4,16,512]{2,1,0:T(8,128)S(1)} collective-permute-done((f32[4,16,512]{2,1,0:T(8,128)S(1)}, f32[4,16,512]{2,1,0:T(8,128)S(1)}, u32[]{:S(2)}, u32[]{:S(2)}) %collective-permute-start) | collective-permute-done | bytes 131104 | tf_op jit(solution)/shard_map/cond/branch_1_fun/ppermute | solution.py:43
  8.3 1.6 %collective-permute-start.1 = (f32[2,16,512]{2,1,0:T(8,128)S(1)}, f32[2,16,512]{2,1,0:T(8,128)S(1)}, u32[]{:S(2)}, u32[]{:S(2)}) collective-permute-start(f32[2,16,512]{2,1,0:T(8,128)S(1)} %get-tuple-element.17), channel_id=1, source_target_pairs={{0,8},{4,12},{8,0},{12,4},{16,24},{20,28},{24,16},{28,20},{1,9},{5... | collective-permute-start | bytes 196616 | tf_op jit(solution)/shard_map/cond/branch_1_fun/ppermute | solution.py:43
  9.9 2.8 %collective-permute-done.1.refs_1_ = f32[2,16,512]{2,1,0:T(8,128)S(1)} collective-permute-done((f32[2,16,512]{2,1,0:T(8,128)S(1)}, f32[2,16,512]{2,1,0:T(8,128)S(1)}, u32[]{:S(2)}, u32[]{:S(2)}) %collective-permute-start.1) | collective-permute-done | bytes 65568 | tf_op jit(solution)/shard_map/cond/branch_1_fun/ppermute | solution.py:43
  12.7 1.6 %collective-permute-start.2 = (f32[1,16,512]{2,1,0:T(8,128)S(1)}, f32[1,16,512]{2,1,0:T(8,128)S(1)}, u32[]{:S(2)}, u32[]{:S(2)}) collective-permute-start(f32[1,16,512]{2,1,0:T(8,128)S(1)} %get-tuple-element.19), channel_id=1, source_target_pairs={{0,16},{4,20},{8,24},{12,28},{16,0},{20,4},{24,8},{28,12},{1,17},{... | collective-permute-start | bytes 98312 | tf_op jit(solution)/shard_map/cond/branch_1_fun/ppermute | solution.py:43
  14.3 2.4 %collective-permute-done.2 = f32[1,16,512]{2,1,0:T(8,128)S(1)} collective-permute-done((f32[1,16,512]{2,1,0:T(8,128)S(1)}, f32[1,16,512]{2,1,0:T(8,128)S(1)}, u32[]{:S(2)}, u32[]{:S(2)}) %collective-permute-start.2) | collective-permute-done | bytes 32800 | tf_op jit(solution)/shard_map/cond/branch_1_fun/ppermute | solution.py:43
  16.7 4.0 %collective-permute-done.5.refs_0_ = f32[2,64,512]{2,1,0:T(8,128)S(1)} collective-permute-done((f32[2,64,512]{2,1,0:T(8,128)S(1)}, f32[2,64,512]{2,1,0:T(8,128)S(1)}, u32[]{:S(2)}, u32[]{:S(2)}) %collective-permute-start.5) | collective-permute-done | bytes 262176 | tf_op jit(solution)/shard_map/ppermute | solution.py:307
  20.6 0.4 shard_map.37
  21.1 0.1 collective-permute-start.6
  21.1 4.8 %collective-permute-done.3.refs_2_ = f32[2,64,512]{2,1,0:T(8,128)S(1)} collective-permute-done((f32[2,64,512]{2,1,0:T(8,128)S(1)}, f32[2,64,512]{2,1,0:T(8,128)S(1)}, u32[]{:S(2)}, u32[]{:S(2)}) %collective-permute-start.3) | collective-permute-done | bytes 262176 | tf_op jit(solution)/shard_map/ppermute | solution.py:307
  25.9 0.9 %shard_map.38 = (f32[4,48,512]{2,1,0:T(8,128)S(1)}, f32[4,48,512]{2,1,0:T(8,128)S(1)}, f32[2,256,512]{2,1,0:T(8,128)S(1)}) custom-call(f32[2,64,512]{2,1,0:T(8,128)S(1)} %collective-permute-done.5.refs_0_, f32[2,64,512]{2,1,0:T(8,128)S(1)} %collective-permute-done.4.refs_1_, f32[2,64,512]{2,1,0:T(8,128)S(1)} %collective-permute-done.3.refs_2_, ...), custom_call_target="tpu_custom_call" | custom-call | tf_op jit(solution)/shard_map/pallas_call | solution.py:32
  26.8 0.1 collective-permute-start.7
  26.9 1.7 %collective-permute-done.7.refs_3_ = f32[4,48,512]{2,1,0:T(8,128)S(1)} collective-permute-done((f32[4,48,512]{2,1,0:T(8,128)S(1)}, f32[4,48,512]{2,1,0:T(8,128)S(1)}, u32[]{:S(2)}, u32[]{:S(2)}) %collective-permute-start.7) | collective-permute-done | bytes 393248 | tf_op jit(solution)/shard_map/ppermute | solution.py:43
  28.6 0.1 shard_map.39
  28.6 1.6 %collective-permute-start.8 = (f32[1,64,512]{2,1,0:T(8,128)S(1)}, f32[1,64,512]{2,1,0:T(8,128)S(1)}, u32[]{:S(2)}, u32[]{:S(2)}) collective-permute-start(f32[1,64,512]{2,1,0:T(8,128)S(1)} %get-tuple-element.62), channel_id=1, source_target_pairs={{0,16},{4,20},{8,24},{12,28},{16,0},{20,4},{24,8},{28,12},{1,17},{... | collective-permute-start | bytes 393224 | tf_op jit(solution)/shard_map/ppermute | solution.py:43
  30.3 1.5 %collective-permute-start.9 = (f32[1,64,512]{2,1,0:T(8,128)S(1)}, f32[1,64,512]{2,1,0:T(8,128)S(1)}, u32[]{:S(2)}, u32[]{:S(2)}) collective-permute-start(f32[1,64,512]{2,1,0:T(8,128)S(1)} %get-tuple-element.63), channel_id=1, source_target_pairs={{0,8},{4,12},{8,0},{12,4},{16,24},{20,28},{24,16},{28,20},{1,9},{5... | collective-permute-start | bytes 393224 | tf_op jit(solution)/shard_map/ppermute | solution.py:43
  31.8 0.4 collective-permute-start.10
  32.2 2.0 %collective-permute-done.8.refs_2_ = f32[1,64,512]{2,1,0:T(8,128)S(1)} collective-permute-done((f32[1,64,512]{2,1,0:T(8,128)S(1)}, f32[1,64,512]{2,1,0:T(8,128)S(1)}, u32[]{:S(2)}, u32[]{:S(2)}) %collective-permute-start.8) | collective-permute-done | bytes 131104 | tf_op jit(solution)/shard_map/ppermute | solution.py:43
  34.2 2.4 %collective-permute-done.9.refs_3_ = f32[1,64,512]{2,1,0:T(8,128)S(1)} collective-permute-done((f32[1,64,512]{2,1,0:T(8,128)S(1)}, f32[1,64,512]{2,1,0:T(8,128)S(1)}, u32[]{:S(2)}, u32[]{:S(2)}) %collective-permute-start.9) | collective-permute-done | bytes 131104 | tf_op jit(solution)/shard_map/ppermute | solution.py:43
  36.7 1.6 %collective-permute-done.10.refs_4_ = f32[1,64,512]{2,1,0:T(8,128)S(1)} collective-permute-done((f32[1,64,512]{2,1,0:T(8,128)S(1)}, f32[1,64,512]{2,1,0:T(8,128)S(1)}, u32[]{:S(2)}, u32[]{:S(2)}) %collective-permute-start.10) | collective-permute-done | bytes 131104 | tf_op jit(solution)/shard_map/ppermute | solution.py:43
  38.3 0.0 copy-start
  38.3 0.1 collective-permute-start.11
  38.4 5.3 %collective-permute-done.11 = f32[1,80,512]{2,1,0:T(8,128)S(1)} collective-permute-done((f32[1,80,512]{2,1,0:T(8,128)S(1)}, f32[1,80,512]{2,1,0:T(8,128)S(1)}, u32[]{:S(2)}, u32[]{:S(2)}) %collective-permute-start.11) | collective-permute-done | bytes 163872 | tf_op jit(solution)/shard_map/ppermute | solution.py:244
  43.7 3.6 %collective-permute-start.12 = (f32[1,80,512]{2,1,0:T(8,128)S(1)}, f32[1,80,512]{2,1,0:T(8,128)S(1)}, u32[]{:S(2)}, u32[]{:S(2)}) collective-permute-start(f32[1,80,512]{2,1,0:T(8,128)S(1)} %add.60), channel_id=1, source_target_pairs={{0,2},{1,3},{2,0},{3,1},{4,5},{5,4},{6,7},{7,6},{8,10},{9,11},{10,... | collective-permute-start | bytes 491528 | tf_op jit(solution)/shard_map/ppermute | solution.py:244
  47.4 3.6 %collective-permute-done.12 = f32[1,80,512]{2,1,0:T(8,128)S(1)} collective-permute-done((f32[1,80,512]{2,1,0:T(8,128)S(1)}, f32[1,80,512]{2,1,0:T(8,128)S(1)}, u32[]{:S(2)}, u32[]{:S(2)}) %collective-permute-start.12) | collective-permute-done | bytes 163872 | tf_op jit(solution)/shard_map/ppermute | solution.py:244
  51.0 2.2 %collective-permute-start.15 = (f32[1,80,512]{2,1,0:T(8,128)S(1)}, f32[1,80,512]{2,1,0:T(8,128)S(1)}, u32[]{:S(2)}, u32[]{:S(2)}) collective-permute-start(f32[1,80,512]{2,1,0:T(8,128)S(1)} %add.61.refs_0_), channel_id=1, source_target_pairs={{0,24},{4,28},{8,16},{12,20},{16,8},{20,12},{24,0},{28,4},{1,25},{... | collective-permute-start | bytes 491528 | tf_op jit(solution)/shard_map/ppermute | solution.py:43
  53.1 0.5 collective-permute-start.14
  53.7 0.8 collective-permute-start.13
  54.5 2.7 %collective-permute-done.15.refs_3_ = f32[1,80,512]{2,1,0:T(8,128)S(1)} collective-permute-done((f32[1,80,512]{2,1,0:T(8,128)S(1)}, f32[1,80,512]{2,1,0:T(8,128)S(1)}, u32[]{:S(2)}, u32[]{:S(2)}) %collective-permute-start.15) | collective-permute-done | bytes 163872 | tf_op jit(solution)/shard_map/ppermute | solution.py:43
  57.2 1.5 %collective-permute-done.14.refs_2_ = f32[1,80,512]{2,1,0:T(8,128)S(1)} collective-permute-done((f32[1,80,512]{2,1,0:T(8,128)S(1)}, f32[1,80,512]{2,1,0:T(8,128)S(1)}, u32[]{:S(2)}, u32[]{:S(2)}) %collective-permute-start.14) | collective-permute-done | bytes 163872 | tf_op jit(solution)/shard_map/ppermute | solution.py:43
  58.7 0.3 collective-permute-done.13.refs_1_
  59.0 0.2 collective-permute-start.17
  59.3 0.9 collective-permute-done.18.refs_6_
  60.1 0.3 collective-permute-done.17.refs_5_
  60.4 2.1 %shard_map.41 = (f32[512,128]{1,0:T(8,128)S(1)}, f32[512,128]{1,0:T(8,128)S(1)}, f32[512,128]{1,0:T(8,128)S(1)}, f32[512,128]{1,0:T(8,128)S(1)}) custom-call(f32[1,80,512]{2,1,0:T(8,128)S(1)} %add.61.refs_0_, f32[1,80,512]{2,1,0:T(8,128)S(1)} %collective-permute-done.13.refs_1_, f32[1,80,512]{2,1,0:T(8,128)S(1)} %collective-permute-done.14.refs_2_, ...), custom_call_target="tpu_custom_call" | custom-call | tf_op jit(solution)/shard_map/pallas_call | solution.py:32
  62.5 0.9 collective-permute-start.20
  63.4 2.6 %collective-permute-start.21 = (f32[512,128]{1,0:T(8,128)S(1)}, f32[512,128]{1,0:T(8,128)S(1)}, u32[]{:S(2)}, u32[]{:S(2)}) collective-permute-start(f32[512,128]{1,0:T(8,128)S(1)} %get-tuple-element.68), channel_id=1, source_target_pairs={{0,2},{1,3},{2,1},{3,0},{4,6},{5,7},{6,5},{7,4},{8,10},{9,11},{10,... | collective-permute-start | bytes 786440 | tf_op jit(solution)/shard_map/ppermute | solution.py:379
  66.0 1.4 %collective-permute-start.22 = (f32[512,128]{1,0:T(8,128)S(1)}, f32[512,128]{1,0:T(8,128)S(1)}, u32[]{:S(2)}, u32[]{:S(2)}) collective-permute-start(f32[512,128]{1,0:T(8,128)S(1)} %get-tuple-element.69), channel_id=1, source_target_pairs={{0,1},{1,0},{2,3},{3,2},{4,5},{5,4},{6,7},{7,6},{8,9},{9,8},{10,11... | collective-permute-start | bytes 786440 | tf_op jit(solution)/shard_map/ppermute | solution.py:379
  67.4 13.8 %collective-permute-done.20.refs_1_ = f32[512,128]{1,0:T(8,128)S(1)} collective-permute-done((f32[512,128]{1,0:T(8,128)S(1)}, f32[512,128]{1,0:T(8,128)S(1)}, u32[]{:S(2)}, u32[]{:S(2)}) %collective-permute-start.20) | collective-permute-done | bytes 262176 | tf_op jit(solution)/shard_map/ppermute | solution.py:379
  81.3 5.7 %collective-permute-done.21.refs_2_ = f32[512,128]{1,0:T(8,128)S(1)} collective-permute-done((f32[512,128]{1,0:T(8,128)S(1)}, f32[512,128]{1,0:T(8,128)S(1)}, u32[]{:S(2)}, u32[]{:S(2)}) %collective-permute-start.21) | collective-permute-done | bytes 262176 | tf_op jit(solution)/shard_map/ppermute | solution.py:379
  87.0 1.0 %shard_map.42 = f32[4,512,128]{2,1,0:T(8,128)} custom-call(f32[512,128]{1,0:T(8,128)S(1)} %get-tuple-element.66.refs_0_, f32[512,128]{1,0:T(8,128)S(1)} %collective-permute-done.20.refs_1_, f32[512,128]{1,0:T(8,128)S(1)} %collective-permute-done.21.refs_2_, f32[512,128]{1,0:T(8,128)S(1)} %collective-permute-done.22.refs_3_), custom_call_target="tpu_custom_call" | custom-call | tf_op jit(solution)/shard_map/pallas_call | solution.py:381
  (17 shorter events, 0.1 us)
Async XLA Ops:
  0.0 6.5 %copy-start.1 = (f32[512,512]{1,0:T(8,128)S(1)}, f32[512,512]{1,0:T(8,128)}, u32[]{:S(2)}) copy-start(f32[512,512]{1,0:T(8,128)} %refs_10_.1) | copy-start | bytes 3145732
  1.1 19.6 %collective-permute-start.5 = (f32[2,64,512]{2,1,0:T(8,128)S(1)}, f32[2,64,512]{2,1,0:T(8,128)S(1)}, u32[]{:S(2)}, u32[]{:S(2)}) collective-permute-start(f32[2,64,512]{2,1,0:T(8,128)S(1)} %dynamic-slice_bitcast_fusion), channel_id=1, source_target_pairs={{0,3},{1,2},{2,0},{3,1},{4,7},{5,6},{6,4},{7,5},{8,11},{9,10},{10,... | collective-permute-start | bytes 786440 | tf_op jit(solution)/shard_map/ppermute | solution.py:307
  3.9 22.0 %collective-permute-start.3 = (f32[2,64,512]{2,1,0:T(8,128)S(1)}, f32[2,64,512]{2,1,0:T(8,128)S(1)}, u32[]{:S(2)}, u32[]{:S(2)}) collective-permute-start(f32[2,64,512]{2,1,0:T(8,128)S(1)} %get-tuple-element.46), channel_id=1, source_target_pairs={{0,2},{1,3},{2,1},{3,0},{4,6},{5,7},{6,5},{7,4},{8,10},{9,11},{10,... | collective-permute-start | bytes 786440 | tf_op jit(solution)/shard_map/ppermute | solution.py:307
  5.3 20.6 %collective-permute-start.4 = (f32[2,64,512]{2,1,0:T(8,128)S(1)}, f32[2,64,512]{2,1,0:T(8,128)S(1)}, u32[]{:S(2)}, u32[]{:S(2)}) collective-permute-start(f32[2,64,512]{2,1,0:T(8,128)S(1)} %get-tuple-element.47), channel_id=1, source_target_pairs={{0,1},{1,0},{2,3},{3,2},{4,5},{5,4},{6,7},{7,6},{8,9},{9,8},{10,11... | collective-permute-start | bytes 786440 | tf_op jit(solution)/shard_map/ppermute | solution.py:307
  6.9 1.4 %collective-permute-start = (f32[4,16,512]{2,1,0:T(8,128)S(1)}, f32[4,16,512]{2,1,0:T(8,128)S(1)}, u32[]{:S(2)}, u32[]{:S(2)}) collective-permute-start(f32[4,16,512]{2,1,0:T(8,128)S(1)} %get-tuple-element.15), channel_id=1, source_target_pairs={{0,4},{4,0},{8,12},{12,8},{16,20},{20,16},{24,28},{28,24},{1,5},{5... | collective-permute-start | bytes 393224 | tf_op jit(solution)/shard_map/cond/branch_1_fun/ppermute | solution.py:43
  8.3 4.3 %collective-permute-start.1 = (f32[2,16,512]{2,1,0:T(8,128)S(1)}, f32[2,16,512]{2,1,0:T(8,128)S(1)}, u32[]{:S(2)}, u32[]{:S(2)}) collective-permute-start(f32[2,16,512]{2,1,0:T(8,128)S(1)} %get-tuple-element.17), channel_id=1, source_target_pairs={{0,8},{4,12},{8,0},{12,4},{16,24},{20,28},{24,16},{28,20},{1,9},{5... | collective-permute-start | bytes 196616 | tf_op jit(solution)/shard_map/cond/branch_1_fun/ppermute | solution.py:43
  12.7 4.0 %collective-permute-start.2 = (f32[1,16,512]{2,1,0:T(8,128)S(1)}, f32[1,16,512]{2,1,0:T(8,128)S(1)}, u32[]{:S(2)}, u32[]{:S(2)}) collective-permute-start(f32[1,16,512]{2,1,0:T(8,128)S(1)} %get-tuple-element.19), channel_id=1, source_target_pairs={{0,16},{4,20},{8,24},{12,28},{16,0},{20,4},{24,8},{28,12},{1,17},{... | collective-permute-start | bytes 98312 | tf_op jit(solution)/shard_map/cond/branch_1_fun/ppermute | solution.py:43
  21.1 4.8 %collective-permute-start.6 = (f32[4,16,512]{2,1,0:T(8,128)S(1)}, f32[4,16,512]{2,1,0:T(8,128)S(1)}, u32[]{:S(2)}, u32[]{:S(2)}) collective-permute-start(f32[4,16,512]{2,1,0:T(8,128)S(1)} %get-tuple-element.53), channel_id=1, source_target_pairs={{0,4},{4,0},{8,12},{12,8},{16,20},{20,16},{24,28},{28,24},{1,5},{5... | collective-permute-start | bytes 393224 | tf_op jit(solution)/shard_map/ppermute | solution.py:43
  26.8 1.8 %collective-permute-start.7 = (f32[4,48,512]{2,1,0:T(8,128)S(1)}, f32[4,48,512]{2,1,0:T(8,128)S(1)}, u32[]{:S(2)}, u32[]{:S(2)}) collective-permute-start(f32[4,48,512]{2,1,0:T(8,128)S(1)} %get-tuple-element.60), channel_id=1, source_target_pairs={{0,4},{4,0},{8,12},{12,8},{16,20},{20,16},{24,28},{28,24},{1,5},{5... | collective-permute-start | bytes 1179656 | tf_op jit(solution)/shard_map/ppermute | solution.py:43
  28.6 5.6 %collective-permute-start.8 = (f32[1,64,512]{2,1,0:T(8,128)S(1)}, f32[1,64,512]{2,1,0:T(8,128)S(1)}, u32[]{:S(2)}, u32[]{:S(2)}) collective-permute-start(f32[1,64,512]{2,1,0:T(8,128)S(1)} %get-tuple-element.62), channel_id=1, source_target_pairs={{0,16},{4,20},{8,24},{12,28},{16,0},{20,4},{24,8},{28,12},{1,17},{... | collective-permute-start | bytes 393224 | tf_op jit(solution)/shard_map/ppermute | solution.py:43
  30.3 6.4 %collective-permute-start.9 = (f32[1,64,512]{2,1,0:T(8,128)S(1)}, f32[1,64,512]{2,1,0:T(8,128)S(1)}, u32[]{:S(2)}, u32[]{:S(2)}) collective-permute-start(f32[1,64,512]{2,1,0:T(8,128)S(1)} %get-tuple-element.63), channel_id=1, source_target_pairs={{0,8},{4,12},{8,0},{12,4},{16,24},{20,28},{24,16},{28,20},{1,9},{5... | collective-permute-start | bytes 393224 | tf_op jit(solution)/shard_map/ppermute | solution.py:43
  31.8 6.5 %collective-permute-start.10 = (f32[1,64,512]{2,1,0:T(8,128)S(1)}, f32[1,64,512]{2,1,0:T(8,128)S(1)}, u32[]{:S(2)}, u32[]{:S(2)}) collective-permute-start(f32[1,64,512]{2,1,0:T(8,128)S(1)} %get-tuple-element.64), channel_id=1, source_target_pairs={{0,24},{4,28},{8,16},{12,20},{16,8},{20,12},{24,0},{28,4},{1,25},{... | collective-permute-start | bytes 393224 | tf_op jit(solution)/shard_map/ppermute | solution.py:43
  38.3 22.1 %copy-start = (f32[2,256,256]{2,1,0:T(8,128)S(1)}, f32[2,256,256]{2,1,0:T(8,128)}, u32[]{:S(2)}) copy-start(f32[2,256,256]{2,1,0:T(8,128)} %refs_8_.1) | copy-start | bytes 1572868
  38.3 5.4 %collective-permute-start.11 = (f32[1,80,512]{2,1,0:T(8,128)S(1)}, f32[1,80,512]{2,1,0:T(8,128)S(1)}, u32[]{:S(2)}, u32[]{:S(2)}) collective-permute-start(f32[1,80,512]{2,1,0:T(8,128)S(1)} %shard_map.40), channel_id=1, source_target_pairs={{0,1},{1,0},{2,3},{3,2},{4,6},{5,7},{6,4},{7,5},{8,9},{9,8},{10,11... | collective-permute-start | bytes 491528 | tf_op jit(solution)/shard_map/ppermute | solution.py:244
  43.7 7.2 %collective-permute-start.12 = (f32[1,80,512]{2,1,0:T(8,128)S(1)}, f32[1,80,512]{2,1,0:T(8,128)S(1)}, u32[]{:S(2)}, u32[]{:S(2)}) collective-permute-start(f32[1,80,512]{2,1,0:T(8,128)S(1)} %add.60), channel_id=1, source_target_pairs={{0,2},{1,3},{2,0},{3,1},{4,5},{5,4},{6,7},{7,6},{8,10},{9,11},{10,... | collective-permute-start | bytes 491528 | tf_op jit(solution)/shard_map/ppermute | solution.py:244
  51.0 6.3 %collective-permute-start.15 = (f32[1,80,512]{2,1,0:T(8,128)S(1)}, f32[1,80,512]{2,1,0:T(8,128)S(1)}, u32[]{:S(2)}, u32[]{:S(2)}) collective-permute-start(f32[1,80,512]{2,1,0:T(8,128)S(1)} %add.61.refs_0_), channel_id=1, source_target_pairs={{0,24},{4,28},{8,16},{12,20},{16,8},{20,12},{24,0},{28,4},{1,25},{... | collective-permute-start | bytes 491528 | tf_op jit(solution)/shard_map/ppermute | solution.py:43
  53.1 5.6 %collective-permute-start.14 = (f32[1,80,512]{2,1,0:T(8,128)S(1)}, f32[1,80,512]{2,1,0:T(8,128)S(1)}, u32[]{:S(2)}, u32[]{:S(2)}) collective-permute-start(f32[1,80,512]{2,1,0:T(8,128)S(1)} %add.61.refs_0_), channel_id=1, source_target_pairs={{0,8},{4,12},{8,0},{12,4},{16,24},{20,28},{24,16},{28,20},{1,9},{5... | collective-permute-start | bytes 491528 | tf_op jit(solution)/shard_map/ppermute | solution.py:43
  53.7 5.3 %collective-permute-start.13 = (f32[1,80,512]{2,1,0:T(8,128)S(1)}, f32[1,80,512]{2,1,0:T(8,128)S(1)}, u32[]{:S(2)}, u32[]{:S(2)}) collective-permute-start(f32[1,80,512]{2,1,0:T(8,128)S(1)} %add.61.refs_0_), channel_id=1, source_target_pairs={{0,16},{4,20},{8,24},{12,28},{16,0},{20,4},{24,8},{28,12},{1,17},{... | collective-permute-start | bytes 491528 | tf_op jit(solution)/shard_map/ppermute | solution.py:43
  54.5 4.7 %collective-permute-start.16 = (f32[1,80,512]{2,1,0:T(8,128)S(1)}, f32[1,80,512]{2,1,0:T(8,128)S(1)}, u32[]{:S(2)}, u32[]{:S(2)}) collective-permute-start(f32[1,80,512]{2,1,0:T(8,128)S(1)} %add.61.refs_0_), channel_id=1, source_target_pairs={{0,4},{4,0},{8,12},{12,8},{16,20},{20,16},{24,28},{28,24},{1,5},{5... | collective-permute-start | bytes 491528 | tf_op jit(solution)/shard_map/ppermute | solution.py:43
  57.2 2.0 %collective-permute-start.19 = (f32[1,80,512]{2,1,0:T(8,128)S(1)}, f32[1,80,512]{2,1,0:T(8,128)S(1)}, u32[]{:S(2)}, u32[]{:S(2)}) collective-permute-start(f32[1,80,512]{2,1,0:T(8,128)S(1)} %collective-permute-done.15.refs_3_), channel_id=1, source_target_pairs={{0,4},{4,0},{8,12},{12,8},{16,20},{20,16},{24,28},{28,24},{1,5},{5... | collective-permute-start | bytes 491528 | tf_op jit(solution)/shard_map/ppermute | solution.py:43
  58.7 1.4 %collective-permute-start.18 = (f32[1,80,512]{2,1,0:T(8,128)S(1)}, f32[1,80,512]{2,1,0:T(8,128)S(1)}, u32[]{:S(2)}, u32[]{:S(2)}) collective-permute-start(f32[1,80,512]{2,1,0:T(8,128)S(1)} %collective-permute-done.14.refs_2_), channel_id=1, source_target_pairs={{0,4},{4,0},{8,12},{12,8},{16,20},{20,16},{24,28},{28,24},{1,5},{5... | collective-permute-start | bytes 491528 | tf_op jit(solution)/shard_map/ppermute | solution.py:43
  59.0 1.4 %collective-permute-start.17 = (f32[1,80,512]{2,1,0:T(8,128)S(1)}, f32[1,80,512]{2,1,0:T(8,128)S(1)}, u32[]{:S(2)}, u32[]{:S(2)}) collective-permute-start(f32[1,80,512]{2,1,0:T(8,128)S(1)} %collective-permute-done.13.refs_1_), channel_id=1, source_target_pairs={{0,4},{4,0},{8,12},{12,8},{16,20},{20,16},{24,28},{28,24},{1,5},{5... | collective-permute-start | bytes 491528 | tf_op jit(solution)/shard_map/ppermute | solution.py:43
  62.5 18.7 %collective-permute-start.20 = (f32[512,128]{1,0:T(8,128)S(1)}, f32[512,128]{1,0:T(8,128)S(1)}, u32[]{:S(2)}, u32[]{:S(2)}) collective-permute-start(f32[512,128]{1,0:T(8,128)S(1)} %get-tuple-element.67), channel_id=1, source_target_pairs={{0,3},{1,2},{2,0},{3,1},{4,7},{5,6},{6,4},{7,5},{8,11},{9,10},{10,... | collective-permute-start | bytes 786440 | tf_op jit(solution)/shard_map/ppermute | solution.py:379
  63.4 23.6 %collective-permute-start.21 = (f32[512,128]{1,0:T(8,128)S(1)}, f32[512,128]{1,0:T(8,128)S(1)}, u32[]{:S(2)}, u32[]{:S(2)}) collective-permute-start(f32[512,128]{1,0:T(8,128)S(1)} %get-tuple-element.68), channel_id=1, source_target_pairs={{0,2},{1,3},{2,1},{3,0},{4,6},{5,7},{6,5},{7,4},{8,10},{9,11},{10,... | collective-permute-start | bytes 786440 | tf_op jit(solution)/shard_map/ppermute | solution.py:379
  66.0 21.0 %collective-permute-start.22 = (f32[512,128]{1,0:T(8,128)S(1)}, f32[512,128]{1,0:T(8,128)S(1)}, u32[]{:S(2)}, u32[]{:S(2)}) collective-permute-start(f32[512,128]{1,0:T(8,128)S(1)} %get-tuple-element.69), channel_id=1, source_target_pairs={{0,1},{1,0},{2,3},{3,2},{4,5},{5,4},{6,7},{7,6},{8,9},{9,8},{10,11... | collective-permute-start | bytes 786440 | tf_op jit(solution)/shard_map/ppermute | solution.py:379

commit v6 on v5

--- a/solution.py
+++ b/solution.py
@@ -28,12 +28,13 @@
     return lax.axis_index("col"), lax.axis_index("row")
 
 
-def kernel_call(body, shapes, *args, scratch=()):
+def kernel_call(body, shapes, *args, scratch=(), halves=()):
     return pl.pallas_call(
         body,
-        out_shape=[jax.ShapeDtypeStruct(shape, jnp.float32) for shape in shapes],
+        out_shape=[jax.ShapeDtypeStruct(shape, jnp.float32) for shape in shapes]
+        + [jax.ShapeDtypeStruct(shape, jnp.bfloat16) for shape in halves],
         in_specs=[pl.BlockSpec(memory_space=pltpu.VMEM)] * len(args),
-        out_specs=[pl.BlockSpec(memory_space=pltpu.VMEM)] * len(shapes),
+        out_specs=[pl.BlockSpec(memory_space=pltpu.VMEM)] * (len(shapes) + len(halves)),
         scratch_shapes=[pltpu.VMEM(shape, kind) for shape, kind in scratch],
         compiler_params=pltpu.CompilerParams(vmem_limit_bytes=24 * 1024 * 1024),
     )(*args)
@@ -99,7 +100,7 @@
 def far_kernel(parts, steps, groups, rest, last, cols_size, *refs):
     place, pieces, refs = here(), refs[: len(steps)], refs[len(steps) :]
     if last:
-        field, keep, send, house, high, low, far_h, far_l = refs
+        field, keep, send, high, low, far_h, far_l = refs
     else:
         field, keep, send, far_h, far_l = refs
     col, core = place[0], place[1] & 1
@@ -113,7 +114,6 @@
             rows = pl.ds(at, own)
             value_h, value_l = split(value)
             if last:
-                house[panel, rows, :] = value
                 high[panel, rows, :], low[panel, rows, :] = value_h, value_l
             if step % groups in rest:
                 slot = 2 * rest.index(step % groups) + panel
@@ -194,11 +194,11 @@
 def tail_kernel(cols_size, groups, shift, ks, *refs):
     group = len(ks)
     place, blocks = here(), refs[: 2 * group]
-    factors, house, field = refs[2 * group : 3 + 2 * group]
-    outs, weights, cross = refs[3 + 2 * group : -2], refs[-2], refs[-1]
+    factors, high, low, field = refs[2 * group : 4 + 2 * group]
+    outs, weights, cross = refs[4 + 2 * group : -2], refs[-2], refs[-1]
     col, core = place[0], place[1] & 1
     me = (place[1] >> shift) & (group - 1)
-    width = house.shape[1]
+    width = high.shape[1]
     parts = 2 * group * blocks[0].shape[0]
     height = 2 * width // groups
     count = height // parts
@@ -221,8 +221,8 @@
     first = split(product(split(factors[0]), split(weights[:width])))
     second = weights[width:] - product(split(cross[...]), first)
     second = split(product(split(factors[1]), split(second)))
-    update = product(split(house[0]), first, FROM_TRANSPOSE)
-    update = update + product(split(house[1]), second, FROM_TRANSPOSE)
+    update = product((high[0], low[0]), first, FROM_TRANSPOSE)
+    update = update + product((high[1], low[1]), second, FROM_TRANSPOSE)
     cols = outs[0].shape[1]
     result = field[...] - update
     for c in range(cols_size):
@@ -329,11 +329,11 @@
             rows = len(rest) * count + (packed if last else 0)
             keep, send, *house = kernel_call(
                 body,
-                [(half, rows, eigvecs)] * 2 + [(2, width, local_rows)] * last,
+                [(half, rows, eigvecs)] * 2,
                 *[pieces[k] for k in steps],
                 vectors,
-                scratch=[((2, width, local_rows), bf16)] * (2 * last)
-                + [((2 * max(1, len(rest)) * near * own, local_rows), bf16)] * 2,
+                scratch=[((2 * max(1, len(rest)) * near * own, local_rows), bf16)] * 2,
+                halves=[(2, width, local_rows)] * (2 * last),
             )
             return [keep, swap(send, "row", rows_size, 1)], *house
 
@@ -349,7 +349,7 @@
                 pieces[k] = cut
             if rest == order and order:
                 (sources,) = far(wanted, rest, False)
-        pair, house = far(steps + [0], others, True)
+        pair, *house = far(steps + [0], others, True)
         order = order + others
         sources = exchanged(sources + pair, stages)
         sums = [same]
@@ -369,7 +369,7 @@
             [(local_rows, out_cols)] * cols_size,
             *gather(part + other),
             tfactors,
-            house,
+            *house,
             vectors,
             scratch=[((2 * width, eigvecs), jnp.float32), ((width, width), jnp.float32)],
         )

time: 88.2 us -> 88.1 us (level)
  no operation moved by 1% of the time
where the time goes in v6:
time: 88.1 us; the launch traced here: 87.9 us
  waiting for transfers between devices  57.1 us (65%)
  starting transfers between devices  23.6 us (27%)
  Pallas kernels  4.89 us (6%)
  local copies, waits for them, and re-layouts  2.23 us (3%)
    ppermute x15, waiting for transfers between devices, swap(): return lax.ppermute(block, axis, [(i, i ^ mask) for i in range(size)])  19.9 us
    ppermute x3, waiting for transfers between devices, per_device(): blocks[k] = lax.ppermute(blocks[k], 'col', pairs)  19.6 us
    ppermute x15, starting transfers between devices, swap(): return lax.ppermute(block, axis, [(i, i ^ mask) for i in range(size)])  10.7 us
    ppermute x2, waiting for transfers between devices, all_reduce_cols(): other = lax.ppermute(part, ('row', 'col'), pairs)  8.88 us
    ppermute x3, waiting for transfers between devices, per_device(): pieces[k] = lax.ppermute(cut, 'col', pairs) if k else cut  8.74 us
    ppermute x3, starting transfers between devices, per_device(): blocks[k] = lax.ppermute(blocks[k], 'col', pairs)  4.9 us
    ppermute x3, starting transfers between devices, per_device(): pieces[k] = lax.ppermute(cut, 'col', pairs) if k else cut  4.23 us
    pallas_call x8, Pallas kernels, kernel_call(): pl.pallas_call(body, out_shape=[jax.ShapeDtypeStruct(shape, jnp.float32)...  3.9 us
  transfers between devices with their start and end apart: 23, of which 18 were waited for; matrix products, arithmetic and copies ran while one was open for 1% of the time, Pallas kernels for 1%

profile of v6, /device:TPU:8, one launch (start us, length us, event | category | flops | bytes accessed | tf_op | source)
XLA Modules:
  0.0 87.9 jit_solution(4638936705971404522)
XLA Ops:
  0.0 1.1 %dynamic-slice_bitcast_fusion = f32[2,64,512]{2,1,0:T(8,128)S(1)} fusion(f32[2,2048,64]{1,2,0:T(8,128)} %param.6, s32[]{:T(128)S(6)} %select_n.12), kind=kLoop, calls=%fused_computation | loop fusion | bytes 524292 | tf_op jit(solution)/shard_map/dynamic_slice | solution.py:303
  1.1 1.6 %collective-permute-start.5 = (f32[2,64,512]{2,1,0:T(8,128)S(1)}, f32[2,64,512]{2,1,0:T(8,128)S(1)}, u32[]{:S(2)}, u32[]{:S(2)}) collective-permute-start(f32[2,64,512]{2,1,0:T(8,128)S(1)} %dynamic-slice_bitcast_fusion), channel_id=1, source_target_pairs={{0,3},{1,2},{2,0},{3,1},{4,7},{5,6},{6,4},{7,5},{8,11},{9,10},{10,... | collective-permute-start | bytes 786440 | tf_op jit(solution)/shard_map/ppermute | solution.py:307
  2.7 1.2 %constant_dynamic-slice_fusion = (f32[2,64,512]{2,1,0:T(8,128)S(1)}, f32[2,64,512]{2,1,0:T(8,128)S(1)}, f32[2,64,512]{2,1,0:T(8,128)S(1)}) fusion(f32[2,64,2048]{2,1,0:T(8,128)} %bitcast.4, s32[]{:T(128)S(6)} %select_n.15, s32[]{:T(128)S(6)} %select_n.14, s32[]{:T(128)S(6)} %select_n.13), kind=kLoop, calls=%fused_computation.1 | loop fusion | bytes 1572876 | tf_op jit(solution)/shard_map/dynamic_slice | solution.py:303
  3.9 1.4 %collective-permute-start.3 = (f32[2,64,512]{2,1,0:T(8,128)S(1)}, f32[2,64,512]{2,1,0:T(8,128)S(1)}, u32[]{:S(2)}, u32[]{:S(2)}) collective-permute-start(f32[2,64,512]{2,1,0:T(8,128)S(1)} %get-tuple-element.47), channel_id=1, source_target_pairs={{0,2},{1,3},{2,1},{3,0},{4,6},{5,7},{6,5},{7,4},{8,10},{9,11},{10,... | collective-permute-start | bytes 786440 | tf_op jit(solution)/shard_map/ppermute | solution.py:307
  5.3 1.2 %collective-permute-start.4 = (f32[2,64,512]{2,1,0:T(8,128)S(1)}, f32[2,64,512]{2,1,0:T(8,128)S(1)}, u32[]{:S(2)}, u32[]{:S(2)}) collective-permute-start(f32[2,64,512]{2,1,0:T(8,128)S(1)} %get-tuple-element.48), channel_id=1, source_target_pairs={{0,1},{1,0},{2,3},{3,2},{4,5},{5,4},{6,7},{7,6},{8,9},{9,8},{10,11... | collective-permute-start | bytes 786440 | tf_op jit(solution)/shard_map/ppermute | solution.py:307
  6.5 10.2 %conditional.1 = (f32[1,16,512]{2,1,0:T(8,128)S(1)}) conditional(s32[]{:T(128)} %convert_element_type.3, () %tuple.17, (f32[2,64,512]{2,1,0:T(8,128)S(1)}, f32[512,512]{1,0:T(8,128)S(1)}) %tuple.25), branch_computations={%region_0.0_spmd, %region_1.0_spmd} | conditional | flops 8192 | bytes 1015936 | solution.py:321
  6.5 0.4 branch_1_fun.3
  6.9 0.1 collective-permute-start
  7.0 1.3 %collective-permute-done.refs_1_ = f32[4,16,512]{2,1,0:T(8,128)S(1)} collective-permute-done((f32[4,16,512]{2,1,0:T(8,128)S(1)}, f32[4,16,512]{2,1,0:T(8,128)S(1)}, u32[]{:S(2)}, u32[]{:S(2)}) %collective-permute-start) | collective-permute-done | bytes 131104 | tf_op jit(solution)/shard_map/cond/branch_1_fun/ppermute | solution.py:44
  8.3 1.6 %collective-permute-start.1 = (f32[2,16,512]{2,1,0:T(8,128)S(1)}, f32[2,16,512]{2,1,0:T(8,128)S(1)}, u32[]{:S(2)}, u32[]{:S(2)}) collective-permute-start(f32[2,16,512]{2,1,0:T(8,128)S(1)} %get-tuple-element.17), channel_id=1, source_target_pairs={{0,8},{4,12},{8,0},{12,4},{16,24},{20,28},{24,16},{28,20},{1,9},{5... | collective-permute-start | bytes 196616 | tf_op jit(solution)/shard_map/cond/branch_1_fun/ppermute | solution.py:44
  9.9 2.8 %collective-permute-done.1.refs_1_ = f32[2,16,512]{2,1,0:T(8,128)S(1)} collective-permute-done((f32[2,16,512]{2,1,0:T(8,128)S(1)}, f32[2,16,512]{2,1,0:T(8,128)S(1)}, u32[]{:S(2)}, u32[]{:S(2)}) %collective-permute-start.1) | collective-permute-done | bytes 65568 | tf_op jit(solution)/shard_map/cond/branch_1_fun/ppermute | solution.py:44
  12.7 1.6 %collective-permute-start.2 = (f32[1,16,512]{2,1,0:T(8,128)S(1)}, f32[1,16,512]{2,1,0:T(8,128)S(1)}, u32[]{:S(2)}, u32[]{:S(2)}) collective-permute-start(f32[1,16,512]{2,1,0:T(8,128)S(1)} %get-tuple-element.19), channel_id=1, source_target_pairs={{0,16},{4,20},{8,24},{12,28},{16,0},{20,4},{24,8},{28,12},{1,17},{... | collective-permute-start | bytes 98312 | tf_op jit(solution)/shard_map/cond/branch_1_fun/ppermute | solution.py:44
  14.3 2.4 %collective-permute-done.2 = f32[1,16,512]{2,1,0:T(8,128)S(1)} collective-permute-done((f32[1,16,512]{2,1,0:T(8,128)S(1)}, f32[1,16,512]{2,1,0:T(8,128)S(1)}, u32[]{:S(2)}, u32[]{:S(2)}) %collective-permute-start.2) | collective-permute-done | bytes 32800 | tf_op jit(solution)/shard_map/cond/branch_1_fun/ppermute | solution.py:44
  16.7 4.0 %collective-permute-done.5.refs_0_ = f32[2,64,512]{2,1,0:T(8,128)S(1)} collective-permute-done((f32[2,64,512]{2,1,0:T(8,128)S(1)}, f32[2,64,512]{2,1,0:T(8,128)S(1)}, u32[]{:S(2)}, u32[]{:S(2)}) %collective-permute-start.5) | collective-permute-done | bytes 262176 | tf_op jit(solution)/shard_map/ppermute | solution.py:307
  20.6 0.4 shard_map.37
  21.1 0.1 collective-permute-start.6
  21.1 4.8 %collective-permute-done.3.refs_2_ = f32[2,64,512]{2,1,0:T(8,128)S(1)} collective-permute-done((f32[2,64,512]{2,1,0:T(8,128)S(1)}, f32[2,64,512]{2,1,0:T(8,128)S(1)}, u32[]{:S(2)}, u32[]{:S(2)}) %collective-permute-start.3) | collective-permute-done | bytes 262176 | tf_op jit(solution)/shard_map/ppermute | solution.py:307
  25.9 0.8 shard_map.38
  26.7 0.1 collective-permute-start.7
  26.8 1.7 %collective-permute-done.7.refs_3_ = f32[4,48,512]{2,1,0:T(8,128)S(1)} collective-permute-done((f32[4,48,512]{2,1,0:T(8,128)S(1)}, f32[4,48,512]{2,1,0:T(8,128)S(1)}, u32[]{:S(2)}, u32[]{:S(2)}) %collective-permute-start.7) | collective-permute-done | bytes 393248 | tf_op jit(solution)/shard_map/ppermute | solution.py:44
  28.5 0.1 shard_map.39
  28.6 1.6 %collective-permute-start.8 = (f32[1,64,512]{2,1,0:T(8,128)S(1)}, f32[1,64,512]{2,1,0:T(8,128)S(1)}, u32[]{:S(2)}, u32[]{:S(2)}) collective-permute-start(f32[1,64,512]{2,1,0:T(8,128)S(1)} %get-tuple-element.63), channel_id=1, source_target_pairs={{0,16},{4,20},{8,24},{12,28},{16,0},{20,4},{24,8},{28,12},{1,17},{... | collective-permute-start | bytes 393224 | tf_op jit(solution)/shard_map/ppermute | solution.py:44
  30.2 1.5 %collective-permute-start.9 = (f32[1,64,512]{2,1,0:T(8,128)S(1)}, f32[1,64,512]{2,1,0:T(8,128)S(1)}, u32[]{:S(2)}, u32[]{:S(2)}) collective-permute-start(f32[1,64,512]{2,1,0:T(8,128)S(1)} %get-tuple-element.64), channel_id=1, source_target_pairs={{0,8},{4,12},{8,0},{12,4},{16,24},{20,28},{24,16},{28,20},{1,9},{5... | collective-permute-start | bytes 393224 | tf_op jit(solution)/shard_map/ppermute | solution.py:44
  31.7 0.4 collective-permute-start.10
  32.1 2.0 %collective-permute-done.8.refs_2_ = f32[1,64,512]{2,1,0:T(8,128)S(1)} collective-permute-done((f32[1,64,512]{2,1,0:T(8,128)S(1)}, f32[1,64,512]{2,1,0:T(8,128)S(1)}, u32[]{:S(2)}, u32[]{:S(2)}) %collective-permute-start.8) | collective-permute-done | bytes 131104 | tf_op jit(solution)/shard_map/ppermute | solution.py:44
  34.2 2.4 %collective-permute-done.9.refs_3_ = f32[1,64,512]{2,1,0:T(8,128)S(1)} collective-permute-done((f32[1,64,512]{2,1,0:T(8,128)S(1)}, f32[1,64,512]{2,1,0:T(8,128)S(1)}, u32[]{:S(2)}, u32[]{:S(2)}) %collective-permute-start.9) | collective-permute-done | bytes 131104 | tf_op jit(solution)/shard_map/ppermute | solution.py:44
  36.6 1.6 %collective-permute-done.10.refs_4_ = f32[1,64,512]{2,1,0:T(8,128)S(1)} collective-permute-done((f32[1,64,512]{2,1,0:T(8,128)S(1)}, f32[1,64,512]{2,1,0:T(8,128)S(1)}, u32[]{:S(2)}, u32[]{:S(2)}) %collective-permute-start.10) | collective-permute-done | bytes 131104 | tf_op jit(solution)/shard_map/ppermute | solution.py:44
  38.2 0.0 copy-start
  38.2 0.1 collective-permute-start.11
  38.3 5.3 %collective-permute-done.11 = f32[1,80,512]{2,1,0:T(8,128)S(1)} collective-permute-done((f32[1,80,512]{2,1,0:T(8,128)S(1)}, f32[1,80,512]{2,1,0:T(8,128)S(1)}, u32[]{:S(2)}, u32[]{:S(2)}) %collective-permute-start.11) | collective-permute-done | bytes 163872 | tf_op jit(solution)/shard_map/ppermute | solution.py:244
  43.6 3.6 %collective-permute-start.12 = (f32[1,80,512]{2,1,0:T(8,128)S(1)}, f32[1,80,512]{2,1,0:T(8,128)S(1)}, u32[]{:S(2)}, u32[]{:S(2)}) collective-permute-start(f32[1,80,512]{2,1,0:T(8,128)S(1)} %add.60), channel_id=1, source_target_pairs={{0,2},{1,3},{2,0},{3,1},{4,5},{5,4},{6,7},{7,6},{8,10},{9,11},{10,... | collective-permute-start | bytes 491528 | tf_op jit(solution)/shard_map/ppermute | solution.py:244
  47.3 3.6 %collective-permute-done.12 = f32[1,80,512]{2,1,0:T(8,128)S(1)} collective-permute-done((f32[1,80,512]{2,1,0:T(8,128)S(1)}, f32[1,80,512]{2,1,0:T(8,128)S(1)}, u32[]{:S(2)}, u32[]{:S(2)}) %collective-permute-start.12) | collective-permute-done | bytes 163872 | tf_op jit(solution)/shard_map/ppermute | solution.py:244
  50.9 2.2 %collective-permute-start.15 = (f32[1,80,512]{2,1,0:T(8,128)S(1)}, f32[1,80,512]{2,1,0:T(8,128)S(1)}, u32[]{:S(2)}, u32[]{:S(2)}) collective-permute-start(f32[1,80,512]{2,1,0:T(8,128)S(1)} %add.61.refs_0_), channel_id=1, source_target_pairs={{0,24},{4,28},{8,16},{12,20},{16,8},{20,12},{24,0},{28,4},{1,25},{... | collective-permute-start | bytes 491528 | tf_op jit(solution)/shard_map/ppermute | solution.py:44
  53.1 0.5 collective-permute-start.14
  53.6 0.8 collective-permute-start.13
  54.4 2.7 %collective-permute-done.15.refs_3_ = f32[1,80,512]{2,1,0:T(8,128)S(1)} collective-permute-done((f32[1,80,512]{2,1,0:T(8,128)S(1)}, f32[1,80,512]{2,1,0:T(8,128)S(1)}, u32[]{:S(2)}, u32[]{:S(2)}) %collective-permute-start.15) | collective-permute-done | bytes 163872 | tf_op jit(solution)/shard_map/ppermute | solution.py:44
  57.2 1.5 %collective-permute-done.14.refs_2_ = f32[1,80,512]{2,1,0:T(8,128)S(1)} collective-permute-done((f32[1,80,512]{2,1,0:T(8,128)S(1)}, f32[1,80,512]{2,1,0:T(8,128)S(1)}, u32[]{:S(2)}, u32[]{:S(2)}) %collective-permute-start.14) | collective-permute-done | bytes 163872 | tf_op jit(solution)/shard_map/ppermute | solution.py:44
  58.7 0.3 collective-permute-done.13.refs_1_
  58.9 0.2 collective-permute-start.17
  59.2 0.9 collective-permute-done.18.refs_6_
  60.1 0.3 collective-permute-done.17.refs_5_
  60.3 2.1 %shard_map.41 = (f32[512,128]{1,0:T(8,128)S(1)}, f32[512,128]{1,0:T(8,128)S(1)}, f32[512,128]{1,0:T(8,128)S(1)}, f32[512,128]{1,0:T(8,128)S(1)}) custom-call(f32[1,80,512]{2,1,0:T(8,128)S(1)} %add.61.refs_0_, f32[1,80,512]{2,1,0:T(8,128)S(1)} %collective-permute-done.13.refs_1_, f32[1,80,512]{2,1,0:T(8,128)S(1)} %collective-permute-done.14.refs_2_, ...), custom_call_target="tpu_custom_call" | custom-call | tf_op jit(solution)/shard_map/pallas_call | solution.py:32
  62.5 0.9 collective-permute-start.20
  63.3 2.6 %collective-permute-start.21 = (f32[512,128]{1,0:T(8,128)S(1)}, f32[512,128]{1,0:T(8,128)S(1)}, u32[]{:S(2)}, u32[]{:S(2)}) collective-permute-start(f32[512,128]{1,0:T(8,128)S(1)} %get-tuple-element.70), channel_id=1, source_target_pairs={{0,2},{1,3},{2,1},{3,0},{4,6},{5,7},{6,5},{7,4},{8,10},{9,11},{10,... | collective-permute-start | bytes 786440 | tf_op jit(solution)/shard_map/ppermute | solution.py:379
  66.0 1.4 %collective-permute-start.22 = (f32[512,128]{1,0:T(8,128)S(1)}, f32[512,128]{1,0:T(8,128)S(1)}, u32[]{:S(2)}, u32[]{:S(2)}) collective-permute-start(f32[512,128]{1,0:T(8,128)S(1)} %get-tuple-element.71), channel_id=1, source_target_pairs={{0,1},{1,0},{2,3},{3,2},{4,5},{5,4},{6,7},{7,6},{8,9},{9,8},{10,11... | collective-permute-start | bytes 786440 | tf_op jit(solution)/shard_map/ppermute | solution.py:379
  67.4 13.8 %collective-permute-done.20.refs_1_ = f32[512,128]{1,0:T(8,128)S(1)} collective-permute-done((f32[512,128]{1,0:T(8,128)S(1)}, f32[512,128]{1,0:T(8,128)S(1)}, u32[]{:S(2)}, u32[]{:S(2)}) %collective-permute-start.20) | collective-permute-done | bytes 262176 | tf_op jit(solution)/shard_map/ppermute | solution.py:379
  81.2 5.7 %collective-permute-done.21.refs_2_ = f32[512,128]{1,0:T(8,128)S(1)} collective-permute-done((f32[512,128]{1,0:T(8,128)S(1)}, f32[512,128]{1,0:T(8,128)S(1)}, u32[]{:S(2)}, u32[]{:S(2)}) %collective-permute-start.21) | collective-permute-done | bytes 262176 | tf_op jit(solution)/shard_map/ppermute | solution.py:379
  86.9 1.0 %shard_map.42 = f32[4,512,128]{2,1,0:T(8,128)} custom-call(f32[512,128]{1,0:T(8,128)S(1)} %get-tuple-element.68.refs_0_, f32[512,128]{1,0:T(8,128)S(1)} %collective-permute-done.20.refs_1_, f32[512,128]{1,0:T(8,128)S(1)} %collective-permute-done.21.refs_2_, f32[512,128]{1,0:T(8,128)S(1)} %collective-permute-done.22.refs_3_), custom_call_target="tpu_custom_call" | custom-call | tf_op jit(solution)/shard_map/pallas_call | solution.py:381
  (17 shorter events, 0.1 us)
Async XLA Ops:
  0.0 6.5 %copy-start.1 = (f32[512,512]{1,0:T(8,128)S(1)}, f32[512,512]{1,0:T(8,128)}, u32[]{:S(2)}) copy-start(f32[512,512]{1,0:T(8,128)} %refs_11_.1) | copy-start | bytes 3145732
  1.1 19.6 %collective-permute-start.5 = (f32[2,64,512]{2,1,0:T(8,128)S(1)}, f32[2,64,512]{2,1,0:T(8,128)S(1)}, u32[]{:S(2)}, u32[]{:S(2)}) collective-permute-start(f32[2,64,512]{2,1,0:T(8,128)S(1)} %dynamic-slice_bitcast_fusion), channel_id=1, source_target_pairs={{0,3},{1,2},{2,0},{3,1},{4,7},{5,6},{6,4},{7,5},{8,11},{9,10},{10,... | collective-permute-start | bytes 786440 | tf_op jit(solution)/shard_map/ppermute | solution.py:307
  3.9 22.0 %collective-permute-start.3 = (f32[2,64,512]{2,1,0:T(8,128)S(1)}, f32[2,64,512]{2,1,0:T(8,128)S(1)}, u32[]{:S(2)}, u32[]{:S(2)}) collective-permute-start(f32[2,64,512]{2,1,0:T(8,128)S(1)} %get-tuple-element.47), channel_id=1, source_target_pairs={{0,2},{1,3},{2,1},{3,0},{4,6},{5,7},{6,5},{7,4},{8,10},{9,11},{10,... | collective-permute-start | bytes 786440 | tf_op jit(solution)/shard_map/ppermute | solution.py:307
  5.3 20.6 %collective-permute-start.4 = (f32[2,64,512]{2,1,0:T(8,128)S(1)}, f32[2,64,512]{2,1,0:T(8,128)S(1)}, u32[]{:S(2)}, u32[]{:S(2)}) collective-permute-start(f32[2,64,512]{2,1,0:T(8,128)S(1)} %get-tuple-element.48), channel_id=1, source_target_pairs={{0,1},{1,0},{2,3},{3,2},{4,5},{5,4},{6,7},{7,6},{8,9},{9,8},{10,11... | collective-permute-start | bytes 786440 | tf_op jit(solution)/shard_map/ppermute | solution.py:307
  6.9 1.4 %collective-permute-start = (f32[4,16,512]{2,1,0:T(8,128)S(1)}, f32[4,16,512]{2,1,0:T(8,128)S(1)}, u32[]{:S(2)}, u32[]{:S(2)}) collective-permute-start(f32[4,16,512]{2,1,0:T(8,128)S(1)} %get-tuple-element.15), channel_id=1, source_target_pairs={{0,4},{4,0},{8,12},{12,8},{16,20},{20,16},{24,28},{28,24},{1,5},{5... | collective-permute-start | bytes 393224 | tf_op jit(solution)/shard_map/cond/branch_1_fun/ppermute | solution.py:44
  8.3 4.3 %collective-permute-start.1 = (f32[2,16,512]{2,1,0:T(8,128)S(1)}, f32[2,16,512]{2,1,0:T(8,128)S(1)}, u32[]{:S(2)}, u32[]{:S(2)}) collective-permute-start(f32[2,16,512]{2,1,0:T(8,128)S(1)} %get-tuple-element.17), channel_id=1, source_target_pairs={{0,8},{4,12},{8,0},{12,4},{16,24},{20,28},{24,16},{28,20},{1,9},{5... | collective-permute-start | bytes 196616 | tf_op jit(solution)/shard_map/cond/branch_1_fun/ppermute | solution.py:44
  12.7 4.0 %collective-permute-start.2 = (f32[1,16,512]{2,1,0:T(8,128)S(1)}, f32[1,16,512]{2,1,0:T(8,128)S(1)}, u32[]{:S(2)}, u32[]{:S(2)}) collective-permute-start(f32[1,16,512]{2,1,0:T(8,128)S(1)} %get-tuple-element.19), channel_id=1, source_target_pairs={{0,16},{4,20},{8,24},{12,28},{16,0},{20,4},{24,8},{28,12},{1,17},{... | collective-permute-start | bytes 98312 | tf_op jit(solution)/shard_map/cond/branch_1_fun/ppermute | solution.py:44
  21.1 4.8 %collective-permute-start.6 = (f32[4,16,512]{2,1,0:T(8,128)S(1)}, f32[4,16,512]{2,1,0:T(8,128)S(1)}, u32[]{:S(2)}, u32[]{:S(2)}) collective-permute-start(f32[4,16,512]{2,1,0:T(8,128)S(1)} %get-tuple-element.54), channel_id=1, source_target_pairs={{0,4},{4,0},{8,12},{12,8},{16,20},{20,16},{24,28},{28,24},{1,5},{5... | collective-permute-start | bytes 393224 | tf_op jit(solution)/shard_map/ppermute | solution.py:44
  26.7 1.8 %collective-permute-start.7 = (f32[4,48,512]{2,1,0:T(8,128)S(1)}, f32[4,48,512]{2,1,0:T(8,128)S(1)}, u32[]{:S(2)}, u32[]{:S(2)}) collective-permute-start(f32[4,48,512]{2,1,0:T(8,128)S(1)} %get-tuple-element.61), channel_id=1, source_target_pairs={{0,4},{4,0},{8,12},{12,8},{16,20},{20,16},{24,28},{28,24},{1,5},{5... | collective-permute-start | bytes 1179656 | tf_op jit(solution)/shard_map/ppermute | solution.py:44
  28.6 5.6 %collective-permute-start.8 = (f32[1,64,512]{2,1,0:T(8,128)S(1)}, f32[1,64,512]{2,1,0:T(8,128)S(1)}, u32[]{:S(2)}, u32[]{:S(2)}) collective-permute-start(f32[1,64,512]{2,1,0:T(8,128)S(1)} %get-tuple-element.63), channel_id=1, source_target_pairs={{0,16},{4,20},{8,24},{12,28},{16,0},{20,4},{24,8},{28,12},{1,17},{... | collective-permute-start | bytes 393224 | tf_op jit(solution)/shard_map/ppermute | solution.py:44
  30.2 6.4 %collective-permute-start.9 = (f32[1,64,512]{2,1,0:T(8,128)S(1)}, f32[1,64,512]{2,1,0:T(8,128)S(1)}, u32[]{:S(2)}, u32[]{:S(2)}) collective-permute-start(f32[1,64,512]{2,1,0:T(8,128)S(1)} %get-tuple-element.64), channel_id=1, source_target_pairs={{0,8},{4,12},{8,0},{12,4},{16,24},{20,28},{24,16},{28,20},{1,9},{5... | collective-permute-start | bytes 393224 | tf_op jit(solution)/shard_map/ppermute | solution.py:44
  31.7 6.5 %collective-permute-start.10 = (f32[1,64,512]{2,1,0:T(8,128)S(1)}, f32[1,64,512]{2,1,0:T(8,128)S(1)}, u32[]{:S(2)}, u32[]{:S(2)}) collective-permute-start(f32[1,64,512]{2,1,0:T(8,128)S(1)} %get-tuple-element.65), channel_id=1, source_target_pairs={{0,24},{4,28},{8,16},{12,20},{16,8},{20,12},{24,0},{28,4},{1,25},{... | collective-permute-start | bytes 393224 | tf_op jit(solution)/shard_map/ppermute | solution.py:44
  38.2 22.1 %copy-start = (f32[2,256,256]{2,1,0:T(8,128)S(1)}, f32[2,256,256]{2,1,0:T(8,128)}, u32[]{:S(2)}) copy-start(f32[2,256,256]{2,1,0:T(8,128)} %refs_8_.1) | copy-start | bytes 1572868
  38.2 5.4 %collective-permute-start.11 = (f32[1,80,512]{2,1,0:T(8,128)S(1)}, f32[1,80,512]{2,1,0:T(8,128)S(1)}, u32[]{:S(2)}, u32[]{:S(2)}) collective-permute-start(f32[1,80,512]{2,1,0:T(8,128)S(1)} %shard_map.40), channel_id=1, source_target_pairs={{0,1},{1,0},{2,3},{3,2},{4,6},{5,7},{6,4},{7,5},{8,9},{9,8},{10,11... | collective-permute-start | bytes 491528 | tf_op jit(solution)/shard_map/ppermute | solution.py:244
  43.6 7.2 %collective-permute-start.12 = (f32[1,80,512]{2,1,0:T(8,128)S(1)}, f32[1,80,512]{2,1,0:T(8,128)S(1)}, u32[]{:S(2)}, u32[]{:S(2)}) collective-permute-start(f32[1,80,512]{2,1,0:T(8,128)S(1)} %add.60), channel_id=1, source_target_pairs={{0,2},{1,3},{2,0},{3,1},{4,5},{5,4},{6,7},{7,6},{8,10},{9,11},{10,... | collective-permute-start | bytes 491528 | tf_op jit(solution)/shard_map/ppermute | solution.py:244
  50.9 6.3 %collective-permute-start.15 = (f32[1,80,512]{2,1,0:T(8,128)S(1)}, f32[1,80,512]{2,1,0:T(8,128)S(1)}, u32[]{:S(2)}, u32[]{:S(2)}) collective-permute-start(f32[1,80,512]{2,1,0:T(8,128)S(1)} %add.61.refs_0_), channel_id=1, source_target_pairs={{0,24},{4,28},{8,16},{12,20},{16,8},{20,12},{24,0},{28,4},{1,25},{... | collective-permute-start | bytes 491528 | tf_op jit(solution)/shard_map/ppermute | solution.py:44
  53.1 5.6 %collective-permute-start.14 = (f32[1,80,512]{2,1,0:T(8,128)S(1)}, f32[1,80,512]{2,1,0:T(8,128)S(1)}, u32[]{:S(2)}, u32[]{:S(2)}) collective-permute-start(f32[1,80,512]{2,1,0:T(8,128)S(1)} %add.61.refs_0_), channel_id=1, source_target_pairs={{0,8},{4,12},{8,0},{12,4},{16,24},{20,28},{24,16},{28,20},{1,9},{5... | collective-permute-start | bytes 491528 | tf_op jit(solution)/shard_map/ppermute | solution.py:44
  53.6 5.3 %collective-permute-start.13 = (f32[1,80,512]{2,1,0:T(8,128)S(1)}, f32[1,80,512]{2,1,0:T(8,128)S(1)}, u32[]{:S(2)}, u32[]{:S(2)}) collective-permute-start(f32[1,80,512]{2,1,0:T(8,128)S(1)} %add.61.refs_0_), channel_id=1, source_target_pairs={{0,16},{4,20},{8,24},{12,28},{16,0},{20,4},{24,8},{28,12},{1,17},{... | collective-permute-start | bytes 491528 | tf_op jit(solution)/shard_map/ppermute | solution.py:44
  54.4 4.7 %collective-permute-start.16 = (f32[1,80,512]{2,1,0:T(8,128)S(1)}, f32[1,80,512]{2,1,0:T(8,128)S(1)}, u32[]{:S(2)}, u32[]{:S(2)}) collective-permute-start(f32[1,80,512]{2,1,0:T(8,128)S(1)} %add.61.refs_0_), channel_id=1, source_target_pairs={{0,4},{4,0},{8,12},{12,8},{16,20},{20,16},{24,28},{28,24},{1,5},{5... | collective-permute-start | bytes 491528 | tf_op jit(solution)/shard_map/ppermute | solution.py:44
  57.2 2.0 %collective-permute-start.19 = (f32[1,80,512]{2,1,0:T(8,128)S(1)}, f32[1,80,512]{2,1,0:T(8,128)S(1)}, u32[]{:S(2)}, u32[]{:S(2)}) collective-permute-start(f32[1,80,512]{2,1,0:T(8,128)S(1)} %collective-permute-done.15.refs_3_), channel_id=1, source_target_pairs={{0,4},{4,0},{8,12},{12,8},{16,20},{20,16},{24,28},{28,24},{1,5},{5... | collective-permute-start | bytes 491528 | tf_op jit(solution)/shard_map/ppermute | solution.py:44
  58.7 1.4 %collective-permute-start.18 = (f32[1,80,512]{2,1,0:T(8,128)S(1)}, f32[1,80,512]{2,1,0:T(8,128)S(1)}, u32[]{:S(2)}, u32[]{:S(2)}) collective-permute-start(f32[1,80,512]{2,1,0:T(8,128)S(1)} %collective-permute-done.14.refs_2_), channel_id=1, source_target_pairs={{0,4},{4,0},{8,12},{12,8},{16,20},{20,16},{24,28},{28,24},{1,5},{5... | collective-permute-start | bytes 491528 | tf_op jit(solution)/shard_map/ppermute | solution.py:44
  58.9 1.4 %collective-permute-start.17 = (f32[1,80,512]{2,1,0:T(8,128)S(1)}, f32[1,80,512]{2,1,0:T(8,128)S(1)}, u32[]{:S(2)}, u32[]{:S(2)}) collective-permute-start(f32[1,80,512]{2,1,0:T(8,128)S(1)} %collective-permute-done.13.refs_1_), channel_id=1, source_target_pairs={{0,4},{4,0},{8,12},{12,8},{16,20},{20,16},{24,28},{28,24},{1,5},{5... | collective-permute-start | bytes 491528 | tf_op jit(solution)/shard_map/ppermute | solution.py:44
  62.5 18.8 %collective-permute-start.20 = (f32[512,128]{1,0:T(8,128)S(1)}, f32[512,128]{1,0:T(8,128)S(1)}, u32[]{:S(2)}, u32[]{:S(2)}) collective-permute-start(f32[512,128]{1,0:T(8,128)S(1)} %get-tuple-element.69), channel_id=1, source_target_pairs={{0,3},{1,2},{2,0},{3,1},{4,7},{5,6},{6,4},{7,5},{8,11},{9,10},{10,... | collective-permute-start | bytes 786440 | tf_op jit(solution)/shard_map/ppermute | solution.py:379
  63.3 23.6 %collective-permute-start.21 = (f32[512,128]{1,0:T(8,128)S(1)}, f32[512,128]{1,0:T(8,128)S(1)}, u32[]{:S(2)}, u32[]{:S(2)}) collective-permute-start(f32[512,128]{1,0:T(8,128)S(1)} %get-tuple-element.70), channel_id=1, source_target_pairs={{0,2},{1,3},{2,1},{3,0},{4,6},{5,7},{6,5},{7,4},{8,10},{9,11},{10,... | collective-permute-start | bytes 786440 | tf_op jit(solution)/shard_map/ppermute | solution.py:379
  66.0 21.0 %collective-permute-start.22 = (f32[512,128]{1,0:T(8,128)S(1)}, f32[512,128]{1,0:T(8,128)S(1)}, u32[]{:S(2)}, u32[]{:S(2)}) collective-permute-start(f32[512,128]{1,0:T(8,128)S(1)} %get-tuple-element.71), channel_id=1, source_target_pairs={{0,1},{1,0},{2,3},{3,2},{4,5},{5,4},{6,7},{7,6},{8,9},{9,8},{10,11... | collective-permute-start | bytes 786440 | tf_op jit(solution)/shard_map/ppermute | solution.py:379

commit v7 on v6

--- a/solution.py
+++ b/solution.py
@@ -22,6 +22,13 @@
         return lax.dot_general(a, b, (contract, ((), ())), preferred_element_type=jnp.float32)
 
     return one(left[0], right[0]) + (one(left[0], right[1]) + one(left[1], right[0]))
+
+
+def joined(left, right, contract=PLAIN):
+    (i,), (j,) = contract
+    left = jnp.concatenate([left[0], left[1], left[0]], i)
+    right = jnp.concatenate([right[0], right[0], right[1]], j)
+    return lax.dot_general(left, right, (contract, ((), ())), preferred_element_type=jnp.float32)
 
 
 def here():
@@ -88,7 +95,7 @@
         for panel in range(2):
             rows = pl.ds(panel * near * own + at, own)
             high[rows, :], low[rows, :] = split(piece[panel])
-    result = product((high[...], low[...]), split(field[...]))
+    result = joined((high[...], low[...]), split(field[...]))
     for j in range(parts // 2):
         rows = keep.shape[1]
         even = result[2 * j * rows : (2 * j + 1) * rows]
@@ -120,11 +127,11 @@
                 rows = pl.ds(inside + slot * near * own, own)
                 far_h[rows, :], far_l[rows, :] = value_h, value_l
     if rest:
-        result = product((far_h[...], far_l[...]), split(field[...]))
+        result = joined((far_h[...], far_l[...]), split(field[...]))
     height = 2 * near * own
     count = height // parts
     if last:
-        cross = product((high[1], low[1]), (high[0], low[0]), BY_TRANSPOSE)
+        cross = joined((high[1], low[1]), (high[0], low[0]), BY_TRANSPOSE)
         rows = cross.shape[0] // parts
         side = keep.shape[2] // cross.shape[1]
         packed = -(-rows // side)

time: 88.1 us -> 88.1 us (level)
  no operation moved by 1% of the time
where the time goes in v7:
time: 88.1 us; the launch traced here: 87.9 us
  waiting for transfers between devices  57.1 us (65%)
  starting transfers between devices  23.6 us (27%)
  Pallas kernels  4.83 us (5%)
  local copies, waits for them, and re-layouts  2.23 us (3%)
    ppermute x15, waiting for transfers between devices, swap(): return lax.ppermute(block, axis, [(i, i ^ mask) for i in range(size)])  19.9 us
    ppermute x3, waiting for transfers between devices, per_device(): blocks[k] = lax.ppermute(blocks[k], 'col', pairs)  19.6 us
    ppermute x15, starting transfers between devices, swap(): return lax.ppermute(block, axis, [(i, i ^ mask) for i in range(size)])  10.7 us
    ppermute x2, waiting for transfers between devices, all_reduce_cols(): other = lax.ppermute(part, ('row', 'col'), pairs)  8.88 us
    ppermute x3, waiting for transfers between devices, per_device(): pieces[k] = lax.ppermute(cut, 'col', pairs) if k else cut  8.81 us
    ppermute x3, starting transfers between devices, per_device(): blocks[k] = lax.ppermute(blocks[k], 'col', pairs)  4.89 us
    ppermute x3, starting transfers between devices, per_device(): pieces[k] = lax.ppermute(cut, 'col', pairs) if k else cut  4.23 us
    pallas_call x8, Pallas kernels, kernel_call(): pl.pallas_call(body, out_shape=[jax.ShapeDtypeStruct(shape, jnp.float32)...  3.83 us
  transfers between devices with their start and end apart: 23, of which 18 were waited for; matrix products, arithmetic and copies ran while one was open for 1% of the time, Pallas kernels for 1%

profile of v7, /device:TPU:8, one launch (start us, length us, event | category | flops | bytes accessed | tf_op | source)
XLA Modules:
  0.0 87.9 jit_solution(5154443720047199509)
XLA Ops:
  0.0 1.1 %dynamic-slice_bitcast_fusion = f32[2,64,512]{2,1,0:T(8,128)S(1)} fusion(f32[2,2048,64]{1,2,0:T(8,128)} %param.6, s32[]{:T(128)S(6)} %select_n.12), kind=kLoop, calls=%fused_computation | loop fusion | bytes 524292 | tf_op jit(solution)/shard_map/dynamic_slice | solution.py:310
  1.1 1.6 %collective-permute-start.5 = (f32[2,64,512]{2,1,0:T(8,128)S(1)}, f32[2,64,512]{2,1,0:T(8,128)S(1)}, u32[]{:S(2)}, u32[]{:S(2)}) collective-permute-start(f32[2,64,512]{2,1,0:T(8,128)S(1)} %dynamic-slice_bitcast_fusion), channel_id=1, source_target_pairs={{0,3},{1,2},{2,0},{3,1},{4,7},{5,6},{6,4},{7,5},{8,11},{9,10},{10,... | collective-permute-start | bytes 786440 | tf_op jit(solution)/shard_map/ppermute | solution.py:314
  2.7 1.2 %constant_dynamic-slice_fusion = (f32[2,64,512]{2,1,0:T(8,128)S(1)}, f32[2,64,512]{2,1,0:T(8,128)S(1)}, f32[2,64,512]{2,1,0:T(8,128)S(1)}) fusion(f32[2,64,2048]{2,1,0:T(8,128)} %bitcast.4, s32[]{:T(128)S(6)} %select_n.15, s32[]{:T(128)S(6)} %select_n.14, s32[]{:T(128)S(6)} %select_n.13), kind=kLoop, calls=%fused_computation.1 | loop fusion | bytes 1572876 | tf_op jit(solution)/shard_map/dynamic_slice | solution.py:310
  3.9 1.4 %collective-permute-start.3 = (f32[2,64,512]{2,1,0:T(8,128)S(1)}, f32[2,64,512]{2,1,0:T(8,128)S(1)}, u32[]{:S(2)}, u32[]{:S(2)}) collective-permute-start(f32[2,64,512]{2,1,0:T(8,128)S(1)} %get-tuple-element.47), channel_id=1, source_target_pairs={{0,2},{1,3},{2,1},{3,0},{4,6},{5,7},{6,5},{7,4},{8,10},{9,11},{10,... | collective-permute-start | bytes 786440 | tf_op jit(solution)/shard_map/ppermute | solution.py:314
  5.3 1.2 %collective-permute-start.4 = (f32[2,64,512]{2,1,0:T(8,128)S(1)}, f32[2,64,512]{2,1,0:T(8,128)S(1)}, u32[]{:S(2)}, u32[]{:S(2)}) collective-permute-start(f32[2,64,512]{2,1,0:T(8,128)S(1)} %get-tuple-element.48), channel_id=1, source_target_pairs={{0,1},{1,0},{2,3},{3,2},{4,5},{5,4},{6,7},{7,6},{8,9},{9,8},{10,11... | collective-permute-start | bytes 786440 | tf_op jit(solution)/shard_map/ppermute | solution.py:314
  6.5 10.2 %conditional.1 = (f32[1,16,512]{2,1,0:T(8,128)S(1)}) conditional(s32[]{:T(128)} %convert_element_type.3, () %tuple.17, (f32[2,64,512]{2,1,0:T(8,128)S(1)}, f32[512,512]{1,0:T(8,128)S(1)}) %tuple.25), branch_computations={%region_0.0_spmd, %region_1.0_spmd} | conditional | flops 8192 | bytes 1015936 | solution.py:328
  6.5 0.4 branch_1_fun.3
  6.9 0.1 collective-permute-start
  6.9 1.3 %collective-permute-done.refs_1_ = f32[4,16,512]{2,1,0:T(8,128)S(1)} collective-permute-done((f32[4,16,512]{2,1,0:T(8,128)S(1)}, f32[4,16,512]{2,1,0:T(8,128)S(1)}, u32[]{:S(2)}, u32[]{:S(2)}) %collective-permute-start) | collective-permute-done | bytes 131104 | tf_op jit(solution)/shard_map/cond/branch_1_fun/ppermute | solution.py:51
  8.3 1.6 %collective-permute-start.1 = (f32[2,16,512]{2,1,0:T(8,128)S(1)}, f32[2,16,512]{2,1,0:T(8,128)S(1)}, u32[]{:S(2)}, u32[]{:S(2)}) collective-permute-start(f32[2,16,512]{2,1,0:T(8,128)S(1)} %get-tuple-element.17), channel_id=1, source_target_pairs={{0,8},{4,12},{8,0},{12,4},{16,24},{20,28},{24,16},{28,20},{1,9},{5... | collective-permute-start | bytes 196616 | tf_op jit(solution)/shard_map/cond/branch_1_fun/ppermute | solution.py:51
  9.8 2.8 %collective-permute-done.1.refs_1_ = f32[2,16,512]{2,1,0:T(8,128)S(1)} collective-permute-done((f32[2,16,512]{2,1,0:T(8,128)S(1)}, f32[2,16,512]{2,1,0:T(8,128)S(1)}, u32[]{:S(2)}, u32[]{:S(2)}) %collective-permute-start.1) | collective-permute-done | bytes 65568 | tf_op jit(solution)/shard_map/cond/branch_1_fun/ppermute | solution.py:51
  12.6 1.6 %collective-permute-start.2 = (f32[1,16,512]{2,1,0:T(8,128)S(1)}, f32[1,16,512]{2,1,0:T(8,128)S(1)}, u32[]{:S(2)}, u32[]{:S(2)}) collective-permute-start(f32[1,16,512]{2,1,0:T(8,128)S(1)} %get-tuple-element.19), channel_id=1, source_target_pairs={{0,16},{4,20},{8,24},{12,28},{16,0},{20,4},{24,8},{28,12},{1,17},{... | collective-permute-start | bytes 98312 | tf_op jit(solution)/shard_map/cond/branch_1_fun/ppermute | solution.py:51
  14.2 2.4 %collective-permute-done.2 = f32[1,16,512]{2,1,0:T(8,128)S(1)} collective-permute-done((f32[1,16,512]{2,1,0:T(8,128)S(1)}, f32[1,16,512]{2,1,0:T(8,128)S(1)}, u32[]{:S(2)}, u32[]{:S(2)}) %collective-permute-start.2) | collective-permute-done | bytes 32800 | tf_op jit(solution)/shard_map/cond/branch_1_fun/ppermute | solution.py:51
  16.6 4.0 %collective-permute-done.5.refs_0_ = f32[2,64,512]{2,1,0:T(8,128)S(1)} collective-permute-done((f32[2,64,512]{2,1,0:T(8,128)S(1)}, f32[2,64,512]{2,1,0:T(8,128)S(1)}, u32[]{:S(2)}, u32[]{:S(2)}) %collective-permute-start.5) | collective-permute-done | bytes 262176 | tf_op jit(solution)/shard_map/ppermute | solution.py:314
  20.6 0.4 shard_map.37
  21.0 0.1 collective-permute-start.6
  21.1 4.8 %collective-permute-done.3.refs_2_ = f32[2,64,512]{2,1,0:T(8,128)S(1)} collective-permute-done((f32[2,64,512]{2,1,0:T(8,128)S(1)}, f32[2,64,512]{2,1,0:T(8,128)S(1)}, u32[]{:S(2)}, u32[]{:S(2)}) %collective-permute-start.3) | collective-permute-done | bytes 262176 | tf_op jit(solution)/shard_map/ppermute | solution.py:314
  25.9 0.8 shard_map.38
  26.7 0.1 collective-permute-start.7
  26.8 1.7 %collective-permute-done.7.refs_3_ = f32[4,48,512]{2,1,0:T(8,128)S(1)} collective-permute-done((f32[4,48,512]{2,1,0:T(8,128)S(1)}, f32[4,48,512]{2,1,0:T(8,128)S(1)}, u32[]{:S(2)}, u32[]{:S(2)}) %collective-permute-start.7) | collective-permute-done | bytes 393248 | tf_op jit(solution)/shard_map/ppermute | solution.py:51
  28.5 0.1 shard_map.39
  28.6 1.6 %collective-permute-start.8 = (f32[1,64,512]{2,1,0:T(8,128)S(1)}, f32[1,64,512]{2,1,0:T(8,128)S(1)}, u32[]{:S(2)}, u32[]{:S(2)}) collective-permute-start(f32[1,64,512]{2,1,0:T(8,128)S(1)} %get-tuple-element.63), channel_id=1, source_target_pairs={{0,16},{4,20},{8,24},{12,28},{16,0},{20,4},{24,8},{28,12},{1,17},{... | collective-permute-start | bytes 393224 | tf_op jit(solution)/shard_map/ppermute | solution.py:51
  30.2 1.5 %collective-permute-start.9 = (f32[1,64,512]{2,1,0:T(8,128)S(1)}, f32[1,64,512]{2,1,0:T(8,128)S(1)}, u32[]{:S(2)}, u32[]{:S(2)}) collective-permute-start(f32[1,64,512]{2,1,0:T(8,128)S(1)} %get-tuple-element.64), channel_id=1, source_target_pairs={{0,8},{4,12},{8,0},{12,4},{16,24},{20,28},{24,16},{28,20},{1,9},{5... | collective-permute-start | bytes 393224 | tf_op jit(solution)/shard_map/ppermute | solution.py:51
  31.7 0.4 collective-permute-start.10
  32.1 2.0 %collective-permute-done.8.refs_2_ = f32[1,64,512]{2,1,0:T(8,128)S(1)} collective-permute-done((f32[1,64,512]{2,1,0:T(8,128)S(1)}, f32[1,64,512]{2,1,0:T(8,128)S(1)}, u32[]{:S(2)}, u32[]{:S(2)}) %collective-permute-start.8) | collective-permute-done | bytes 131104 | tf_op jit(solution)/shard_map/ppermute | solution.py:51
  34.2 2.4 %collective-permute-done.9.refs_3_ = f32[1,64,512]{2,1,0:T(8,128)S(1)} collective-permute-done((f32[1,64,512]{2,1,0:T(8,128)S(1)}, f32[1,64,512]{2,1,0:T(8,128)S(1)}, u32[]{:S(2)}, u32[]{:S(2)}) %collective-permute-start.9) | collective-permute-done | bytes 131104 | tf_op jit(solution)/shard_map/ppermute | solution.py:51
  36.6 1.6 %collective-permute-done.10.refs_4_ = f32[1,64,512]{2,1,0:T(8,128)S(1)} collective-permute-done((f32[1,64,512]{2,1,0:T(8,128)S(1)}, f32[1,64,512]{2,1,0:T(8,128)S(1)}, u32[]{:S(2)}, u32[]{:S(2)}) %collective-permute-start.10) | collective-permute-done | bytes 131104 | tf_op jit(solution)/shard_map/ppermute | solution.py:51
  38.2 0.0 copy-start
  38.2 0.1 collective-permute-start.11
  38.3 5.3 %collective-permute-done.11 = f32[1,80,512]{2,1,0:T(8,128)S(1)} collective-permute-done((f32[1,80,512]{2,1,0:T(8,128)S(1)}, f32[1,80,512]{2,1,0:T(8,128)S(1)}, u32[]{:S(2)}, u32[]{:S(2)}) %collective-permute-start.11) | collective-permute-done | bytes 163872 | tf_op jit(solution)/shard_map/ppermute | solution.py:251
  43.6 3.6 %collective-permute-start.12 = (f32[1,80,512]{2,1,0:T(8,128)S(1)}, f32[1,80,512]{2,1,0:T(8,128)S(1)}, u32[]{:S(2)}, u32[]{:S(2)}) collective-permute-start(f32[1,80,512]{2,1,0:T(8,128)S(1)} %add.60), channel_id=1, source_target_pairs={{0,2},{1,3},{2,0},{3,1},{4,5},{5,4},{6,7},{7,6},{8,10},{9,11},{10,... | collective-permute-start | bytes 491528 | tf_op jit(solution)/shard_map/ppermute | solution.py:251
  47.3 3.6 %collective-permute-done.12 = f32[1,80,512]{2,1,0:T(8,128)S(1)} collective-permute-done((f32[1,80,512]{2,1,0:T(8,128)S(1)}, f32[1,80,512]{2,1,0:T(8,128)S(1)}, u32[]{:S(2)}, u32[]{:S(2)}) %collective-permute-start.12) | collective-permute-done | bytes 163872 | tf_op jit(solution)/shard_map/ppermute | solution.py:251
  50.9 2.2 %collective-permute-start.15 = (f32[1,80,512]{2,1,0:T(8,128)S(1)}, f32[1,80,512]{2,1,0:T(8,128)S(1)}, u32[]{:S(2)}, u32[]{:S(2)}) collective-permute-start(f32[1,80,512]{2,1,0:T(8,128)S(1)} %add.61.refs_0_), channel_id=1, source_target_pairs={{0,24},{4,28},{8,16},{12,20},{16,8},{20,12},{24,0},{28,4},{1,25},{... | collective-permute-start | bytes 491528 | tf_op jit(solution)/shard_map/ppermute | solution.py:51
  53.1 0.5 collective-permute-start.14
  53.6 0.8 collective-permute-start.13
  54.4 2.7 %collective-permute-done.15.refs_3_ = f32[1,80,512]{2,1,0:T(8,128)S(1)} collective-permute-done((f32[1,80,512]{2,1,0:T(8,128)S(1)}, f32[1,80,512]{2,1,0:T(8,128)S(1)}, u32[]{:S(2)}, u32[]{:S(2)}) %collective-permute-start.15) | collective-permute-done | bytes 163872 | tf_op jit(solution)/shard_map/ppermute | solution.py:51
  57.2 1.5 %collective-permute-done.14.refs_2_ = f32[1,80,512]{2,1,0:T(8,128)S(1)} collective-permute-done((f32[1,80,512]{2,1,0:T(8,128)S(1)}, f32[1,80,512]{2,1,0:T(8,128)S(1)}, u32[]{:S(2)}, u32[]{:S(2)}) %collective-permute-start.14) | collective-permute-done | bytes 163872 | tf_op jit(solution)/shard_map/ppermute | solution.py:51
  58.7 0.3 collective-permute-done.13.refs_1_
  58.9 0.2 collective-permute-start.17
  59.2 0.9 collective-permute-done.18.refs_6_
  60.1 0.3 collective-permute-done.17.refs_5_
  60.3 2.1 %shard_map.41 = (f32[512,128]{1,0:T(8,128)S(1)}, f32[512,128]{1,0:T(8,128)S(1)}, f32[512,128]{1,0:T(8,128)S(1)}, f32[512,128]{1,0:T(8,128)S(1)}) custom-call(f32[1,80,512]{2,1,0:T(8,128)S(1)} %add.61.refs_0_, f32[1,80,512]{2,1,0:T(8,128)S(1)} %collective-permute-done.13.refs_1_, f32[1,80,512]{2,1,0:T(8,128)S(1)} %collective-permute-done.14.refs_2_, ...), custom_call_target="tpu_custom_call" | custom-call | tf_op jit(solution)/shard_map/pallas_call | solution.py:39
  62.5 0.9 collective-permute-start.20
  63.3 2.6 %collective-permute-start.21 = (f32[512,128]{1,0:T(8,128)S(1)}, f32[512,128]{1,0:T(8,128)S(1)}, u32[]{:S(2)}, u32[]{:S(2)}) collective-permute-start(f32[512,128]{1,0:T(8,128)S(1)} %get-tuple-element.70), channel_id=1, source_target_pairs={{0,2},{1,3},{2,1},{3,0},{4,6},{5,7},{6,5},{7,4},{8,10},{9,11},{10,... | collective-permute-start | bytes 786440 | tf_op jit(solution)/shard_map/ppermute | solution.py:386
  66.0 1.4 %collective-permute-start.22 = (f32[512,128]{1,0:T(8,128)S(1)}, f32[512,128]{1,0:T(8,128)S(1)}, u32[]{:S(2)}, u32[]{:S(2)}) collective-permute-start(f32[512,128]{1,0:T(8,128)S(1)} %get-tuple-element.71), channel_id=1, source_target_pairs={{0,1},{1,0},{2,3},{3,2},{4,5},{5,4},{6,7},{7,6},{8,9},{9,8},{10,11... | collective-permute-start | bytes 786440 | tf_op jit(solution)/shard_map/ppermute | solution.py:386
  67.4 13.9 %collective-permute-done.20.refs_1_ = f32[512,128]{1,0:T(8,128)S(1)} collective-permute-done((f32[512,128]{1,0:T(8,128)S(1)}, f32[512,128]{1,0:T(8,128)S(1)}, u32[]{:S(2)}, u32[]{:S(2)}) %collective-permute-start.20) | collective-permute-done | bytes 262176 | tf_op jit(solution)/shard_map/ppermute | solution.py:386
  81.2 5.7 %collective-permute-done.21.refs_2_ = f32[512,128]{1,0:T(8,128)S(1)} collective-permute-done((f32[512,128]{1,0:T(8,128)S(1)}, f32[512,128]{1,0:T(8,128)S(1)}, u32[]{:S(2)}, u32[]{:S(2)}) %collective-permute-start.21) | collective-permute-done | bytes 262176 | tf_op jit(solution)/shard_map/ppermute | solution.py:386
  86.9 1.0 %shard_map.42 = f32[4,512,128]{2,1,0:T(8,128)} custom-call(f32[512,128]{1,0:T(8,128)S(1)} %get-tuple-element.68.refs_0_, f32[512,128]{1,0:T(8,128)S(1)} %collective-permute-done.20.refs_1_, f32[512,128]{1,0:T(8,128)S(1)} %collective-permute-done.21.refs_2_, f32[512,128]{1,0:T(8,128)S(1)} %collective-permute-done.22.refs_3_), custom_call_target="tpu_custom_call" | custom-call | tf_op jit(solution)/shard_map/pallas_call | solution.py:388
  (17 shorter events, 0.1 us)
Async XLA Ops:
  0.0 6.5 %copy-start.1 = (f32[512,512]{1,0:T(8,128)S(1)}, f32[512,512]{1,0:T(8,128)}, u32[]{:S(2)}) copy-start(f32[512,512]{1,0:T(8,128)} %refs_11_.1) | copy-start | bytes 3145732
  1.1 19.6 %collective-permute-start.5 = (f32[2,64,512]{2,1,0:T(8,128)S(1)}, f32[2,64,512]{2,1,0:T(8,128)S(1)}, u32[]{:S(2)}, u32[]{:S(2)}) collective-permute-start(f32[2,64,512]{2,1,0:T(8,128)S(1)} %dynamic-slice_bitcast_fusion), channel_id=1, source_target_pairs={{0,3},{1,2},{2,0},{3,1},{4,7},{5,6},{6,4},{7,5},{8,11},{9,10},{10,... | collective-permute-start | bytes 786440 | tf_op jit(solution)/shard_map/ppermute | solution.py:314
  3.9 22.0 %collective-permute-start.3 = (f32[2,64,512]{2,1,0:T(8,128)S(1)}, f32[2,64,512]{2,1,0:T(8,128)S(1)}, u32[]{:S(2)}, u32[]{:S(2)}) collective-permute-start(f32[2,64,512]{2,1,0:T(8,128)S(1)} %get-tuple-element.47), channel_id=1, source_target_pairs={{0,2},{1,3},{2,1},{3,0},{4,6},{5,7},{6,5},{7,4},{8,10},{9,11},{10,... | collective-permute-start | bytes 786440 | tf_op jit(solution)/shard_map/ppermute | solution.py:314
  5.3 20.6 %collective-permute-start.4 = (f32[2,64,512]{2,1,0:T(8,128)S(1)}, f32[2,64,512]{2,1,0:T(8,128)S(1)}, u32[]{:S(2)}, u32[]{:S(2)}) collective-permute-start(f32[2,64,512]{2,1,0:T(8,128)S(1)} %get-tuple-element.48), channel_id=1, source_target_pairs={{0,1},{1,0},{2,3},{3,2},{4,5},{5,4},{6,7},{7,6},{8,9},{9,8},{10,11... | collective-permute-start | bytes 786440 | tf_op jit(solution)/shard_map/ppermute | solution.py:314
  6.9 1.4 %collective-permute-start = (f32[4,16,512]{2,1,0:T(8,128)S(1)}, f32[4,16,512]{2,1,0:T(8,128)S(1)}, u32[]{:S(2)}, u32[]{:S(2)}) collective-permute-start(f32[4,16,512]{2,1,0:T(8,128)S(1)} %get-tuple-element.15), channel_id=1, source_target_pairs={{0,4},{4,0},{8,12},{12,8},{16,20},{20,16},{24,28},{28,24},{1,5},{5... | collective-permute-start | bytes 393224 | tf_op jit(solution)/shard_map/cond/branch_1_fun/ppermute | solution.py:51
  8.3 4.3 %collective-permute-start.1 = (f32[2,16,512]{2,1,0:T(8,128)S(1)}, f32[2,16,512]{2,1,0:T(8,128)S(1)}, u32[]{:S(2)}, u32[]{:S(2)}) collective-permute-start(f32[2,16,512]{2,1,0:T(8,128)S(1)} %get-tuple-element.17), channel_id=1, source_target_pairs={{0,8},{4,12},{8,0},{12,4},{16,24},{20,28},{24,16},{28,20},{1,9},{5... | collective-permute-start | bytes 196616 | tf_op jit(solution)/shard_map/cond/branch_1_fun/ppermute | solution.py:51
  12.6 4.0 %collective-permute-start.2 = (f32[1,16,512]{2,1,0:T(8,128)S(1)}, f32[1,16,512]{2,1,0:T(8,128)S(1)}, u32[]{:S(2)}, u32[]{:S(2)}) collective-permute-start(f32[1,16,512]{2,1,0:T(8,128)S(1)} %get-tuple-element.19), channel_id=1, source_target_pairs={{0,16},{4,20},{8,24},{12,28},{16,0},{20,4},{24,8},{28,12},{1,17},{... | collective-permute-start | bytes 98312 | tf_op jit(solution)/shard_map/cond/branch_1_fun/ppermute | solution.py:51
  21.0 4.9 %collective-permute-start.6 = (f32[4,16,512]{2,1,0:T(8,128)S(1)}, f32[4,16,512]{2,1,0:T(8,128)S(1)}, u32[]{:S(2)}, u32[]{:S(2)}) collective-permute-start(f32[4,16,512]{2,1,0:T(8,128)S(1)} %get-tuple-element.54), channel_id=1, source_target_pairs={{0,4},{4,0},{8,12},{12,8},{16,20},{20,16},{24,28},{28,24},{1,5},{5... | collective-permute-start | bytes 393224 | tf_op jit(solution)/shard_map/ppermute | solution.py:51
  26.7 1.8 %collective-permute-start.7 = (f32[4,48,512]{2,1,0:T(8,128)S(1)}, f32[4,48,512]{2,1,0:T(8,128)S(1)}, u32[]{:S(2)}, u32[]{:S(2)}) collective-permute-start(f32[4,48,512]{2,1,0:T(8,128)S(1)} %get-tuple-element.61), channel_id=1, source_target_pairs={{0,4},{4,0},{8,12},{12,8},{16,20},{20,16},{24,28},{28,24},{1,5},{5... | collective-permute-start | bytes 1179656 | tf_op jit(solution)/shard_map/ppermute | solution.py:51
  28.6 5.6 %collective-permute-start.8 = (f32[1,64,512]{2,1,0:T(8,128)S(1)}, f32[1,64,512]{2,1,0:T(8,128)S(1)}, u32[]{:S(2)}, u32[]{:S(2)}) collective-permute-start(f32[1,64,512]{2,1,0:T(8,128)S(1)} %get-tuple-element.63), channel_id=1, source_target_pairs={{0,16},{4,20},{8,24},{12,28},{16,0},{20,4},{24,8},{28,12},{1,17},{... | collective-permute-start | bytes 393224 | tf_op jit(solution)/shard_map/ppermute | solution.py:51
  30.2 6.4 %collective-permute-start.9 = (f32[1,64,512]{2,1,0:T(8,128)S(1)}, f32[1,64,512]{2,1,0:T(8,128)S(1)}, u32[]{:S(2)}, u32[]{:S(2)}) collective-permute-start(f32[1,64,512]{2,1,0:T(8,128)S(1)} %get-tuple-element.64), channel_id=1, source_target_pairs={{0,8},{4,12},{8,0},{12,4},{16,24},{20,28},{24,16},{28,20},{1,9},{5... | collective-permute-start | bytes 393224 | tf_op jit(solution)/shard_map/ppermute | solution.py:51
  31.7 6.5 %collective-permute-start.10 = (f32[1,64,512]{2,1,0:T(8,128)S(1)}, f32[1,64,512]{2,1,0:T(8,128)S(1)}, u32[]{:S(2)}, u32[]{:S(2)}) collective-permute-start(f32[1,64,512]{2,1,0:T(8,128)S(1)} %get-tuple-element.65), channel_id=1, source_target_pairs={{0,24},{4,28},{8,16},{12,20},{16,8},{20,12},{24,0},{28,4},{1,25},{... | collective-permute-start | bytes 393224 | tf_op jit(solution)/shard_map/ppermute | solution.py:51
  38.2 22.1 %copy-start = (f32[2,256,256]{2,1,0:T(8,128)S(1)}, f32[2,256,256]{2,1,0:T(8,128)}, u32[]{:S(2)}) copy-start(f32[2,256,256]{2,1,0:T(8,128)} %refs_8_.1) | copy-start | bytes 1572868
  38.2 5.4 %collective-permute-start.11 = (f32[1,80,512]{2,1,0:T(8,128)S(1)}, f32[1,80,512]{2,1,0:T(8,128)S(1)}, u32[]{:S(2)}, u32[]{:S(2)}) collective-permute-start(f32[1,80,512]{2,1,0:T(8,128)S(1)} %shard_map.40), channel_id=1, source_target_pairs={{0,1},{1,0},{2,3},{3,2},{4,6},{5,7},{6,4},{7,5},{8,9},{9,8},{10,11... | collective-permute-start | bytes 491528 | tf_op jit(solution)/shard_map/ppermute | solution.py:251
  43.6 7.2 %collective-permute-start.12 = (f32[1,80,512]{2,1,0:T(8,128)S(1)}, f32[1,80,512]{2,1,0:T(8,128)S(1)}, u32[]{:S(2)}, u32[]{:S(2)}) collective-permute-start(f32[1,80,512]{2,1,0:T(8,128)S(1)} %add.60), channel_id=1, source_target_pairs={{0,2},{1,3},{2,0},{3,1},{4,5},{5,4},{6,7},{7,6},{8,10},{9,11},{10,... | collective-permute-start | bytes 491528 | tf_op jit(solution)/shard_map/ppermute | solution.py:251
  50.9 6.3 %collective-permute-start.15 = (f32[1,80,512]{2,1,0:T(8,128)S(1)}, f32[1,80,512]{2,1,0:T(8,128)S(1)}, u32[]{:S(2)}, u32[]{:S(2)}) collective-permute-start(f32[1,80,512]{2,1,0:T(8,128)S(1)} %add.61.refs_0_), channel_id=1, source_target_pairs={{0,24},{4,28},{8,16},{12,20},{16,8},{20,12},{24,0},{28,4},{1,25},{... | collective-permute-start | bytes 491528 | tf_op jit(solution)/shard_map/ppermute | solution.py:51
  53.1 5.6 %collective-permute-start.14 = (f32[1,80,512]{2,1,0:T(8,128)S(1)}, f32[1,80,512]{2,1,0:T(8,128)S(1)}, u32[]{:S(2)}, u32[]{:S(2)}) collective-permute-start(f32[1,80,512]{2,1,0:T(8,128)S(1)} %add.61.refs_0_), channel_id=1, source_target_pairs={{0,8},{4,12},{8,0},{12,4},{16,24},{20,28},{24,16},{28,20},{1,9},{5... | collective-permute-start | bytes 491528 | tf_op jit(solution)/shard_map/ppermute | solution.py:51
  53.6 5.3 %collective-permute-start.13 = (f32[1,80,512]{2,1,0:T(8,128)S(1)}, f32[1,80,512]{2,1,0:T(8,128)S(1)}, u32[]{:S(2)}, u32[]{:S(2)}) collective-permute-start(f32[1,80,512]{2,1,0:T(8,128)S(1)} %add.61.refs_0_), channel_id=1, source_target_pairs={{0,16},{4,20},{8,24},{12,28},{16,0},{20,4},{24,8},{28,12},{1,17},{... | collective-permute-start | bytes 491528 | tf_op jit(solution)/shard_map/ppermute | solution.py:51
  54.4 4.7 %collective-permute-start.16 = (f32[1,80,512]{2,1,0:T(8,128)S(1)}, f32[1,80,512]{2,1,0:T(8,128)S(1)}, u32[]{:S(2)}, u32[]{:S(2)}) collective-permute-start(f32[1,80,512]{2,1,0:T(8,128)S(1)} %add.61.refs_0_), channel_id=1, source_target_pairs={{0,4},{4,0},{8,12},{12,8},{16,20},{20,16},{24,28},{28,24},{1,5},{5... | collective-permute-start | bytes 491528 | tf_op jit(solution)/shard_map/ppermute | solution.py:51
  57.2 2.0 %collective-permute-start.19 = (f32[1,80,512]{2,1,0:T(8,128)S(1)}, f32[1,80,512]{2,1,0:T(8,128)S(1)}, u32[]{:S(2)}, u32[]{:S(2)}) collective-permute-start(f32[1,80,512]{2,1,0:T(8,128)S(1)} %collective-permute-done.15.refs_3_), channel_id=1, source_target_pairs={{0,4},{4,0},{8,12},{12,8},{16,20},{20,16},{24,28},{28,24},{1,5},{5... | collective-permute-start | bytes 491528 | tf_op jit(solution)/shard_map/ppermute | solution.py:51
  58.7 1.4 %collective-permute-start.18 = (f32[1,80,512]{2,1,0:T(8,128)S(1)}, f32[1,80,512]{2,1,0:T(8,128)S(1)}, u32[]{:S(2)}, u32[]{:S(2)}) collective-permute-start(f32[1,80,512]{2,1,0:T(8,128)S(1)} %collective-permute-done.14.refs_2_), channel_id=1, source_target_pairs={{0,4},{4,0},{8,12},{12,8},{16,20},{20,16},{24,28},{28,24},{1,5},{5... | collective-permute-start | bytes 491528 | tf_op jit(solution)/shard_map/ppermute | solution.py:51
  58.9 1.4 %collective-permute-start.17 = (f32[1,80,512]{2,1,0:T(8,128)S(1)}, f32[1,80,512]{2,1,0:T(8,128)S(1)}, u32[]{:S(2)}, u32[]{:S(2)}) collective-permute-start(f32[1,80,512]{2,1,0:T(8,128)S(1)} %collective-permute-done.13.refs_1_), channel_id=1, source_target_pairs={{0,4},{4,0},{8,12},{12,8},{16,20},{20,16},{24,28},{28,24},{1,5},{5... | collective-permute-start | bytes 491528 | tf_op jit(solution)/shard_map/ppermute | solution.py:51
  62.5 18.7 %collective-permute-start.20 = (f32[512,128]{1,0:T(8,128)S(1)}, f32[512,128]{1,0:T(8,128)S(1)}, u32[]{:S(2)}, u32[]{:S(2)}) collective-permute-start(f32[512,128]{1,0:T(8,128)S(1)} %get-tuple-element.69), channel_id=1, source_target_pairs={{0,3},{1,2},{2,0},{3,1},{4,7},{5,6},{6,4},{7,5},{8,11},{9,10},{10,... | collective-permute-start | bytes 786440 | tf_op jit(solution)/shard_map/ppermute | solution.py:386
  63.3 23.6 %collective-permute-start.21 = (f32[512,128]{1,0:T(8,128)S(1)}, f32[512,128]{1,0:T(8,128)S(1)}, u32[]{:S(2)}, u32[]{:S(2)}) collective-permute-start(f32[512,128]{1,0:T(8,128)S(1)} %get-tuple-element.70), channel_id=1, source_target_pairs={{0,2},{1,3},{2,1},{3,0},{4,6},{5,7},{6,5},{7,4},{8,10},{9,11},{10,... | collective-permute-start | bytes 786440 | tf_op jit(solution)/shard_map/ppermute | solution.py:386
  66.0 21.0 %collective-permute-start.22 = (f32[512,128]{1,0:T(8,128)S(1)}, f32[512,128]{1,0:T(8,128)S(1)}, u32[]{:S(2)}, u32[]{:S(2)}) collective-permute-start(f32[512,128]{1,0:T(8,128)S(1)} %get-tuple-element.71), channel_id=1, source_target_pairs={{0,1},{1,0},{2,3},{3,2},{4,5},{5,4},{6,7},{7,6},{8,9},{9,8},{10,11... | collective-permute-start | bytes 786440 | tf_op jit(solution)/shard_map/ppermute | solution.py:386

commit v8 on v6

--- a/solution.py
+++ b/solution.py
@@ -183,6 +183,10 @@
     out[0, groups * count :] = total[len(order) * count :]
 
 
+def add_kernel(left, right, out):
+    out[...] = left[...] + right[...]
+
+
 def assemble_kernel(shift, group, *refs):
     place, blocks, out = here(), refs[:-1], refs[-1]
     me = (place[1] >> shift) & (group - 1)
@@ -244,7 +248,7 @@
         other = lax.ppermute(part, ("row", "col"), pairs)
         if step == bits - 1:
             return part, other
-        part = part + other
+        (part,) = kernel_call(add_kernel, [part.shape], part, other)
 
 
 def make_per_device(rows_size, cols_size):
@@ -367,7 +371,7 @@
                 tail_kernel, cols_size, groups, stages[1][0], [0] + exchange_order(stages[1][1])
             ),
             [(local_rows, out_cols)] * cols_size,
-            *gather(part + other),
+            *gather(kernel_call(add_kernel, [part.shape], part, other)[0]),
             tfactors,
             *house,
             vectors,

time: 88.1 us -> 88.1 us (level)
    pallas_call x8 -> x10, Pallas kernels: 3.9 us -> 3.94 us  [kernel_call(): pl.pallas_call(body, out_shape=[jax.ShapeDtypeStruct(shape, jnp.float32)...]
where the time goes in v8:
time: 88.1 us; the launch traced here: 87.9 us
  waiting for transfers between devices  57.1 us (65%)
  starting transfers between devices  23.6 us (27%)
  Pallas kernels  4.93 us (6%)
  local copies, waits for them, and re-layouts  2.23 us (3%)
    ppermute x15, waiting for transfers between devices, swap(): return lax.ppermute(block, axis, [(i, i ^ mask) for i in range(size)])  19.9 us
    ppermute x3, waiting for transfers between devices, per_device(): blocks[k] = lax.ppermute(blocks[k], 'col', pairs)  19.6 us
    ppermute x15, starting transfers between devices, swap(): return lax.ppermute(block, axis, [(i, i ^ mask) for i in range(size)])  10.7 us
    ppermute x2, waiting for transfers between devices, all_reduce_cols(): other = lax.ppermute(part, ('row', 'col'), pairs)  8.88 us
    ppermute x3, waiting for transfers between devices, per_device(): pieces[k] = lax.ppermute(cut, 'col', pairs) if k else cut  8.74 us
    ppermute x3, starting transfers between devices, per_device(): blocks[k] = lax.ppermute(blocks[k], 'col', pairs)  4.9 us
    ppermute x3, starting transfers between devices, per_device(): pieces[k] = lax.ppermute(cut, 'col', pairs) if k else cut  4.23 us
    pallas_call x10, Pallas kernels, kernel_call(): pl.pallas_call(body, out_shape=[jax.ShapeDtypeStruct(shape, jnp.float32)...  3.94 us
  transfers between devices with their start and end apart: 23, of which 18 were waited for; matrix products, arithmetic and copies ran while one was open for 1% of the time, Pallas kernels for 1%

profile of v8, /device:TPU:8, one launch (start us, length us, event | category | flops | bytes accessed | tf_op | source)
XLA Modules:
  0.0 87.9 jit_solution(2979662783010220179)
XLA Ops:
  0.0 1.1 %dynamic-slice_bitcast_fusion = f32[2,64,512]{2,1,0:T(8,128)S(1)} fusion(f32[2,2048,64]{1,2,0:T(8,128)} %param.6, s32[]{:T(128)S(6)} %select_n.12), kind=kLoop, calls=%fused_computation | loop fusion | bytes 524292 | tf_op jit(solution)/shard_map/dynamic_slice | solution.py:307
  1.1 1.6 %collective-permute-start.5 = (f32[2,64,512]{2,1,0:T(8,128)S(1)}, f32[2,64,512]{2,1,0:T(8,128)S(1)}, u32[]{:S(2)}, u32[]{:S(2)}) collective-permute-start(f32[2,64,512]{2,1,0:T(8,128)S(1)} %dynamic-slice_bitcast_fusion), channel_id=1, source_target_pairs={{0,3},{1,2},{2,0},{3,1},{4,7},{5,6},{6,4},{7,5},{8,11},{9,10},{10,... | collective-permute-start | bytes 786440 | tf_op jit(solution)/shard_map/ppermute | solution.py:311
  2.7 1.2 %constant_dynamic-slice_fusion = (f32[2,64,512]{2,1,0:T(8,128)S(1)}, f32[2,64,512]{2,1,0:T(8,128)S(1)}, f32[2,64,512]{2,1,0:T(8,128)S(1)}) fusion(f32[2,64,2048]{2,1,0:T(8,128)} %bitcast.4, s32[]{:T(128)S(6)} %select_n.15, s32[]{:T(128)S(6)} %select_n.14, s32[]{:T(128)S(6)} %select_n.13), kind=kLoop, calls=%fused_computation.1 | loop fusion | bytes 1572876 | tf_op jit(solution)/shard_map/dynamic_slice | solution.py:307
  3.9 1.4 %collective-permute-start.3 = (f32[2,64,512]{2,1,0:T(8,128)S(1)}, f32[2,64,512]{2,1,0:T(8,128)S(1)}, u32[]{:S(2)}, u32[]{:S(2)}) collective-permute-start(f32[2,64,512]{2,1,0:T(8,128)S(1)} %get-tuple-element.47), channel_id=1, source_target_pairs={{0,2},{1,3},{2,1},{3,0},{4,6},{5,7},{6,5},{7,4},{8,10},{9,11},{10,... | collective-permute-start | bytes 786440 | tf_op jit(solution)/shard_map/ppermute | solution.py:311
  5.3 1.2 %collective-permute-start.4 = (f32[2,64,512]{2,1,0:T(8,128)S(1)}, f32[2,64,512]{2,1,0:T(8,128)S(1)}, u32[]{:S(2)}, u32[]{:S(2)}) collective-permute-start(f32[2,64,512]{2,1,0:T(8,128)S(1)} %get-tuple-element.48), channel_id=1, source_target_pairs={{0,1},{1,0},{2,3},{3,2},{4,5},{5,4},{6,7},{7,6},{8,9},{9,8},{10,11... | collective-permute-start | bytes 786440 | tf_op jit(solution)/shard_map/ppermute | solution.py:311
  6.5 10.2 %conditional.1 = (f32[1,16,512]{2,1,0:T(8,128)S(1)}) conditional(s32[]{:T(128)} %convert_element_type.3, () %tuple.17, (f32[2,64,512]{2,1,0:T(8,128)S(1)}, f32[512,512]{1,0:T(8,128)S(1)}) %tuple.25), branch_computations={%region_0.0_spmd, %region_1.0_spmd} | conditional | flops 8192 | bytes 1015936 | solution.py:325
  6.5 0.4 branch_1_fun.3
  6.9 0.1 collective-permute-start
  7.0 1.3 %collective-permute-done.refs_1_ = f32[4,16,512]{2,1,0:T(8,128)S(1)} collective-permute-done((f32[4,16,512]{2,1,0:T(8,128)S(1)}, f32[4,16,512]{2,1,0:T(8,128)S(1)}, u32[]{:S(2)}, u32[]{:S(2)}) %collective-permute-start) | collective-permute-done | bytes 131104 | tf_op jit(solution)/shard_map/cond/branch_1_fun/ppermute | solution.py:44
  8.3 1.6 %collective-permute-start.1 = (f32[2,16,512]{2,1,0:T(8,128)S(1)}, f32[2,16,512]{2,1,0:T(8,128)S(1)}, u32[]{:S(2)}, u32[]{:S(2)}) collective-permute-start(f32[2,16,512]{2,1,0:T(8,128)S(1)} %get-tuple-element.17), channel_id=1, source_target_pairs={{0,8},{4,12},{8,0},{12,4},{16,24},{20,28},{24,16},{28,20},{1,9},{5... | collective-permute-start | bytes 196616 | tf_op jit(solution)/shard_map/cond/branch_1_fun/ppermute | solution.py:44
  9.9 2.8 %collective-permute-done.1.refs_1_ = f32[2,16,512]{2,1,0:T(8,128)S(1)} collective-permute-done((f32[2,16,512]{2,1,0:T(8,128)S(1)}, f32[2,16,512]{2,1,0:T(8,128)S(1)}, u32[]{:S(2)}, u32[]{:S(2)}) %collective-permute-start.1) | collective-permute-done | bytes 65568 | tf_op jit(solution)/shard_map/cond/branch_1_fun/ppermute | solution.py:44
  12.7 1.6 %collective-permute-start.2 = (f32[1,16,512]{2,1,0:T(8,128)S(1)}, f32[1,16,512]{2,1,0:T(8,128)S(1)}, u32[]{:S(2)}, u32[]{:S(2)}) collective-permute-start(f32[1,16,512]{2,1,0:T(8,128)S(1)} %get-tuple-element.19), channel_id=1, source_target_pairs={{0,16},{4,20},{8,24},{12,28},{16,0},{20,4},{24,8},{28,12},{1,17},{... | collective-permute-start | bytes 98312 | tf_op jit(solution)/shard_map/cond/branch_1_fun/ppermute | solution.py:44
  14.3 2.4 %collective-permute-done.2 = f32[1,16,512]{2,1,0:T(8,128)S(1)} collective-permute-done((f32[1,16,512]{2,1,0:T(8,128)S(1)}, f32[1,16,512]{2,1,0:T(8,128)S(1)}, u32[]{:S(2)}, u32[]{:S(2)}) %collective-permute-start.2) | collective-permute-done | bytes 32800 | tf_op jit(solution)/shard_map/cond/branch_1_fun/ppermute | solution.py:44
  16.7 4.0 %collective-permute-done.5.refs_0_ = f32[2,64,512]{2,1,0:T(8,128)S(1)} collective-permute-done((f32[2,64,512]{2,1,0:T(8,128)S(1)}, f32[2,64,512]{2,1,0:T(8,128)S(1)}, u32[]{:S(2)}, u32[]{:S(2)}) %collective-permute-start.5) | collective-permute-done | bytes 262176 | tf_op jit(solution)/shard_map/ppermute | solution.py:311
  20.6 0.4 shard_map.37
  21.1 0.1 collective-permute-start.6
  21.1 4.8 %collective-permute-done.3.refs_2_ = f32[2,64,512]{2,1,0:T(8,128)S(1)} collective-permute-done((f32[2,64,512]{2,1,0:T(8,128)S(1)}, f32[2,64,512]{2,1,0:T(8,128)S(1)}, u32[]{:S(2)}, u32[]{:S(2)}) %collective-permute-start.3) | collective-permute-done | bytes 262176 | tf_op jit(solution)/shard_map/ppermute | solution.py:311
  25.9 0.8 shard_map.38
  26.7 0.1 collective-permute-start.7
  26.8 1.7 %collective-permute-done.7.refs_3_ = f32[4,48,512]{2,1,0:T(8,128)S(1)} collective-permute-done((f32[4,48,512]{2,1,0:T(8,128)S(1)}, f32[4,48,512]{2,1,0:T(8,128)S(1)}, u32[]{:S(2)}, u32[]{:S(2)}) %collective-permute-start.7) | collective-permute-done | bytes 393248 | tf_op jit(solution)/shard_map/ppermute | solution.py:44
  28.5 0.1 shard_map.39
  28.6 1.6 %collective-permute-start.8 = (f32[1,64,512]{2,1,0:T(8,128)S(1)}, f32[1,64,512]{2,1,0:T(8,128)S(1)}, u32[]{:S(2)}, u32[]{:S(2)}) collective-permute-start(f32[1,64,512]{2,1,0:T(8,128)S(1)} %get-tuple-element.63), channel_id=1, source_target_pairs={{0,16},{4,20},{8,24},{12,28},{16,0},{20,4},{24,8},{28,12},{1,17},{... | collective-permute-start | bytes 393224 | tf_op jit(solution)/shard_map/ppermute | solution.py:44
  30.2 1.5 %collective-permute-start.9 = (f32[1,64,512]{2,1,0:T(8,128)S(1)}, f32[1,64,512]{2,1,0:T(8,128)S(1)}, u32[]{:S(2)}, u32[]{:S(2)}) collective-permute-start(f32[1,64,512]{2,1,0:T(8,128)S(1)} %get-tuple-element.64), channel_id=1, source_target_pairs={{0,8},{4,12},{8,0},{12,4},{16,24},{20,28},{24,16},{28,20},{1,9},{5... | collective-permute-start | bytes 393224 | tf_op jit(solution)/shard_map/ppermute | solution.py:44
  31.7 0.4 collective-permute-start.10
  32.1 2.0 %collective-permute-done.8.refs_2_ = f32[1,64,512]{2,1,0:T(8,128)S(1)} collective-permute-done((f32[1,64,512]{2,1,0:T(8,128)S(1)}, f32[1,64,512]{2,1,0:T(8,128)S(1)}, u32[]{:S(2)}, u32[]{:S(2)}) %collective-permute-start.8) | collective-permute-done | bytes 131104 | tf_op jit(solution)/shard_map/ppermute | solution.py:44
  34.2 2.4 %collective-permute-done.9.refs_3_ = f32[1,64,512]{2,1,0:T(8,128)S(1)} collective-permute-done((f32[1,64,512]{2,1,0:T(8,128)S(1)}, f32[1,64,512]{2,1,0:T(8,128)S(1)}, u32[]{:S(2)}, u32[]{:S(2)}) %collective-permute-start.9) | collective-permute-done | bytes 131104 | tf_op jit(solution)/shard_map/ppermute | solution.py:44
  36.6 1.6 %collective-permute-done.10.refs_4_ = f32[1,64,512]{2,1,0:T(8,128)S(1)} collective-permute-done((f32[1,64,512]{2,1,0:T(8,128)S(1)}, f32[1,64,512]{2,1,0:T(8,128)S(1)}, u32[]{:S(2)}, u32[]{:S(2)}) %collective-permute-start.10) | collective-permute-done | bytes 131104 | tf_op jit(solution)/shard_map/ppermute | solution.py:44
  38.2 0.0 copy-start
  38.2 0.1 collective-permute-start.11
  38.3 5.3 %collective-permute-done.11.right = f32[1,80,512]{2,1,0:T(8,128)S(1)} collective-permute-done((f32[1,80,512]{2,1,0:T(8,128)S(1)}, f32[1,80,512]{2,1,0:T(8,128)S(1)}, u32[]{:S(2)}, u32[]{:S(2)}) %collective-permute-start.11) | collective-permute-done | bytes 163872 | tf_op jit(solution)/shard_map/ppermute | solution.py:248
  43.6 3.6 %collective-permute-start.12 = (f32[1,80,512]{2,1,0:T(8,128)S(1)}, f32[1,80,512]{2,1,0:T(8,128)S(1)}, u32[]{:S(2)}, u32[]{:S(2)}) collective-permute-start(f32[1,80,512]{2,1,0:T(8,128)S(1)} %shard_map.41.left), channel_id=1, source_target_pairs={{0,2},{1,3},{2,0},{3,1},{4,5},{5,4},{6,7},{7,6},{8,10},{9,11},{10,... | collective-permute-start | bytes 491528 | tf_op jit(solution)/shard_map/ppermute | solution.py:248
  47.3 3.6 %collective-permute-done.12.right = f32[1,80,512]{2,1,0:T(8,128)S(1)} collective-permute-done((f32[1,80,512]{2,1,0:T(8,128)S(1)}, f32[1,80,512]{2,1,0:T(8,128)S(1)}, u32[]{:S(2)}, u32[]{:S(2)}) %collective-permute-start.12) | collective-permute-done | bytes 163872 | tf_op jit(solution)/shard_map/ppermute | solution.py:248
  50.9 2.2 %collective-permute-start.15 = (f32[1,80,512]{2,1,0:T(8,128)S(1)}, f32[1,80,512]{2,1,0:T(8,128)S(1)}, u32[]{:S(2)}, u32[]{:S(2)}) collective-permute-start(f32[1,80,512]{2,1,0:T(8,128)S(1)} %shard_map.42.refs_0_), channel_id=1, source_target_pairs={{0,24},{4,28},{8,16},{12,20},{16,8},{20,12},{24,0},{28,4},{1,25},{... | collective-permute-start | bytes 491528 | tf_op jit(solution)/shard_map/ppermute | solution.py:44
  53.1 0.5 collective-permute-start.14
  53.6 0.8 collective-permute-start.13
  54.4 2.7 %collective-permute-done.15.refs_3_ = f32[1,80,512]{2,1,0:T(8,128)S(1)} collective-permute-done((f32[1,80,512]{2,1,0:T(8,128)S(1)}, f32[1,80,512]{2,1,0:T(8,128)S(1)}, u32[]{:S(2)}, u32[]{:S(2)}) %collective-permute-start.15) | collective-permute-done | bytes 163872 | tf_op jit(solution)/shard_map/ppermute | solution.py:44
  57.2 1.5 %collective-permute-done.14.refs_2_ = f32[1,80,512]{2,1,0:T(8,128)S(1)} collective-permute-done((f32[1,80,512]{2,1,0:T(8,128)S(1)}, f32[1,80,512]{2,1,0:T(8,128)S(1)}, u32[]{:S(2)}, u32[]{:S(2)}) %collective-permute-start.14) | collective-permute-done | bytes 163872 | tf_op jit(solution)/shard_map/ppermute | solution.py:44
  58.7 0.3 collective-permute-done.13.refs_1_
  58.9 0.2 collective-permute-start.17
  59.2 0.9 collective-permute-done.18.refs_6_
  60.0 0.3 collective-permute-done.17.refs_5_
  60.3 2.1 %shard_map.43 = (f32[512,128]{1,0:T(8,128)S(1)}, f32[512,128]{1,0:T(8,128)S(1)}, f32[512,128]{1,0:T(8,128)S(1)}, f32[512,128]{1,0:T(8,128)S(1)}) custom-call(f32[1,80,512]{2,1,0:T(8,128)S(1)} %shard_map.42.refs_0_, f32[1,80,512]{2,1,0:T(8,128)S(1)} %collective-permute-done.13.refs_1_, f32[1,80,512]{2,1,0:T(8,128)S(1)} %collective-permute-done.14.refs_2_, ...), custom_call_target="tpu_custom_call" | custom-call | tf_op jit(solution)/shard_map/pallas_call | solution.py:32
  62.5 0.9 collective-permute-start.20
  63.3 2.6 %collective-permute-start.21 = (f32[512,128]{1,0:T(8,128)S(1)}, f32[512,128]{1,0:T(8,128)S(1)}, u32[]{:S(2)}, u32[]{:S(2)}) collective-permute-start(f32[512,128]{1,0:T(8,128)S(1)} %get-tuple-element.70), channel_id=1, source_target_pairs={{0,2},{1,3},{2,1},{3,0},{4,6},{5,7},{6,5},{7,4},{8,10},{9,11},{10,... | collective-permute-start | bytes 786440 | tf_op jit(solution)/shard_map/ppermute | solution.py:383
  66.0 1.4 %collective-permute-start.22 = (f32[512,128]{1,0:T(8,128)S(1)}, f32[512,128]{1,0:T(8,128)S(1)}, u32[]{:S(2)}, u32[]{:S(2)}) collective-permute-start(f32[512,128]{1,0:T(8,128)S(1)} %get-tuple-element.71), channel_id=1, source_target_pairs={{0,1},{1,0},{2,3},{3,2},{4,5},{5,4},{6,7},{7,6},{8,9},{9,8},{10,11... | collective-permute-start | bytes 786440 | tf_op jit(solution)/shard_map/ppermute | solution.py:383
  67.4 13.8 %collective-permute-done.20.refs_1_ = f32[512,128]{1,0:T(8,128)S(1)} collective-permute-done((f32[512,128]{1,0:T(8,128)S(1)}, f32[512,128]{1,0:T(8,128)S(1)}, u32[]{:S(2)}, u32[]{:S(2)}) %collective-permute-start.20) | collective-permute-done | bytes 262176 | tf_op jit(solution)/shard_map/ppermute | solution.py:383
  81.2 5.7 %collective-permute-done.21.refs_2_ = f32[512,128]{1,0:T(8,128)S(1)} collective-permute-done((f32[512,128]{1,0:T(8,128)S(1)}, f32[512,128]{1,0:T(8,128)S(1)}, u32[]{:S(2)}, u32[]{:S(2)}) %collective-permute-start.21) | collective-permute-done | bytes 262176 | tf_op jit(solution)/shard_map/ppermute | solution.py:383
  86.9 1.0 %shard_map.44 = f32[4,512,128]{2,1,0:T(8,128)} custom-call(f32[512,128]{1,0:T(8,128)S(1)} %get-tuple-element.68.refs_0_, f32[512,128]{1,0:T(8,128)S(1)} %collective-permute-done.20.refs_1_, f32[512,128]{1,0:T(8,128)S(1)} %collective-permute-done.21.refs_2_, f32[512,128]{1,0:T(8,128)S(1)} %collective-permute-done.22.refs_3_), custom_call_target="tpu_custom_call" | custom-call | tf_op jit(solution)/shard_map/pallas_call | solution.py:385
  (17 shorter events, 0.1 us)
Async XLA Ops:
  0.0 6.5 %copy-start.1 = (f32[512,512]{1,0:T(8,128)S(1)}, f32[512,512]{1,0:T(8,128)}, u32[]{:S(2)}) copy-start(f32[512,512]{1,0:T(8,128)} %refs_11_.1) | copy-start | bytes 3145732
  1.1 19.6 %collective-permute-start.5 = (f32[2,64,512]{2,1,0:T(8,128)S(1)}, f32[2,64,512]{2,1,0:T(8,128)S(1)}, u32[]{:S(2)}, u32[]{:S(2)}) collective-permute-start(f32[2,64,512]{2,1,0:T(8,128)S(1)} %dynamic-slice_bitcast_fusion), channel_id=1, source_target_pairs={{0,3},{1,2},{2,0},{3,1},{4,7},{5,6},{6,4},{7,5},{8,11},{9,10},{10,... | collective-permute-start | bytes 786440 | tf_op jit(solution)/shard_map/ppermute | solution.py:311
  3.9 22.0 %collective-permute-start.3 = (f32[2,64,512]{2,1,0:T(8,128)S(1)}, f32[2,64,512]{2,1,0:T(8,128)S(1)}, u32[]{:S(2)}, u32[]{:S(2)}) collective-permute-start(f32[2,64,512]{2,1,0:T(8,128)S(1)} %get-tuple-element.47), channel_id=1, source_target_pairs={{0,2},{1,3},{2,1},{3,0},{4,6},{5,7},{6,5},{7,4},{8,10},{9,11},{10,... | collective-permute-start | bytes 786440 | tf_op jit(solution)/shard_map/ppermute | solution.py:311
  5.3 20.6 %collective-permute-start.4 = (f32[2,64,512]{2,1,0:T(8,128)S(1)}, f32[2,64,512]{2,1,0:T(8,128)S(1)}, u32[]{:S(2)}, u32[]{:S(2)}) collective-permute-start(f32[2,64,512]{2,1,0:T(8,128)S(1)} %get-tuple-element.48), channel_id=1, source_target_pairs={{0,1},{1,0},{2,3},{3,2},{4,5},{5,4},{6,7},{7,6},{8,9},{9,8},{10,11... | collective-permute-start | bytes 786440 | tf_op jit(solution)/shard_map/ppermute | solution.py:311
  6.9 1.4 %collective-permute-start = (f32[4,16,512]{2,1,0:T(8,128)S(1)}, f32[4,16,512]{2,1,0:T(8,128)S(1)}, u32[]{:S(2)}, u32[]{:S(2)}) collective-permute-start(f32[4,16,512]{2,1,0:T(8,128)S(1)} %get-tuple-element.15), channel_id=1, source_target_pairs={{0,4},{4,0},{8,12},{12,8},{16,20},{20,16},{24,28},{28,24},{1,5},{5... | collective-permute-start | bytes 393224 | tf_op jit(solution)/shard_map/cond/branch_1_fun/ppermute | solution.py:44
  8.3 4.3 %collective-permute-start.1 = (f32[2,16,512]{2,1,0:T(8,128)S(1)}, f32[2,16,512]{2,1,0:T(8,128)S(1)}, u32[]{:S(2)}, u32[]{:S(2)}) collective-permute-start(f32[2,16,512]{2,1,0:T(8,128)S(1)} %get-tuple-element.17), channel_id=1, source_target_pairs={{0,8},{4,12},{8,0},{12,4},{16,24},{20,28},{24,16},{28,20},{1,9},{5... | collective-permute-start | bytes 196616 | tf_op jit(solution)/shard_map/cond/branch_1_fun/ppermute | solution.py:44
  12.7 4.0 %collective-permute-start.2 = (f32[1,16,512]{2,1,0:T(8,128)S(1)}, f32[1,16,512]{2,1,0:T(8,128)S(1)}, u32[]{:S(2)}, u32[]{:S(2)}) collective-permute-start(f32[1,16,512]{2,1,0:T(8,128)S(1)} %get-tuple-element.19), channel_id=1, source_target_pairs={{0,16},{4,20},{8,24},{12,28},{16,0},{20,4},{24,8},{28,12},{1,17},{... | collective-permute-start | bytes 98312 | tf_op jit(solution)/shard_map/cond/branch_1_fun/ppermute | solution.py:44
  21.1 4.8 %collective-permute-start.6 = (f32[4,16,512]{2,1,0:T(8,128)S(1)}, f32[4,16,512]{2,1,0:T(8,128)S(1)}, u32[]{:S(2)}, u32[]{:S(2)}) collective-permute-start(f32[4,16,512]{2,1,0:T(8,128)S(1)} %get-tuple-element.54), channel_id=1, source_target_pairs={{0,4},{4,0},{8,12},{12,8},{16,20},{20,16},{24,28},{28,24},{1,5},{5... | collective-permute-start | bytes 393224 | tf_op jit(solution)/shard_map/ppermute | solution.py:44
  26.7 1.8 %collective-permute-start.7 = (f32[4,48,512]{2,1,0:T(8,128)S(1)}, f32[4,48,512]{2,1,0:T(8,128)S(1)}, u32[]{:S(2)}, u32[]{:S(2)}) collective-permute-start(f32[4,48,512]{2,1,0:T(8,128)S(1)} %get-tuple-element.61), channel_id=1, source_target_pairs={{0,4},{4,0},{8,12},{12,8},{16,20},{20,16},{24,28},{28,24},{1,5},{5... | collective-permute-start | bytes 1179656 | tf_op jit(solution)/shard_map/ppermute | solution.py:44
  28.6 5.6 %collective-permute-start.8 = (f32[1,64,512]{2,1,0:T(8,128)S(1)}, f32[1,64,512]{2,1,0:T(8,128)S(1)}, u32[]{:S(2)}, u32[]{:S(2)}) collective-permute-start(f32[1,64,512]{2,1,0:T(8,128)S(1)} %get-tuple-element.63), channel_id=1, source_target_pairs={{0,16},{4,20},{8,24},{12,28},{16,0},{20,4},{24,8},{28,12},{1,17},{... | collective-permute-start | bytes 393224 | tf_op jit(solution)/shard_map/ppermute | solution.py:44
  30.2 6.4 %collective-permute-start.9 = (f32[1,64,512]{2,1,0:T(8,128)S(1)}, f32[1,64,512]{2,1,0:T(8,128)S(1)}, u32[]{:S(2)}, u32[]{:S(2)}) collective-permute-start(f32[1,64,512]{2,1,0:T(8,128)S(1)} %get-tuple-element.64), channel_id=1, source_target_pairs={{0,8},{4,12},{8,0},{12,4},{16,24},{20,28},{24,16},{28,20},{1,9},{5... | collective-permute-start | bytes 393224 | tf_op jit(solution)/shard_map/ppermute | solution.py:44
  31.7 6.5 %collective-permute-start.10 = (f32[1,64,512]{2,1,0:T(8,128)S(1)}, f32[1,64,512]{2,1,0:T(8,128)S(1)}, u32[]{:S(2)}, u32[]{:S(2)}) collective-permute-start(f32[1,64,512]{2,1,0:T(8,128)S(1)} %get-tuple-element.65), channel_id=1, source_target_pairs={{0,24},{4,28},{8,16},{12,20},{16,8},{20,12},{24,0},{28,4},{1,25},{... | collective-permute-start | bytes 393224 | tf_op jit(solution)/shard_map/ppermute | solution.py:44
  38.2 22.1 %copy-start = (f32[2,256,256]{2,1,0:T(8,128)S(1)}, f32[2,256,256]{2,1,0:T(8,128)}, u32[]{:S(2)}) copy-start(f32[2,256,256]{2,1,0:T(8,128)} %refs_8_.1) | copy-start | bytes 1572868
  38.2 5.4 %collective-permute-start.11 = (f32[1,80,512]{2,1,0:T(8,128)S(1)}, f32[1,80,512]{2,1,0:T(8,128)S(1)}, u32[]{:S(2)}, u32[]{:S(2)}) collective-permute-start(f32[1,80,512]{2,1,0:T(8,128)S(1)} %shard_map.40.left), channel_id=1, source_target_pairs={{0,1},{1,0},{2,3},{3,2},{4,6},{5,7},{6,4},{7,5},{8,9},{9,8},{10,11... | collective-permute-start | bytes 491528 | tf_op jit(solution)/shard_map/ppermute | solution.py:248
  43.6 7.2 %collective-permute-start.12 = (f32[1,80,512]{2,1,0:T(8,128)S(1)}, f32[1,80,512]{2,1,0:T(8,128)S(1)}, u32[]{:S(2)}, u32[]{:S(2)}) collective-permute-start(f32[1,80,512]{2,1,0:T(8,128)S(1)} %shard_map.41.left), channel_id=1, source_target_pairs={{0,2},{1,3},{2,0},{3,1},{4,5},{5,4},{6,7},{7,6},{8,10},{9,11},{10,... | collective-permute-start | bytes 491528 | tf_op jit(solution)/shard_map/ppermute | solution.py:248
  50.9 6.3 %collective-permute-start.15 = (f32[1,80,512]{2,1,0:T(8,128)S(1)}, f32[1,80,512]{2,1,0:T(8,128)S(1)}, u32[]{:S(2)}, u32[]{:S(2)}) collective-permute-start(f32[1,80,512]{2,1,0:T(8,128)S(1)} %shard_map.42.refs_0_), channel_id=1, source_target_pairs={{0,24},{4,28},{8,16},{12,20},{16,8},{20,12},{24,0},{28,4},{1,25},{... | collective-permute-start | bytes 491528 | tf_op jit(solution)/shard_map/ppermute | solution.py:44
  53.1 5.6 %collective-permute-start.14 = (f32[1,80,512]{2,1,0:T(8,128)S(1)}, f32[1,80,512]{2,1,0:T(8,128)S(1)}, u32[]{:S(2)}, u32[]{:S(2)}) collective-permute-start(f32[1,80,512]{2,1,0:T(8,128)S(1)} %shard_map.42.refs_0_), channel_id=1, source_target_pairs={{0,8},{4,12},{8,0},{12,4},{16,24},{20,28},{24,16},{28,20},{1,9},{5... | collective-permute-start | bytes 491528 | tf_op jit(solution)/shard_map/ppermute | solution.py:44
  53.6 5.3 %collective-permute-start.13 = (f32[1,80,512]{2,1,0:T(8,128)S(1)}, f32[1,80,512]{2,1,0:T(8,128)S(1)}, u32[]{:S(2)}, u32[]{:S(2)}) collective-permute-start(f32[1,80,512]{2,1,0:T(8,128)S(1)} %shard_map.42.refs_0_), channel_id=1, source_target_pairs={{0,16},{4,20},{8,24},{12,28},{16,0},{20,4},{24,8},{28,12},{1,17},{... | collective-permute-start | bytes 491528 | tf_op jit(solution)/shard_map/ppermute | solution.py:44
  54.4 4.7 %collective-permute-start.16 = (f32[1,80,512]{2,1,0:T(8,128)S(1)}, f32[1,80,512]{2,1,0:T(8,128)S(1)}, u32[]{:S(2)}, u32[]{:S(2)}) collective-permute-start(f32[1,80,512]{2,1,0:T(8,128)S(1)} %shard_map.42.refs_0_), channel_id=1, source_target_pairs={{0,4},{4,0},{8,12},{12,8},{16,20},{20,16},{24,28},{28,24},{1,5},{5... | collective-permute-start | bytes 491528 | tf_op jit(solution)/shard_map/ppermute | solution.py:44
  57.2 2.0 %collective-permute-start.19 = (f32[1,80,512]{2,1,0:T(8,128)S(1)}, f32[1,80,512]{2,1,0:T(8,128)S(1)}, u32[]{:S(2)}, u32[]{:S(2)}) collective-permute-start(f32[1,80,512]{2,1,0:T(8,128)S(1)} %collective-permute-done.15.refs_3_), channel_id=1, source_target_pairs={{0,4},{4,0},{8,12},{12,8},{16,20},{20,16},{24,28},{28,24},{1,5},{5... | collective-permute-start | bytes 491528 | tf_op jit(solution)/shard_map/ppermute | solution.py:44
  58.7 1.4 %collective-permute-start.18 = (f32[1,80,512]{2,1,0:T(8,128)S(1)}, f32[1,80,512]{2,1,0:T(8,128)S(1)}, u32[]{:S(2)}, u32[]{:S(2)}) collective-permute-start(f32[1,80,512]{2,1,0:T(8,128)S(1)} %collective-permute-done.14.refs_2_), channel_id=1, source_target_pairs={{0,4},{4,0},{8,12},{12,8},{16,20},{20,16},{24,28},{28,24},{1,5},{5... | collective-permute-start | bytes 491528 | tf_op jit(solution)/shard_map/ppermute | solution.py:44
  58.9 1.4 %collective-permute-start.17 = (f32[1,80,512]{2,1,0:T(8,128)S(1)}, f32[1,80,512]{2,1,0:T(8,128)S(1)}, u32[]{:S(2)}, u32[]{:S(2)}) collective-permute-start(f32[1,80,512]{2,1,0:T(8,128)S(1)} %collective-permute-done.13.refs_1_), channel_id=1, source_target_pairs={{0,4},{4,0},{8,12},{12,8},{16,20},{20,16},{24,28},{28,24},{1,5},{5... | collective-permute-start | bytes 491528 | tf_op jit(solution)/shard_map/ppermute | solution.py:44
  62.5 18.8 %collective-permute-start.20 = (f32[512,128]{1,0:T(8,128)S(1)}, f32[512,128]{1,0:T(8,128)S(1)}, u32[]{:S(2)}, u32[]{:S(2)}) collective-permute-start(f32[512,128]{1,0:T(8,128)S(1)} %get-tuple-element.69), channel_id=1, source_target_pairs={{0,3},{1,2},{2,0},{3,1},{4,7},{5,6},{6,4},{7,5},{8,11},{9,10},{10,... | collective-permute-start | bytes 786440 | tf_op jit(solution)/shard_map/ppermute | solution.py:383
  63.3 23.6 %collective-permute-start.21 = (f32[512,128]{1,0:T(8,128)S(1)}, f32[512,128]{1,0:T(8,128)S(1)}, u32[]{:S(2)}, u32[]{:S(2)}) collective-permute-start(f32[512,128]{1,0:T(8,128)S(1)} %get-tuple-element.70), channel_id=1, source_target_pairs={{0,2},{1,3},{2,1},{3,0},{4,6},{5,7},{6,5},{7,4},{8,10},{9,11},{10,... | collective-permute-start | bytes 786440 | tf_op jit(solution)/shard_map/ppermute | solution.py:383
  66.0 21.0 %collective-permute-start.22 = (f32[512,128]{1,0:T(8,128)S(1)}, f32[512,128]{1,0:T(8,128)S(1)}, u32[]{:S(2)}, u32[]{:S(2)}) collective-permute-start(f32[512,128]{1,0:T(8,128)S(1)} %get-tuple-element.71), channel_id=1, source_target_pairs={{0,1},{1,0},{2,3},{3,2},{4,5},{5,4},{6,7},{7,6},{8,9},{9,8},{10,11... | collective-permute-start | bytes 786440 | tf_op jit(solution)/shard_map/ppermute | solution.py:383
